TPU v7x, 32 devices: a whole 2x2x4 slice. The times are simulated.
32 devices in a mesh: row: 8 (over y, x, core), tensor: 4 (over z).
Axes of the slice: x: 2, y: 2, z: 4, core: 2. Of those that a mesh axis runs over, the one named last changes fastest.
Arguments:
- latents: bfloat16 [4, 16, 64, 2240], P(None, 'row', None, 'tensor'), may hold values from -6 to 6
- clip_height: int32 [4], replicated, may hold values from 8 to 16, as said below
- clip_width: int32 [4], replicated, may hold values from 32 to 64, as said below
- expand_weight: bfloat16 [2, 2240, 5600], P(None, None, 'tensor'), may hold values from -0.125 to 0.125
- expand_bias: float32 [2, 5600], P(None, 'tensor'), may hold values from -3 to 3
- depth_weight: float32 [3, 3, 2, 5600], P(None, None, None, 'tensor'), may hold values from -2 to 2
- depth_bias: float32 [2, 5600], P(None, 'tensor'), may hold values from -3 to 3
- project_weight: bfloat16 [5600, 2240], P('tensor'), may hold values from -0.109375 to 0.109375
Outputs:
- block_output: bfloat16 [4, 16, 64, 2240], P(None, 'row', None, 'tensor')
Inputs may be any that keep to these rules, and one draw needn't show every extreme that they name: `clip_height`: one clip spans all 16 rows and another exactly 8 of them. `clip_width`: one clip spans all 64 columns and another exactly 32 of them.
All inputs are finite; a program needn't handle non-finite values.
Results may differ from a plain program's by a relative error of at most 0.0062.
Values may be sent and summed in bfloat16 or wider, within the bound.
No kernel may reach another device: no remote copies, remote signals or barrier semaphores. Data moves between devices by JAX's collectives and lax.ppermute only.
A program may use at most 128 MiB of HBM per device.

v0:
```python
import functools

import jax
import jax.numpy as jnp
from jax import lax
from jax.experimental import pallas as pl
from jax.experimental.pallas import tpu as pltpu
from jax.sharding import PartitionSpec as P

LANES = 512
GROUP = 16
TILE = 256


def halo_rows(cells):
    count = lax.axis_size("row")
    ends = count - 1
    head = cells[:, :1]
    tail = cells[:, -1:]
    above = lax.ppermute(tail, "row", [(i, i + 1) for i in range(ends)])
    below = lax.ppermute(head, "row", [(i + 1, i) for i in range(ends)])
    return jnp.concatenate([above, cells, below], axis=1)


def depthwise(padded, depth_weight, depth_bias, row_count, col_count):
    widened = jnp.pad(padded, ((0, 0), (0, 0), (1, 1), (0, 0), (0, 0)))
    out_shape = (widened.shape[0], row_count, col_count) + widened.shape[3:]
    depth_out = jnp.zeros(out_shape, jnp.float32) + depth_bias
    for tap_row in range(3):
        for tap_col in range(3):
            depth_out = (
                depth_out
                + depth_weight[tap_row, tap_col]
                * widened[:, tap_row : tap_row + row_count, tap_col : tap_col + col_count]
            )
    return depth_out


def on_device_plain(
    latents,
    clip_height,
    clip_width,
    expand_weight,
    expand_bias,
    depth_weight,
    depth_bias,
    project_weight,
):
    batch_size, row_count, col_count, depth = latents.shape
    tokens = batch_size * row_count * col_count
    first_row = lax.axis_index("row") * row_count
    row_ids = first_row + jnp.arange(row_count, dtype=jnp.int32)
    col_ids = jnp.arange(col_count, dtype=jnp.int32)
    valid_mask = (
        (row_ids[None, :, None] < clip_height[:, None, None])
        & (col_ids[None, None, :] < clip_width[:, None, None])
    ).astype(jnp.float32)[..., None]
    channels = latents.reshape(tokens, depth).T
    gathered = lax.all_gather(channels, "tensor", axis=0, tiled=True)
    pre_act = jnp.einsum("dt,kdf->tkf", gathered, expand_weight, preferred_element_type=jnp.float32)
    pre_act = pre_act.reshape(batch_size, row_count, col_count, 2, -1)
    expanded = (jax.nn.silu(pre_act + expand_bias) * valid_mask[..., None]).astype(jnp.bfloat16)
    padded = halo_rows(expanded)
    depth_out = depthwise(padded, depth_weight, depth_bias, row_count, col_count)
    hidden = (depth_out[:, :, :, 0] * jax.nn.silu(depth_out[:, :, :, 1])).astype(jnp.bfloat16)
    partial_term = jnp.einsum(
        "tf,fd->dt", hidden.reshape(tokens, -1), project_weight, preferred_element_type=jnp.float32
    ).astype(jnp.bfloat16)
    summed = lax.psum_scatter(partial_term, "tensor", scatter_dimension=0, tiled=True)
    summed = summed.T.reshape(latents.shape).astype(jnp.float32)
    return (summed * valid_mask).astype(jnp.bfloat16)


def slot_clips(width_ref, batch_size):
    narrow, least = jnp.int32(0), width_ref[0]
    for b in range(1, batch_size):
        closer = width_ref[b] < least
        narrow = jnp.where(closer, b, narrow)
        least = jnp.where(closer, width_ref[b], least)
    return [jnp.where(narrow <= s, s + 1, s) for s in range(batch_size - 1)] + [narrow]


def slot_widths(batch_size, col_count):
    return [col_count] * (batch_size - 1) + [col_count // 2]


class Chunk:
    def __init__(self, slots, widths, depth):
        self.slots = slots
        self.widths = [widths[s] for s in slots]
        self.starts = [sum(self.widths[:i]) for i in range(len(slots))]
        self.kept = sum(self.widths)
        self.block = -(-self.kept // 128) * 128
        self.depth, self.rest = depth, depth - LANES
        across = LANES // self.block
        groups = self.rest // GROUP
        self.places = [(g // across * GROUP, g % across * self.block) for g in range(groups)]
        self.lines = self.kept + -(-groups // across) * GROUP
        self.tokens = 2 * self.kept
        self.full, self.left = self.tokens // 128, self.tokens % 128
        self.upper = -(-depth // (2 * GROUP)) * GROUP
        self.unit = (self.full * depth + (self.upper if self.left else 0), 128)

    def clips(self, width_ref, batch_size):
        order = slot_clips(width_ref, batch_size)
        return [order[s] for s in self.slots]

    def mask_column(self, height_ref, width_ref, row_id):
        pieces = []
        clips = self.clips(width_ref, width_ref.shape[0])
        for clip, width in zip(clips, self.widths):
            bound = jnp.where((row_id >= 0) & (row_id < height_ref[clip]), width_ref[clip], 0)
            col = lax.broadcasted_iota(jnp.int32, (width, 128), 0)
            pieces.append((col < bound).astype(jnp.float32))
        return jnp.concatenate(pieces, axis=0)

    def put_unit(self, unit_ref, sums):
        depth, at = self.depth, self.full * self.depth
        for b in range(self.full):
            unit_ref[b * depth : (b + 1) * depth, :] = sums[:, b * 128 : (b + 1) * 128]
        if self.left:
            tail = sums[:, self.full * 128 :]
            lower = depth - self.upper
            unit_ref[at : at + self.upper, : self.left] = tail[: self.upper]
            unit_ref[at : at + lower, self.left :] = tail[self.upper :]
            if lower < self.upper:
                unit_ref[at + lower :, self.left :] = jnp.zeros(
                    (self.upper - lower, 128 - self.left), sums.dtype
                )

    def get_unit(self, unit):
        depth, at = self.depth, self.full * self.depth
        blocks = [unit[b * depth : (b + 1) * depth, :] for b in range(self.full)]
        if self.left:
            lower = depth - self.upper
            blocks.append(
                jnp.concatenate(
                    [unit[at : at + self.upper, : self.left], unit[at : at + lower, self.left :]], axis=0
                )
            )
        return jnp.concatenate(blocks, axis=1)


def parity_of():
    return lax.rem(lax.axis_index("row"), 2)


def row_of(place, parity):
    return jnp.where(parity == 0, (-1, 0, 1, 2)[place], (2, 1, 0, -1)[place])


def silu(v):
    h = 0.5 * v
    return h + h * jnp.tanh(h)


def pack_kernel(width_ref, x_ref, *out_refs, chunks):
    parity = parity_of()
    for chunk, out_ref in zip(chunks, out_refs):
        for place in range(2):
            row = jnp.where(parity == 0, 1 - place, place)
            tails = []
            for clip, width, at in zip(
                chunk.clips(width_ref, x_ref.shape[0]), chunk.widths, chunk.starts
            ):
                out_ref[place, at : at + width, :] = x_ref[clip, row, :width, :LANES]
                tails.append(x_ref[clip, row, :width, LANES:].astype(jnp.float32))
            if chunk.block > chunk.kept:
                tails.append(jnp.zeros((chunk.block - chunk.kept, chunk.rest), jnp.float32))
            turned = jnp.concatenate(tails, axis=0).T.astype(jnp.bfloat16)
            kept = chunk.kept
            out_ref[place, kept:, :] = jnp.zeros((chunk.lines - kept, LANES), jnp.bfloat16)
            for g, (down, over) in enumerate(chunk.places):
                out_ref[place, kept + down : kept + down + GROUP, over : over + chunk.block] = turned[
                    g * GROUP : (g + 1) * GROUP
                ]


def hidden_kernel(height_ref, width_ref, *refs, chunk, shards, groups, count):
    own_refs = refs[:shards]
    inner_refs = refs[shards : shards + count]
    outer_refs = refs[shards + count : shards + 2 * count]
    w_ref, eb_ref, dw_ref, db_ref, out_ref, x_scr, m_scr, e_scr = refs[shards + 2 * count :]
    kept, rest, depth = chunk.kept, chunk.rest, chunk.depth
    me = lax.axis_index("tensor")
    parity = parity_of()
    subs = w_ref.shape[2] // TILE

    @pl.when(pl.program_id(0) == 0)
    def _():
        spots = {j: (g, i) for g, js in enumerate(groups) for i, j in enumerate(js)}
        for place in range(4):
            tails = []
            lines = slice(place * kept, (place + 1) * kept)
            for j in range(shards):
                g, i = spots[j]
                packet = (
                    outer_refs[g].at[i],
                    own_refs[j].at[1],
                    own_refs[j].at[0],
                    inner_refs[g].at[i],
                )[place]
                x_scr[lines, j * LANES : (j + 1) * LANES] = packet[:kept, :]
                for down, over in chunk.places:
                    tails.append(packet[kept + down : kept + down + GROUP, over : over + chunk.block])
            turned = jnp.concatenate(tails, axis=0).astype(jnp.float32).T
            x_scr[lines, shards * LANES :] = turned[:kept].astype(jnp.bfloat16)
            row_id = lax.axis_index("row") * 2 + row_of(place, parity)
            m_scr[lines, :] = chunk.mask_column(height_ref, width_ref, row_id)

    bases = [pl.multiple_of(lax.bitwise_xor(me, j) * depth, GROUP) for j in range(shards)]
    for sub in range(subs):
        units = slice(sub * TILE, (sub + 1) * TILE)
        for k in range(2):
            weight = jnp.concatenate(
                [w_ref[k, pl.ds(base, LANES), units] for base in bases]
                + [w_ref[k, pl.ds(pl.multiple_of(base + LANES, GROUP), rest), units] for base in bases],
                axis=0,
            )
            pre_act = jnp.dot(x_scr[...], weight, preferred_element_type=jnp.float32)
            mask = jnp.concatenate([m_scr[...]] * (TILE // 128), axis=1)
            e_scr[sub, k] = silu(pre_act + eb_ref[k : k + 1, units]) * mask

    line = lax.broadcasted_iota(jnp.int32, (kept, TILE), 0)
    not_first, not_last = None, None
    for at, width in zip(chunk.starts, chunk.widths):
        first, last = line != at, line != at + width - 1
        not_first = first if not_first is None else not_first & first
        not_last = last if not_last is None else not_last & last
    for sub in range(subs):
        units = slice(sub * TILE, (sub + 1) * TILE)
        for place in (1, 2):
            halves = []
            for k in range(2):
                sums = []
                for tap_col in range(3):
                    total = None
                    for i in range(3):
                        tap_row = jnp.where(parity == 0, i, 2 - i)
                        cells = e_scr[sub, k, (place + i - 1) * kept : (place + i) * kept, :]
                        term = dw_ref[tap_row, tap_col, k : k + 1, units] * cells
                        total = term if total is None else total + term
                    sums.append(total)
                left = jnp.where(not_first, pltpu.roll(sums[0], 1, 0), 0.0)
                right = jnp.where(not_last, pltpu.roll(sums[2], kept - 1, 0), 0.0)
                halves.append(sums[1] + left + right + db_ref[k : k + 1, units])
            hidden = halves[0] * silu(halves[1])
            out_ref[(2 - place) * kept : (3 - place) * kept, units] = hidden.astype(jnp.bfloat16)


def project(weight_ref, hidden_ref):
    return lax.dot_general(
        weight_ref[...],
        hidden_ref[...],
        (((1,), (1,)), ((), ())),
        preferred_element_type=jnp.float32,
    )


def unit_kernel(place_ref, weight_ref, hidden_ref, *refs, chunk):
    out_ref = refs[-1]
    sums = project(weight_ref, hidden_ref)
    for ref in refs[:-1]:
        sums = sums + chunk.get_unit(ref[...].astype(jnp.float32))
    chunk.put_unit(out_ref, sums.astype(jnp.bfloat16))


def final_kernel(place_ref, height_ref, width_ref, weight_ref, hidden_ref, *refs, chunk, sources):
    out_ref = refs[-1]
    if len(refs) > sources + 1:
        out_ref[...] = refs[sources][...]
    sums = project(weight_ref, hidden_ref)
    for ref in refs[:sources]:
        sums = sums + chunk.get_unit(ref[...].astype(jnp.float32))
    cells = sums.T
    parity = parity_of()
    for place in range(2):
        row = jnp.where(parity == 0, 1 - place, place)
        row_id = lax.axis_index("row") * 2 + row
        mask = chunk.mask_column(height_ref, width_ref, row_id)[:, :1] > 0
        part = cells[place * chunk.kept : (place + 1) * chunk.kept]
        part = jnp.where(mask, part, 0.0).astype(jnp.bfloat16)
        clips = chunk.clips(width_ref, width_ref.shape[0])
        for clip, width, at in zip(clips, chunk.widths, chunk.starts):
            out_ref[clip, row, :width, :] = part[at : at + width]
            if width < out_ref.shape[2]:
                blank = jnp.zeros((out_ref.shape[2] - width, chunk.depth), jnp.bfloat16)
                out_ref[clip, row, width:, :] = blank


VMEM = pl.BlockSpec(memory_space=pltpu.VMEM)
MIB = 1024 * 1024


def after(value, *others):
    return lax.optimization_barrier((value,) + others)[0]


def on_device_packed(
    latents,
    clip_height,
    clip_width,
    expand_weight,
    expand_bias,
    depth_weight,
    depth_bias,
    project_weight,
):
    batch_size, row_count, col_count, depth = latents.shape
    shards, row_devices = lax.axis_size("tensor"), lax.axis_size("row")
    hidden_count = expand_weight.shape[2]
    full_depth = shards * depth
    chunks = chunks_of(batch_size, col_count, depth)
    own = pl.pallas_call(
        functools.partial(pack_kernel, chunks=chunks),
        out_shape=[jax.ShapeDtypeStruct((2, c.lines, LANES), jnp.bfloat16) for c in chunks],
        grid_spec=pltpu.PrefetchScalarGridSpec(
            num_scalar_prefetch=1, grid=(), in_specs=[VMEM], out_specs=[VMEM] * len(chunks)
        ),
        name="pack",
    )(clip_width, latents)
    me = lax.axis_index("tensor").astype(jnp.int32).reshape(1)
    project_turned = project_weight.T

    sibling = [(i, i ^ 1) for i in range(row_devices)]
    beyond = [(i, i + 1) for i in range(1, row_devices - 1, 2)]
    beyond = beyond + [(b, a) for a, b in beyond]
    near = [(i, i ^ 1) for i in range(4)]
    two_off = [(i, i ^ 2) for i in range(4)]
    middle = [(1, 2), (2, 1)]
    to_end = [(2, 3), (1, 0)]
    from_end = [(0, 1), (3, 2)]

    def halos(packets, groups):
        inner = [jnp.concatenate([packets[j][:1] for j in js], axis=0) for js in groups]
        outer = [jnp.concatenate([packets[j][1:] for j in js], axis=0) for js in groups]
        return (
            [lax.ppermute(x, "row", sibling) for x in inner],
            [lax.ppermute(x, "row", beyond) for x in outer],
        )

    def relay(mine):
        second = lax.ppermute(mine, "tensor", two_off)
        first = lax.ppermute(mine, "tensor", near)
        across = lax.ppermute(after(mine, second), "tensor", middle)
        passed = lax.ppermute(second, "tensor", to_end)
        return [mine, first, second, across + passed]

    def direct(mine):
        return [mine] + [
            lax.ppermute(mine, "tensor", [(i, i ^ j) for i in range(4)]) for j in range(1, 4)
        ]

    out = None
    packets = relay(own[0])
    groups = ((0,), (1, 2), (3,))
    inner, outer = halos(packets, groups)
    upcoming = direct(after(own[1], packets[3]))
    for number, chunk in enumerate(chunks):
        if number:
            packets, groups = list(lax.optimization_barrier((*upcoming, hidden))[:shards]), ((0, 1, 2, 3),)
            inner, outer = halos(packets, groups)
            packets[0] = after(packets[0], last_unit)
        wide = 2 * TILE
        whole = lambda shape: pl.BlockSpec(shape, lambda f, *_: (0,) * len(shape))
        lines = 4 * chunk.kept
        hidden = pl.pallas_call(
            functools.partial(
                hidden_kernel, chunk=chunk, shards=shards, groups=groups, count=len(groups)
            ),
            out_shape=jax.ShapeDtypeStruct((chunk.tokens, hidden_count), jnp.bfloat16),
            grid_spec=pltpu.PrefetchScalarGridSpec(
                num_scalar_prefetch=2,
                grid=(-(-hidden_count // wide),),
                in_specs=[whole(p.shape) for p in packets + inner + outer]
                + [
                    pl.BlockSpec((2, full_depth, wide), lambda f, *_: (0, 0, f)),
                    pl.BlockSpec((2, wide), lambda f, *_: (0, f)),
                    pl.BlockSpec((3, 3, 2, wide), lambda f, *_: (0, 0, 0, f)),
                    pl.BlockSpec((2, wide), lambda f, *_: (0, f)),
                ],
                out_specs=pl.BlockSpec((chunk.tokens, wide), lambda f, *_: (0, f)),
                scratch_shapes=[
                    pltpu.VMEM((lines, full_depth), jnp.bfloat16),
                    pltpu.VMEM((lines, 128), jnp.float32),
                    pltpu.VMEM((2, 2, lines, TILE), jnp.float32),
                ],
            ),
            compiler_params=pltpu.CompilerParams(vmem_limit_bytes=40 * MIB),
            cost_estimate=pl.CostEstimate(
                flops=4 * lines * full_depth * hidden_count,
                bytes_accessed=4 * full_depth * hidden_count,
                transcendentals=3 * lines * hidden_count,
            ),
            name="expand_conv",
        )(
            clip_height,
            clip_width,
            *packets,
            *inner,
            *outer,
            expand_weight,
            expand_bias,
            depth_weight,
            depth_bias,
        )

        weight_of = lambda j: pl.BlockSpec(
            (depth, hidden_count), lambda f, place, *_: (lax.bitwise_xor(place[0], j), 0)
        )
        cost = pl.CostEstimate(
            flops=2 * chunk.tokens * depth * hidden_count,
            bytes_accessed=2 * depth * hidden_count + 2 * chunk.tokens * hidden_count,
            transcendentals=0,
        )

        def unit(j, *added):
            return pl.pallas_call(
                functools.partial(unit_kernel, chunk=chunk),
                out_shape=jax.ShapeDtypeStruct(chunk.unit, jnp.bfloat16),
                grid_spec=pltpu.PrefetchScalarGridSpec(
                    num_scalar_prefetch=1,
                    grid=(1,),
                    in_specs=[weight_of(j), whole(hidden.shape)] + [whole(chunk.unit)] * len(added),
                    out_specs=whole(chunk.unit),
                ),
                compiler_params=pltpu.CompilerParams(vmem_limit_bytes=24 * MIB),
                cost_estimate=cost,
                name=f"project_{j}",
            )(me, project_turned, hidden, *added)

        if number:
            hidden = after(hidden, *arrived)
        far = unit(3)
        relayed = lax.ppermute(far, "tensor", from_end)
        across = lax.ppermute(far, "tensor", middle)
        close = unit(1)
        relayed, across = lax.optimization_barrier((relayed, across))
        last_unit = unit(2, relayed)
        arrived = [
            across,
            lax.ppermute(last_unit, "tensor", two_off),
            lax.ppermute(after(close, relayed), "tensor", near),
        ]
        extra = [] if out is None else [out]
        out = pl.pallas_call(
            functools.partial(final_kernel, chunk=chunk, sources=len(arrived)),
            out_shape=jax.ShapeDtypeStruct(latents.shape, jnp.bfloat16),
            grid_spec=pltpu.PrefetchScalarGridSpec(
                num_scalar_prefetch=3,
                grid=(1,),
                in_specs=[weight_of(0), whole(hidden.shape)]
                + [whole(chunk.unit)] * len(arrived)
                + [whole(latents.shape)] * len(extra),
                out_specs=whole(latents.shape),
            ),
            compiler_params=pltpu.CompilerParams(vmem_limit_bytes=24 * MIB),
            cost_estimate=cost,
            name="finish",
        )(me, clip_height, clip_width, project_turned, hidden, *arrived, *extra)
    return out


def chunks_of(batch_size, col_count, depth):
    widths = slot_widths(batch_size, col_count)
    half = batch_size // 2
    return [Chunk(slots, widths, depth) for slots in (list(range(half)), list(range(half, batch_size)))]


def on_device(latents, clip_height, clip_width, expand_weight, *rest_of):
    batch_size, row_count, col_count, depth = latents.shape
    fits = (
        batch_size >= 2
        and row_count == 2
        and lax.axis_size("row") % 2 == 0
        and lax.axis_size("tensor") == 4
        and depth > LANES
        and (depth - LANES) % GROUP == 0
        and depth % GROUP == 0
        and all(
            c.block in (128, 256, 512) and c.kept % GROUP == 0 and c.left in (0, 64)
            for c in chunks_of(batch_size, col_count, depth)
        )
    )
    run = on_device_packed if fits else on_device_plain
    return run(latents, clip_height, clip_width, expand_weight, *rest_of)


def solution(mesh):
    in_specs = (
        P(None, "row", None, "tensor"),
        P(),
        P(),
        P(None, None, "tensor"),
        P(None, "tensor"),
        P(None, None, None, "tensor"),
        P(None, "tensor"),
        P("tensor", None),
    )
    out_specs = P(None, "row", None, "tensor")
    return jax.shard_map(
        on_device, mesh=mesh, in_specs=in_specs, out_specs=out_specs, check_vma=False
    )
```

profile of v0, /device:TPU:2, one launch (start us, length us, event | category | flops | bytes accessed | tf_op | source)
XLA Modules:
  0.0 126.3 jit_solution(16930463618178408294)
XLA Ops:
  0.0 2.6 %pack.1 = (bf16[2,144,512]{2,1,0:T(8,128)(2,1)}, bf16[2,112,512]{2,1,0:T(8,128)(2,1)}) custom-call(s32[4]{0:T(128)} %width_ref.9, bf16[4,2,64,560]{3,2,1,0:T(8,128)(2,1)} %x_ref.1), custom_call_target="tpu_custom_call" | custom-call | tf_op jit(solution)/shard_map/pack/pallas_call | solution.py:314
  2.6 2.6 %collective-permute-start = (bf16[2,144,512]{2,1,0:T(8,128)(2,1)}, bf16[2,144,512]{2,1,0:T(8,128)(2,1)S(1)}, u32[]{:S(2)}, u32[]{:S(2)}) collective-permute-start(bf16[2,144,512]{2,1,0:T(8,128)(2,1)} %get-tuple-element.23.refs_0_), channel_id=1, source_target_pairs={{0,2},{1,3},{2,0},{3,1},{4,6},{5,7},{6,4},{7,5},{8,10},{9,11},{10,... | collective-permute-start | bytes 884744 | tf_op jit(solution)/shard_map/ppermute | solution.py:343
  5.2 1.6 %collective-permute-start.6 = (bf16[2,144,512]{2,1,0:T(8,128)(2,1)}, bf16[2,144,512]{2,1,0:T(8,128)(2,1)S(1)}, u32[]{:S(2)}, u32[]{:S(2)}) collective-permute-start(bf16[2,144,512]{2,1,0:T(8,128)(2,1)} %get-tuple-element.23.refs_0_), channel_id=1, source_target_pairs={{0,1},{1,0},{2,3},{3,2},{4,5},{5,4},{6,7},{7,6},{8,9},{9,8},{10,11... | collective-permute-start | bytes 884744 | tf_op jit(solution)/shard_map/ppermute | solution.py:344
  6.8 1.0 fusion.3
  7.8 1.9 %collective-permute-start.10 = (bf16[1,144,512]{2,1,0:T(8,128)(2,1)S(1)}, bf16[1,144,512]{2,1,0:T(8,128)(2,1)S(1)}, u32[]{:S(2)}, u32[]{:S(2)}) collective-permute-start(bf16[1,144,512]{2,1,0:T(8,128)(2,1)S(1)} %get-tuple-element.43), channel_id=1, source_target_pairs={{4,8},{12,16},{20,24},{8,4},{16,12},{24,20},{5,9},{13,17},{21,25},... | collective-permute-start | bytes 442376 | tf_op jit(solution)/shard_map/ppermute | solution.py:339
  9.7 1.7 %collective-permute-start.7 = (bf16[1,144,512]{2,1,0:T(8,128)(2,1)S(1)}, bf16[1,144,512]{2,1,0:T(8,128)(2,1)S(1)}, u32[]{:S(2)}, u32[]{:S(2)}) collective-permute-start(bf16[1,144,512]{2,1,0:T(8,128)(2,1)S(1)} %get-tuple-element.44), channel_id=1, source_target_pairs={{0,4},{4,0},{8,12},{12,8},{16,20},{20,16},{24,28},{28,24},{1,5},{5... | collective-permute-start | bytes 442376 | tf_op jit(solution)/shard_map/ppermute | solution.py:338
  11.4 7.5 %collective-permute-done.refs_2_ = bf16[2,144,512]{2,1,0:T(8,128)(2,1)S(1)} collective-permute-done((bf16[2,144,512]{2,1,0:T(8,128)(2,1)}, bf16[2,144,512]{2,1,0:T(8,128)(2,1)S(1)}, u32[]{:S(2)}, u32[]{:S(2)}) %collective-permute-start) | collective-permute-done | bytes 294944 | tf_op jit(solution)/shard_map/ppermute | solution.py:343
  18.9 0.7 collective-permute-start.1
  19.6 1.3 %collective-permute-start.2 = (bf16[2,144,512]{2,1,0:T(8,128)(2,1)S(1)}, bf16[2,144,512]{2,1,0:T(8,128)(2,1)S(1)}, u32[]{:S(2)}, u32[]{:S(2)}) collective-permute-start(bf16[2,144,512]{2,1,0:T(8,128)(2,1)S(1)} %collective-permute-done.refs_2_), channel_id=1, source_target_pairs={{2,3},{1,0},{6,7},{5,4},{10,11},{9,8},{14,15},{13,12},{18,19},{17,... | collective-permute-start | bytes 884744 | tf_op jit(solution)/shard_map/ppermute | solution.py:346
  21.1 2.6 %collective-permute-start.11 = (bf16[2,144,512]{2,1,0:T(8,128)(2,1)S(1)}, bf16[2,144,512]{2,1,0:T(8,128)(2,1)S(1)}, u32[]{:S(2)}, u32[]{:S(2)}) collective-permute-start(bf16[2,144,512]{2,1,0:T(8,128)(2,1)S(1)} %pad_maximum_fusion.3), channel_id=1, source_target_pairs={{4,8},{12,16},{20,24},{8,4},{16,12},{24,20},{5,9},{13,17},{21,25},... | collective-permute-start | bytes 884744 | tf_op jit(solution)/shard_map/ppermute | solution.py:339
  23.8 6.2 %collective-permute-done.2 = bf16[2,144,512]{2,1,0:T(8,128)(2,1)S(1)} collective-permute-done((bf16[2,144,512]{2,1,0:T(8,128)(2,1)S(1)}, bf16[2,144,512]{2,1,0:T(8,128)(2,1)S(1)}, u32[]{:S(2)}, u32[]{:S(2)}) %collective-permute-start.2) | collective-permute-done | bytes 294944 | tf_op jit(solution)/shard_map/ppermute | solution.py:346
  30.1 1.9 %collective-permute-start.12 = (bf16[1,144,512]{2,1,0:T(8,128)(2,1)S(1)}, bf16[1,144,512]{2,1,0:T(8,128)(2,1)S(1)}, u32[]{:S(2)}, u32[]{:S(2)}) collective-permute-start(bf16[1,144,512]{2,1,0:T(8,128)(2,1)S(1)} %get-tuple-element.37), channel_id=1, source_target_pairs={{4,8},{12,16},{20,24},{8,4},{16,12},{24,20},{5,9},{13,17},{21,25},... | collective-permute-start | bytes 442376 | tf_op jit(solution)/shard_map/ppermute | solution.py:339
  32.0 1.7 %collective-permute-start.9 = (bf16[1,144,512]{2,1,0:T(8,128)(2,1)S(1)}, bf16[1,144,512]{2,1,0:T(8,128)(2,1)S(1)}, u32[]{:S(2)}, u32[]{:S(2)}) collective-permute-start(bf16[1,144,512]{2,1,0:T(8,128)(2,1)S(1)} %get-tuple-element.38), channel_id=1, source_target_pairs={{0,4},{4,0},{8,12},{12,8},{16,20},{20,16},{24,28},{28,24},{1,5},{5... | collective-permute-start | bytes 442376 | tf_op jit(solution)/shard_map/ppermute | solution.py:338
  33.7 3.8 %collective-permute-start.5 = (bf16[2,112,512]{2,1,0:T(8,128)(2,1)}, bf16[2,112,512]{2,1,0:T(8,128)(2,1)S(1)}, u32[]{:S(2)}, u32[]{:S(2)}) collective-permute-start(bf16[2,112,512]{2,1,0:T(8,128)(2,1)} %get-tuple-element.27.refs_0_), channel_id=1, source_target_pairs={{0,3},{1,2},{2,1},{3,0},{4,7},{5,6},{6,5},{7,4},{8,11},{9,10},{10,... | collective-permute-start | bytes 688136 | tf_op jit(solution)/shard_map/ppermute | solution.py:351
  37.5 0.4 collective-permute-start.4
  37.9 1.1 collective-permute-start.3
  39.0 1.0 copy-done.1
  40.0 0.7 copy-done.3
  40.7 0.7 copy-done.5
  41.3 0.9 copy-done.7
  42.2 0.7 copy-done.9
  42.9 0.7 copy-done.11
  43.6 14.8 %expand_conv.2.hidden_ref = bf16[256,1400]{1,0:T(8,128)(2,1)S(1)} custom-call(s32[4]{0:T(128)S(1)} %copy-done.5, s32[4]{0:T(128)S(1)} %copy-done.3, bf16[2,144,512]{2,1,0:T(8,128)(2,1)S(1)} %copy-done.1, bf16[2,144,512]{2,1,0:T(8,128)(2,1)S(1)} %collective-permute-done.6.refs_1_, bf16[2,144,512]{2,1,0:T(8,128)(2,1)S(1)} %collective-permute-done.refs_2_, ...), custom_call_target="tpu_custom_call" | custom-call | flops 6422528000 | bytes 12544000 | tf_op jit(solution)/shard_map/expand_conv/pallas_call | solution.py:367
  58.7 2.0 %collective-permute-start.15 = (bf16[4,112,512]{2,1,0:T(8,128)(2,1)S(1)}, bf16[4,112,512]{2,1,0:T(8,128)(2,1)S(1)}, u32[]{:S(2)}, u32[]{:S(2)}) collective-permute-start(bf16[4,112,512]{2,1,0:T(8,128)(2,1)S(1)} %pad_maximum_fusion), channel_id=1, source_target_pairs={{0,4},{4,0},{8,12},{12,8},{16,20},{20,16},{24,28},{28,24},{1,5},{5... | collective-permute-start | bytes 1376264 | tf_op jit(solution)/shard_map/ppermute | solution.py:338
  60.7 0.8 pad_maximum_fusion.1
  61.5 1.9 %collective-permute-start.16 = (bf16[4,112,512]{2,1,0:T(8,128)(2,1)}, bf16[4,112,512]{2,1,0:T(8,128)(2,1)S(1)}, u32[]{:S(2)}, u32[]{:S(2)}) collective-permute-start(bf16[4,112,512]{2,1,0:T(8,128)(2,1)} %pad_maximum_fusion.1), channel_id=1, source_target_pairs={{4,8},{12,16},{20,24},{8,4},{16,12},{24,20},{5,9},{13,17},{21,25},... | collective-permute-start | bytes 1376264 | tf_op jit(solution)/shard_map/ppermute | solution.py:339
  63.4 2.8 %copy-done = bf16[1400,2240]{0,1:T(8,128)(2,1)S(1)} copy-done((bf16[1400,2240]{0,1:T(8,128)(2,1)S(1)}, bf16[1400,2240]{0,1:T(8,128)(2,1)}, u32[]{:S(2)}) %copy-start) | copy-done | bytes 6272024
  66.2 0.6 project_3.2
  66.8 0.7 collective-permute-start.14
  67.5 7.6 %collective-permute-start.13 = (bf16[1120,128]{1,0:T(8,128)(2,1)S(1)}, bf16[1120,128]{1,0:T(8,128)(2,1)S(1)}, u32[]{:S(2)}, u32[]{:S(2)}) collective-permute-start(bf16[1120,128]{1,0:T(8,128)(2,1)S(1)} %project_3.2), channel_id=1, source_target_pairs={{0,1},{3,2},{4,5},{7,6},{8,9},{11,10},{12,13},{15,14},{16,17},{19,... | collective-permute-start | bytes 860168 | tf_op jit(solution)/shard_map/ppermute | solution.py:435
  75.1 0.6 project_1.2
  75.8 6.2 %collective-permute-done.13.refs_0_ = bf16[1120,128]{1,0:T(8,128)(2,1)S(1)} collective-permute-done((bf16[1120,128]{1,0:T(8,128)(2,1)S(1)}, bf16[1120,128]{1,0:T(8,128)(2,1)S(1)}, u32[]{:S(2)}, u32[]{:S(2)}) %collective-permute-start.13) | collective-permute-done | bytes 286752 | tf_op jit(solution)/shard_map/ppermute | solution.py:435
  82.0 0.6 project_2.2
  82.7 2.4 %collective-permute-start.17 = (bf16[1120,128]{1,0:T(8,128)(2,1)S(1)}, bf16[1120,128]{1,0:T(8,128)(2,1)S(1)}, u32[]{:S(2)}, u32[]{:S(2)}) collective-permute-start(bf16[1120,128]{1,0:T(8,128)(2,1)S(1)} %project_2.2), channel_id=1, source_target_pairs={{0,2},{1,3},{2,0},{3,1},{4,6},{5,7},{6,4},{7,5},{8,10},{9,11},{10,... | collective-permute-start | bytes 860168 | tf_op jit(solution)/shard_map/ppermute | solution.py:442
  85.1 0.2 collective-permute-start.18
  85.4 12.0 %expand_conv.3.hidden_ref = bf16[192,1400]{1,0:T(8,128)(2,1)S(1)} custom-call(s32[4]{0:T(128)S(1)} %copy-done.6, s32[4]{0:T(128)S(1)} %copy-done.4, bf16[2,112,512]{2,1,0:T(8,128)(2,1)S(1)} %copy-done.2, bf16[2,112,512]{2,1,0:T(8,128)(2,1)S(1)} %collective-permute-done.3.refs_1_, bf16[2,112,512]{2,1,0:T(8,128)(2,1)S(1)} %collective-permute-done.4.refs_2_, ...), custom_call_target="tpu_custom_call" | custom-call | flops 4816896000 | bytes 12544000 | tf_op jit(solution)/shard_map/expand_conv/pallas_call | solution.py:367
  97.4 1.6 %collective-permute-done.17.refs_1_ = bf16[1120,128]{1,0:T(8,128)(2,1)S(1)} collective-permute-done((bf16[1120,128]{1,0:T(8,128)(2,1)S(1)}, bf16[1120,128]{1,0:T(8,128)(2,1)S(1)}, u32[]{:S(2)}, u32[]{:S(2)}) %collective-permute-start.17) | collective-permute-done | bytes 286752 | tf_op jit(solution)/shard_map/ppermute | solution.py:442
  99.0 0.7 project_3.3
  99.7 0.7 collective-permute-start.20
  100.4 5.9 %collective-permute-start.19 = (bf16[848,128]{1,0:T(8,128)(2,1)S(1)}, bf16[848,128]{1,0:T(8,128)(2,1)S(1)}, u32[]{:S(2)}, u32[]{:S(2)}) collective-permute-start(bf16[848,128]{1,0:T(8,128)(2,1)S(1)} %project_3.3), channel_id=1, source_target_pairs={{0,1},{3,2},{4,5},{7,6},{8,9},{11,10},{12,13},{15,14},{16,17},{19,... | collective-permute-start | bytes 651272 | tf_op jit(solution)/shard_map/ppermute | solution.py:435
  106.3 0.7 project_1.3
  107.0 3.0 %collective-permute-done.19.refs_0_ = bf16[848,128]{1,0:T(8,128)(2,1)S(1)} collective-permute-done((bf16[848,128]{1,0:T(8,128)(2,1)S(1)}, bf16[848,128]{1,0:T(8,128)(2,1)S(1)}, u32[]{:S(2)}, u32[]{:S(2)}) %collective-permute-start.19) | collective-permute-done | bytes 217120 | tf_op jit(solution)/shard_map/ppermute | solution.py:435
  110.0 0.7 project_2.3
  110.7 3.6 %collective-permute-start.21 = (bf16[848,128]{1,0:T(8,128)(2,1)S(1)}, bf16[848,128]{1,0:T(8,128)(2,1)S(1)}, u32[]{:S(2)}, u32[]{:S(2)}) collective-permute-start(bf16[848,128]{1,0:T(8,128)(2,1)S(1)} %project_2.3), channel_id=1, source_target_pairs={{0,2},{1,3},{2,0},{3,1},{4,6},{5,7},{6,4},{7,5},{8,10},{9,11},{10,... | collective-permute-start | bytes 651272 | tf_op jit(solution)/shard_map/ppermute | solution.py:442
  114.3 1.3 %finish.2.refs_3_ = bf16[4,2,64,560]{3,2,1,0:T(8,128)(2,1)S(1)} custom-call(s32[1]{0:T(128)} %bitcast.place_ref, s32[4]{0:T(128)S(1)} %copy-done.6, s32[4]{0:T(128)S(1)} %copy-done.4, bf16[2240,1400]{1,0:T(8,128)(2,1)S(1)} %bitcast.10, bf16[256,1400]{1,0:T(8,128)(2,1)S(1)} %expand_conv.2.hidden_ref, bf16[1120,128]{1,0:T(8,128)(2,1)S(1)} %collective-permute-done.14.refs_0_, ...), custom_call_target="tpu_custom_call" | custom-call | flops 401408000 | bytes 2284800 | tf_op jit(solution)/shard_map/finish/pallas_call | solution.py:446
  115.7 7.6 %collective-permute-done.21.refs_1_ = bf16[848,128]{1,0:T(8,128)(2,1)S(1)} collective-permute-done((bf16[848,128]{1,0:T(8,128)(2,1)S(1)}, bf16[848,128]{1,0:T(8,128)(2,1)S(1)}, u32[]{:S(2)}, u32[]{:S(2)}) %collective-permute-start.21) | collective-permute-done | bytes 217120 | tf_op jit(solution)/shard_map/ppermute | solution.py:442
  123.2 0.8 collective-permute-done.22.refs_2_
  124.1 2.2 %finish.3 = bf16[4,2,64,560]{3,2,1,0:T(8,128)(2,1)} custom-call(s32[1]{0:T(128)} %bitcast.place_ref, s32[4]{0:T(128)S(1)} %copy-done.6, s32[4]{0:T(128)S(1)} %copy-done.4, bf16[2240,1400]{1,0:T(8,128)(2,1)S(1)} %bitcast.11, bf16[192,1400]{1,0:T(8,128)(2,1)S(1)} %expand_conv.3.hidden_ref, bf16[848,128]{1,0:T(8,128)(2,1)S(1)} %collective-permute-done.20.refs_0_, ...), custom_call_target="tpu_custom_call" | custom-call | flops 301056000 | bytes 2105600 | tf_op jit(solution)/shard_map/finish/pallas_call | solution.py:446
  (51 shorter events, 0.5 us)
Async XLA Ops:
  2.6 16.3 %collective-permute-start = (bf16[2,144,512]{2,1,0:T(8,128)(2,1)}, bf16[2,144,512]{2,1,0:T(8,128)(2,1)S(1)}, u32[]{:S(2)}, u32[]{:S(2)}) collective-permute-start(bf16[2,144,512]{2,1,0:T(8,128)(2,1)} %get-tuple-element.23.refs_0_), channel_id=1, source_target_pairs={{0,2},{1,3},{2,0},{3,1},{4,6},{5,7},{6,4},{7,5},{8,10},{9,11},{10,... | collective-permute-start | bytes 884744 | tf_op jit(solution)/shard_map/ppermute | solution.py:343
  5.2 15.7 %collective-permute-start.6 = (bf16[2,144,512]{2,1,0:T(8,128)(2,1)}, bf16[2,144,512]{2,1,0:T(8,128)(2,1)S(1)}, u32[]{:S(2)}, u32[]{:S(2)}) collective-permute-start(bf16[2,144,512]{2,1,0:T(8,128)(2,1)} %get-tuple-element.23.refs_0_), channel_id=1, source_target_pairs={{0,1},{1,0},{2,3},{3,2},{4,5},{5,4},{6,7},{7,6},{8,9},{9,8},{10,11... | collective-permute-start | bytes 884744 | tf_op jit(solution)/shard_map/ppermute | solution.py:344
  7.8 24.2 %collective-permute-start.10 = (bf16[1,144,512]{2,1,0:T(8,128)(2,1)S(1)}, bf16[1,144,512]{2,1,0:T(8,128)(2,1)S(1)}, u32[]{:S(2)}, u32[]{:S(2)}) collective-permute-start(bf16[1,144,512]{2,1,0:T(8,128)(2,1)S(1)} %get-tuple-element.43), channel_id=1, source_target_pairs={{4,8},{12,16},{20,24},{8,4},{16,12},{24,20},{5,9},{13,17},{21,25},... | collective-permute-start | bytes 442376 | tf_op jit(solution)/shard_map/ppermute | solution.py:339
  9.7 23.9 %collective-permute-start.7 = (bf16[1,144,512]{2,1,0:T(8,128)(2,1)S(1)}, bf16[1,144,512]{2,1,0:T(8,128)(2,1)S(1)}, u32[]{:S(2)}, u32[]{:S(2)}) collective-permute-start(bf16[1,144,512]{2,1,0:T(8,128)(2,1)S(1)} %get-tuple-element.44), channel_id=1, source_target_pairs={{0,4},{4,0},{8,12},{12,8},{16,20},{20,16},{24,28},{28,24},{1,5},{5... | collective-permute-start | bytes 442376 | tf_op jit(solution)/shard_map/ppermute | solution.py:338
  18.9 2.2 %collective-permute-start.1 = (bf16[2,144,512]{2,1,0:T(8,128)(2,1)}, bf16[2,144,512]{2,1,0:T(8,128)(2,1)S(1)}, u32[]{:S(2)}, u32[]{:S(2)}) collective-permute-start(bf16[2,144,512]{2,1,0:T(8,128)(2,1)} %get-tuple-element.23.refs_0_), channel_id=1, source_target_pairs={{1,2},{2,1},{5,6},{6,5},{9,10},{10,9},{13,14},{14,13},{17,18},{18,... | collective-permute-start | bytes 884744 | tf_op jit(solution)/shard_map/ppermute | solution.py:345
  19.6 10.4 %collective-permute-start.2 = (bf16[2,144,512]{2,1,0:T(8,128)(2,1)S(1)}, bf16[2,144,512]{2,1,0:T(8,128)(2,1)S(1)}, u32[]{:S(2)}, u32[]{:S(2)}) collective-permute-start(bf16[2,144,512]{2,1,0:T(8,128)(2,1)S(1)} %collective-permute-done.refs_2_), channel_id=1, source_target_pairs={{2,3},{1,0},{6,7},{5,4},{10,11},{9,8},{14,15},{13,12},{18,19},{17,... | collective-permute-start | bytes 884744 | tf_op jit(solution)/shard_map/ppermute | solution.py:346
  21.0 16.5 %collective-permute-start.8 = (bf16[2,144,512]{2,1,0:T(8,128)(2,1)S(1)}, bf16[2,144,512]{2,1,0:T(8,128)(2,1)S(1)}, u32[]{:S(2)}, u32[]{:S(2)}) collective-permute-start(bf16[2,144,512]{2,1,0:T(8,128)(2,1)S(1)} %pad_maximum_fusion.2), channel_id=1, source_target_pairs={{0,4},{4,0},{8,12},{12,8},{16,20},{20,16},{24,28},{28,24},{1,5},{5... | collective-permute-start | bytes 884744 | tf_op jit(solution)/shard_map/ppermute | solution.py:338
  21.1 37.3 %copy-start.2 = (bf16[2,112,512]{2,1,0:T(8,128)(2,1)S(1)}, bf16[2,112,512]{2,1,0:T(8,128)(2,1)}, u32[]{:S(2)}) copy-start(bf16[2,112,512]{2,1,0:T(8,128)(2,1)} %get-tuple-element.27.refs_0_) | copy-start | bytes 688132
  21.1 16.8 %collective-permute-start.11 = (bf16[2,144,512]{2,1,0:T(8,128)(2,1)S(1)}, bf16[2,144,512]{2,1,0:T(8,128)(2,1)S(1)}, u32[]{:S(2)}, u32[]{:S(2)}) collective-permute-start(bf16[2,144,512]{2,1,0:T(8,128)(2,1)S(1)} %pad_maximum_fusion.3), channel_id=1, source_target_pairs={{4,8},{12,16},{20,24},{8,4},{16,12},{24,20},{5,9},{13,17},{21,25},... | collective-permute-start | bytes 884744 | tf_op jit(solution)/shard_map/ppermute | solution.py:339
  30.1 8.9 %collective-permute-start.12 = (bf16[1,144,512]{2,1,0:T(8,128)(2,1)S(1)}, bf16[1,144,512]{2,1,0:T(8,128)(2,1)S(1)}, u32[]{:S(2)}, u32[]{:S(2)}) collective-permute-start(bf16[1,144,512]{2,1,0:T(8,128)(2,1)S(1)} %get-tuple-element.37), channel_id=1, source_target_pairs={{4,8},{12,16},{20,24},{8,4},{16,12},{24,20},{5,9},{13,17},{21,25},... | collective-permute-start | bytes 442376 | tf_op jit(solution)/shard_map/ppermute | solution.py:339
  32.0 7.0 %collective-permute-start.9 = (bf16[1,144,512]{2,1,0:T(8,128)(2,1)S(1)}, bf16[1,144,512]{2,1,0:T(8,128)(2,1)S(1)}, u32[]{:S(2)}, u32[]{:S(2)}) collective-permute-start(bf16[1,144,512]{2,1,0:T(8,128)(2,1)S(1)} %get-tuple-element.38), channel_id=1, source_target_pairs={{0,4},{4,0},{8,12},{12,8},{16,20},{20,16},{24,28},{28,24},{1,5},{5... | collective-permute-start | bytes 442376 | tf_op jit(solution)/shard_map/ppermute | solution.py:338
  33.7 24.7 %collective-permute-start.5 = (bf16[2,112,512]{2,1,0:T(8,128)(2,1)}, bf16[2,112,512]{2,1,0:T(8,128)(2,1)S(1)}, u32[]{:S(2)}, u32[]{:S(2)}) collective-permute-start(bf16[2,112,512]{2,1,0:T(8,128)(2,1)} %get-tuple-element.27.refs_0_), channel_id=1, source_target_pairs={{0,3},{1,2},{2,1},{3,0},{4,7},{5,6},{6,5},{7,4},{8,11},{9,10},{10,... | collective-permute-start | bytes 688136 | tf_op jit(solution)/shard_map/ppermute | solution.py:351
  37.5 20.9 %collective-permute-start.4 = (bf16[2,112,512]{2,1,0:T(8,128)(2,1)}, bf16[2,112,512]{2,1,0:T(8,128)(2,1)S(1)}, u32[]{:S(2)}, u32[]{:S(2)}) collective-permute-start(bf16[2,112,512]{2,1,0:T(8,128)(2,1)} %get-tuple-element.27.refs_0_), channel_id=1, source_target_pairs={{0,2},{1,3},{2,0},{3,1},{4,6},{5,7},{6,4},{7,5},{8,10},{9,11},{10,... | collective-permute-start | bytes 688136 | tf_op jit(solution)/shard_map/ppermute | solution.py:351
  37.9 20.5 %collective-permute-start.3 = (bf16[2,112,512]{2,1,0:T(8,128)(2,1)}, bf16[2,112,512]{2,1,0:T(8,128)(2,1)S(1)}, u32[]{:S(2)}, u32[]{:S(2)}) collective-permute-start(bf16[2,112,512]{2,1,0:T(8,128)(2,1)} %get-tuple-element.27.refs_0_), channel_id=1, source_target_pairs={{0,1},{1,0},{2,3},{3,2},{4,5},{5,4},{6,7},{7,6},{8,9},{9,8},{10,11... | collective-permute-start | bytes 688136 | tf_op jit(solution)/shard_map/ppermute | solution.py:351
  39.0 1.0 copy-start.1
  40.0 0.7 copy-start.3
  40.6 0.7 copy-start.5
  41.3 0.9 copy-start.7
  42.2 0.7 copy-start.9
  42.9 0.7 copy-start.11
  58.5 26.8 %copy-start.4 = (s32[4]{0:T(128)S(1)}, s32[4]{0:T(128)}, u32[]{:S(2)}) copy-start(s32[4]{0:T(128)} %width_ref.9) | copy-start | bytes 52
  58.5 26.8 %copy-start.6 = (s32[4]{0:T(128)S(1)}, s32[4]{0:T(128)}, u32[]{:S(2)}) copy-start(s32[4]{0:T(128)} %height_ref.7) | copy-start | bytes 52
  58.5 26.8 %copy-start.8 = (f32[3,3,2,1400]{3,2,1,0:T(2,128)S(1)}, f32[3,3,2,1400]{3,2,1,0:T(2,128)}, u32[]{:S(2)}) copy-start(f32[3,3,2,1400]{3,2,1,0:T(2,128)} %refs_8_.1) | copy-start | bytes 302404
  58.5 26.8 %copy-start.10 = (f32[2,1400]{1,0:T(2,128)S(1)}, f32[2,1400]{1,0:T(2,128)}, u32[]{:S(2)}) copy-start(f32[2,1400]{1,0:T(2,128)} %refs_7_.1) | copy-start | bytes 33604
  58.6 26.8 %copy-start.12 = (f32[2,1400]{1,0:T(2,128)S(1)}, f32[2,1400]{1,0:T(2,128)}, u32[]{:S(2)}) copy-start(f32[2,1400]{1,0:T(2,128)} %refs_9_.1) | copy-start | bytes 33604
  58.7 26.6 %collective-permute-start.15 = (bf16[4,112,512]{2,1,0:T(8,128)(2,1)S(1)}, bf16[4,112,512]{2,1,0:T(8,128)(2,1)S(1)}, u32[]{:S(2)}, u32[]{:S(2)}) collective-permute-start(bf16[4,112,512]{2,1,0:T(8,128)(2,1)S(1)} %pad_maximum_fusion), channel_id=1, source_target_pairs={{0,4},{4,0},{8,12},{12,8},{16,20},{20,16},{24,28},{28,24},{1,5},{5... | collective-permute-start | bytes 1376264 | tf_op jit(solution)/shard_map/ppermute | solution.py:338
  61.5 23.8 %collective-permute-start.16 = (bf16[4,112,512]{2,1,0:T(8,128)(2,1)}, bf16[4,112,512]{2,1,0:T(8,128)(2,1)S(1)}, u32[]{:S(2)}, u32[]{:S(2)}) collective-permute-start(bf16[4,112,512]{2,1,0:T(8,128)(2,1)} %pad_maximum_fusion.1), channel_id=1, source_target_pairs={{4,8},{12,16},{20,24},{8,4},{16,12},{24,20},{5,9},{13,17},{21,25},... | collective-permute-start | bytes 1376264 | tf_op jit(solution)/shard_map/ppermute | solution.py:339
  63.4 2.8 %copy-start = (bf16[1400,2240]{0,1:T(8,128)(2,1)S(1)}, bf16[1400,2240]{0,1:T(8,128)(2,1)}, u32[]{:S(2)}) copy-start(bf16[1400,2240]{0,1:T(8,128)(2,1)} %param.15) | copy-start | bytes 18816004
  66.8 8.9 %collective-permute-start.14 = (bf16[1120,128]{1,0:T(8,128)(2,1)S(1)}, bf16[1120,128]{1,0:T(8,128)(2,1)S(1)}, u32[]{:S(2)}, u32[]{:S(2)}) collective-permute-start(bf16[1120,128]{1,0:T(8,128)(2,1)S(1)} %project_3.2), channel_id=1, source_target_pairs={{1,2},{2,1},{5,6},{6,5},{9,10},{10,9},{13,14},{14,13},{17,18},{18,... | collective-permute-start | bytes 860168 | tf_op jit(solution)/shard_map/ppermute | solution.py:436
  67.5 14.5 %collective-permute-start.13 = (bf16[1120,128]{1,0:T(8,128)(2,1)S(1)}, bf16[1120,128]{1,0:T(8,128)(2,1)S(1)}, u32[]{:S(2)}, u32[]{:S(2)}) collective-permute-start(bf16[1120,128]{1,0:T(8,128)(2,1)S(1)} %project_3.2), channel_id=1, source_target_pairs={{0,1},{3,2},{4,5},{7,6},{8,9},{11,10},{12,13},{15,14},{16,17},{19,... | collective-permute-start | bytes 860168 | tf_op jit(solution)/shard_map/ppermute | solution.py:435
  75.7 23.2 %slice-start = ((s8[6307840]{0:T(1024)(128)(4,1)}), s8[4194304]{0:T(1024)(128)(4,1)S(1)}, s32[]{:S(2)}) async-start(s8[6307840]{0:T(1024)(128)(4,1)} %bitcast.5), calls=%async_computation | async-start | bytes 8388608
  82.7 16.3 %slice-start.1 = ((s8[6307840]{0:T(1024)(128)(4,1)}), s8[2113536]{0:T(1024)(128)(4,1)S(1)}, s32[]{:S(2)}) async-start(s8[6307840]{0:T(1024)(128)(4,1)} %bitcast.5), calls=%async_computation.1 | async-start | bytes 4227072
  82.7 16.3 %collective-permute-start.17 = (bf16[1120,128]{1,0:T(8,128)(2,1)S(1)}, bf16[1120,128]{1,0:T(8,128)(2,1)S(1)}, u32[]{:S(2)}, u32[]{:S(2)}) collective-permute-start(bf16[1120,128]{1,0:T(8,128)(2,1)S(1)} %project_2.2), channel_id=1, source_target_pairs={{0,2},{1,3},{2,0},{3,1},{4,6},{5,7},{6,4},{7,5},{8,10},{9,11},{10,... | collective-permute-start | bytes 860168 | tf_op jit(solution)/shard_map/ppermute | solution.py:442
  85.1 13.9 %collective-permute-start.18 = (bf16[1120,128]{1,0:T(8,128)(2,1)S(1)}, bf16[1120,128]{1,0:T(8,128)(2,1)S(1)}, u32[]{:S(2)}, u32[]{:S(2)}) collective-permute-start(bf16[1120,128]{1,0:T(8,128)(2,1)S(1)} %project_1.2), channel_id=1, source_target_pairs={{0,1},{1,0},{2,3},{3,2},{4,5},{5,4},{6,7},{7,6},{8,9},{9,8},{10,11... | collective-permute-start | bytes 860168 | tf_op jit(solution)/shard_map/ppermute | solution.py:443
  99.7 7.3 %collective-permute-start.20 = (bf16[848,128]{1,0:T(8,128)(2,1)S(1)}, bf16[848,128]{1,0:T(8,128)(2,1)S(1)}, u32[]{:S(2)}, u32[]{:S(2)}) collective-permute-start(bf16[848,128]{1,0:T(8,128)(2,1)S(1)} %project_3.3), channel_id=1, source_target_pairs={{1,2},{2,1},{5,6},{6,5},{9,10},{10,9},{13,14},{14,13},{17,18},{18,... | collective-permute-start | bytes 651272 | tf_op jit(solution)/shard_map/ppermute | solution.py:436
  100.4 9.7 %collective-permute-start.19 = (bf16[848,128]{1,0:T(8,128)(2,1)S(1)}, bf16[848,128]{1,0:T(8,128)(2,1)S(1)}, u32[]{:S(2)}, u32[]{:S(2)}) collective-permute-start(bf16[848,128]{1,0:T(8,128)(2,1)S(1)} %project_3.3), channel_id=1, source_target_pairs={{0,1},{3,2},{4,5},{7,6},{8,9},{11,10},{12,13},{15,14},{16,17},{19,... | collective-permute-start | bytes 651272 | tf_op jit(solution)/shard_map/ppermute | solution.py:435
  110.7 12.5 %collective-permute-start.21 = (bf16[848,128]{1,0:T(8,128)(2,1)S(1)}, bf16[848,128]{1,0:T(8,128)(2,1)S(1)}, u32[]{:S(2)}, u32[]{:S(2)}) collective-permute-start(bf16[848,128]{1,0:T(8,128)(2,1)S(1)} %project_2.3), channel_id=1, source_target_pairs={{0,2},{1,3},{2,0},{3,1},{4,6},{5,7},{6,4},{7,5},{8,10},{9,11},{10,... | collective-permute-start | bytes 651272 | tf_op jit(solution)/shard_map/ppermute | solution.py:442
  114.3 9.8 %collective-permute-start.22 = (bf16[848,128]{1,0:T(8,128)(2,1)S(1)}, bf16[848,128]{1,0:T(8,128)(2,1)S(1)}, u32[]{:S(2)}, u32[]{:S(2)}) collective-permute-start(bf16[848,128]{1,0:T(8,128)(2,1)S(1)} %project_1.3), channel_id=1, source_target_pairs={{0,1},{1,0},{2,3},{3,2},{4,5},{5,4},{6,7},{7,6},{8,9},{9,8},{10,11... | collective-permute-start | bytes 651272 | tf_op jit(solution)/shard_map/ppermute | solution.py:443
where the time goes:
time: 127 us; the launch traced here: 126 us
  starting transfers between devices  46.2 us (36%)
  Pallas kernels  37 us (29%)
  waiting for transfers between devices  33 us (26%)
  local copies, waits for them, and re-layouts  8.54 us (7%)
    pallas_call x2, Pallas kernels, on_device_packed(): pl.pallas_call(functools.partial(hidden_kernel, chunk=chunk, shards=shard...  26.8 us
    ppermute x2, starting transfers between devices, on_device_packed(): relayed = lax.ppermute(far, 'tensor', from_end)  13.5 us
    ppermute x2, waiting for transfers between devices, on_device_packed(): relayed = lax.ppermute(far, 'tensor', from_end)  9.28 us
    ppermute x2, waiting for transfers between devices, on_device_packed(): lax.ppermute(last_unit, 'tensor', two_off)  9.16 us
    ppermute x4, starting transfers between devices, halos(): lax.ppermute(x, 'row', beyond)  8.37 us
    ppermute x1, waiting for transfers between devices, relay(): second = lax.ppermute(mine, 'tensor', two_off)  7.52 us
    unnamed x30, local copies, waits for them, and re-layouts  7.41 us
    ppermute x1, waiting for transfers between devices, relay(): passed = lax.ppermute(second, 'tensor', to_end)  6.2 us
  transfers between devices with their start and end apart: 23, of which 7 were waited for; matrix products, arithmetic and copies ran while one was open for 2% of the time, Pallas kernels for 24%

commit v1 on v0

--- a/solution.py
+++ b/solution.py
@@ -154,9 +154,13 @@
     return h + h * jnp.tanh(h)
 
 
-def pack_kernel(width_ref, x_ref, *out_refs, chunks):
+def pack_kernel(height_ref, width_ref, x_ref, *refs, chunks):
     parity = parity_of()
-    for chunk, out_ref in zip(chunks, out_refs):
+    out_refs, mask_refs = refs[: len(chunks)], refs[len(chunks) :]
+    for chunk, out_ref, mask_ref in zip(chunks, out_refs, mask_refs):
+        for place in range(4):
+            row_id = lax.axis_index("row") * 2 + row_of(place, parity)
+            mask_ref[place] = chunk.mask_column(height_ref, width_ref, row_id)
         for place in range(2):
             row = jnp.where(parity == 0, 1 - place, place)
             tails = []
@@ -176,76 +180,134 @@
                 ]
 
 
-def hidden_kernel(height_ref, width_ref, *refs, chunk, shards, groups, count):
-    own_refs = refs[:shards]
-    inner_refs = refs[shards : shards + count]
-    outer_refs = refs[shards + count : shards + 2 * count]
-    w_ref, eb_ref, dw_ref, db_ref, out_ref, x_scr, m_scr, e_scr = refs[shards + 2 * count :]
-    kept, rest, depth = chunk.kept, chunk.rest, chunk.depth
+def tiles_of(hidden_count):
+    return [slice(at, min(at + TILE, hidden_count)) for at in range(0, hidden_count, TILE)]
+
+
+def gather_rows(x_scr, chunk, rows):
+    kept = chunk.kept
+    for place, packets in enumerate(rows):
+        lines = slice(place * kept, (place + 1) * kept)
+        tails = []
+        for j, packet in enumerate(packets):
+            x_scr[lines, j * LANES : (j + 1) * LANES] = packet[:kept, :]
+            for down, over in chunk.places:
+                tails.append(packet[kept + down : kept + down + GROUP, over : over + chunk.block])
+        turned = jnp.concatenate(tails, axis=0).astype(jnp.float32).T
+        x_scr[lines, len(packets) * LANES :] = turned[:kept].astype(jnp.bfloat16)
+
+
+def load_kernel(w_ref, out_ref, token_ref, sems, *, shards, depth):
     me = lax.axis_index("tensor")
+    rest = depth - LANES
+    copies = []
+    for k in range(2):
+        for j in range(shards):
+            base = lax.bitwise_xor(me, j) * depth
+            for part, (source, size, target) in enumerate(
+                ((base, LANES, j * LANES), (base + LANES, rest, shards * LANES + j * rest))
+            ):
+                copies.append(
+                    pltpu.make_async_copy(
+                        w_ref.at[k, pl.ds(pl.multiple_of(source, GROUP), size)],
+                        out_ref.at[k, pl.ds(target, size)],
+                        sems.at[k, j, part],
+                    )
+                )
+    for copy in copies:
+        copy.start()
+    token_ref[...] = jnp.zeros_like(token_ref)
+    for copy in copies:
+        copy.wait()
+
+
+def expand(x_scr, w_ref, par_ref, k, units):
+    pre_act = jnp.dot(x_scr[...], w_ref[k, :, units], preferred_element_type=jnp.float32)
+    return silu(pre_act + par_ref[18 + k : 19 + k, units])
+
+
+def masked(cells, mask):
+    width = cells.shape[1]
+    return cells * jnp.concatenate([mask] * -(-width // 128), axis=1)[:, :width]
+
+
+def own_kernel(*refs, chunk, shards):
+    packet_refs, (mask_ref, par_ref, w_ref, out_ref, x_scr) = refs[:shards], refs[shards:]
+    kept = chunk.kept
+    gather_rows(x_scr, chunk, [[p.at[1] for p in packet_refs], [p.at[0] for p in packet_refs]])
+    mask = jnp.concatenate([mask_ref[1], mask_ref[2]], axis=0)
+    for units in tiles_of(w_ref.shape[2]):
+        for k in range(2):
+            out_ref[k, :, units] = masked(expand(x_scr, w_ref, par_ref, k, units), mask)
+
+
+def hidden_kernel(*refs, chunk, shards, groups):
+    count = len(groups)
+    inner_refs, outer_refs = refs[:count], refs[count : 2 * count]
+    own_ref, mask_ref, par_ref, w_ref, out_ref, x_scr = refs[2 * count :]
+    kept = chunk.kept
     parity = parity_of()
-    subs = w_ref.shape[2] // TILE
-
-    @pl.when(pl.program_id(0) == 0)
-    def _():
-        spots = {j: (g, i) for g, js in enumerate(groups) for i, j in enumerate(js)}
-        for place in range(4):
-            tails = []
-            lines = slice(place * kept, (place + 1) * kept)
-            for j in range(shards):
-                g, i = spots[j]
-                packet = (
-                    outer_refs[g].at[i],
-                    own_refs[j].at[1],
-                    own_refs[j].at[0],
-                    inner_refs[g].at[i],
-                )[place]
-                x_scr[lines, j * LANES : (j + 1) * LANES] = packet[:kept, :]
-                for down, over in chunk.places:
-                    tails.append(packet[kept + down : kept + down + GROUP, over : over + chunk.block])
-            turned = jnp.concatenate(tails, axis=0).astype(jnp.float32).T
-            x_scr[lines, shards * LANES :] = turned[:kept].astype(jnp.bfloat16)
-            row_id = lax.axis_index("row") * 2 + row_of(place, parity)
-            m_scr[lines, :] = chunk.mask_column(height_ref, width_ref, row_id)
-
-    bases = [pl.multiple_of(lax.bitwise_xor(me, j) * depth, GROUP) for j in range(shards)]
-    for sub in range(subs):
-        units = slice(sub * TILE, (sub + 1) * TILE)
+    spots = {j: (g, i) for g, js in enumerate(groups) for i, j in enumerate(js)}
+    gather_rows(
+        x_scr,
+        chunk,
+        [[refs_of[spots[j][0]].at[spots[j][1]] for j in range(shards)] for refs_of in (outer_refs, inner_refs)],
+    )
+    mask = jnp.concatenate([mask_ref[0], mask_ref[3]], axis=0)
+
+    def around(units):
+        return [
+            masked(expand(x_scr, w_ref, par_ref, k, units), mask) for k in range(2)
+        ]
+
+    def convolve(units, cells):
+        width = units.stop - units.start
+        line = lax.broadcasted_iota(jnp.int32, (kept, width), 0)
+        not_first, not_last = None, None
+        for at, size in zip(chunk.starts, chunk.widths):
+            first, last = line != at, line != at + size - 1
+            not_first = first if not_first is None else not_first & first
+            not_last = last if not_last is None else not_last & last
+        halves = ([], [])
         for k in range(2):
-            weight = jnp.concatenate(
-                [w_ref[k, pl.ds(base, LANES), units] for base in bases]
-                + [w_ref[k, pl.ds(pl.multiple_of(base + LANES, GROUP), rest), units] for base in bases],
-                axis=0,
-            )
-            pre_act = jnp.dot(x_scr[...], weight, preferred_element_type=jnp.float32)
-            mask = jnp.concatenate([m_scr[...]] * (TILE // 128), axis=1)
-            e_scr[sub, k] = silu(pre_act + eb_ref[k : k + 1, units]) * mask
-
-    line = lax.broadcasted_iota(jnp.int32, (kept, TILE), 0)
-    not_first, not_last = None, None
-    for at, width in zip(chunk.starts, chunk.widths):
-        first, last = line != at, line != at + width - 1
-        not_first = first if not_first is None else not_first & first
-        not_last = last if not_last is None else not_last & last
-    for sub in range(subs):
-        units = slice(sub * TILE, (sub + 1) * TILE)
-        for place in (1, 2):
-            halves = []
-            for k in range(2):
+            rows = [
+                cells[k][:kept],
+                own_ref[k, :kept, units],
+                own_ref[k, kept:, units],
+                cells[k][kept:],
+            ]
+            taps = [
+                [
+                    jnp.where(
+                        parity == 0,
+                        par_ref[i * 6 + col * 2 + k : i * 6 + col * 2 + k + 1, units],
+                        par_ref[(2 - i) * 6 + col * 2 + k : (2 - i) * 6 + col * 2 + k + 1, units],
+                    )
+                    for col in range(3)
+                ]
+                for i in range(3)
+            ]
+            for place in range(2):
                 sums = []
                 for tap_col in range(3):
                     total = None
                     for i in range(3):
-                        tap_row = jnp.where(parity == 0, i, 2 - i)
-                        cells = e_scr[sub, k, (place + i - 1) * kept : (place + i) * kept, :]
-                        term = dw_ref[tap_row, tap_col, k : k + 1, units] * cells
+                        term = taps[i][tap_col] * rows[place + i]
                         total = term if total is None else total + term
                     sums.append(total)
                 left = jnp.where(not_first, pltpu.roll(sums[0], 1, 0), 0.0)
                 right = jnp.where(not_last, pltpu.roll(sums[2], kept - 1, 0), 0.0)
-                halves.append(sums[1] + left + right + db_ref[k : k + 1, units])
-            hidden = halves[0] * silu(halves[1])
-            out_ref[(2 - place) * kept : (3 - place) * kept, units] = hidden.astype(jnp.bfloat16)
+                halves[k].append(sums[1] + left + right + par_ref[20 + k : 21 + k, units])
+        for place in range(2):
+            hidden = halves[0][place] * silu(halves[1][place])
+            out_ref[(1 - place) * kept : (2 - place) * kept, units] = hidden.astype(jnp.bfloat16)
+
+    tiles = tiles_of(w_ref.shape[2])
+    cells = around(tiles[0])
+    for t, units in enumerate(tiles):
+        coming = around(tiles[t + 1]) if t + 1 < len(tiles) else None
+        convolve(units, cells)
+        cells = coming
 
 
 def project(weight_ref, hidden_ref):
@@ -265,7 +327,7 @@
     chunk.put_unit(out_ref, sums.astype(jnp.bfloat16))
 
 
-def final_kernel(place_ref, height_ref, width_ref, weight_ref, hidden_ref, *refs, chunk, sources):
+def final_kernel(place_ref, width_ref, mask_ref, weight_ref, hidden_ref, *refs, chunk, sources):
     out_ref = refs[-1]
     if len(refs) > sources + 1:
         out_ref[...] = refs[sources][...]
@@ -276,8 +338,7 @@
     parity = parity_of()
     for place in range(2):
         row = jnp.where(parity == 0, 1 - place, place)
-        row_id = lax.axis_index("row") * 2 + row
-        mask = chunk.mask_column(height_ref, width_ref, row_id)[:, :1] > 0
+        mask = mask_ref[2 - place][:, :1] > 0
         part = cells[place * chunk.kept : (place + 1) * chunk.kept]
         part = jnp.where(mask, part, 0.0).astype(jnp.bfloat16)
         clips = chunk.clips(width_ref, width_ref.shape[0])
@@ -311,14 +372,20 @@
     hidden_count = expand_weight.shape[2]
     full_depth = shards * depth
     chunks = chunks_of(batch_size, col_count, depth)
-    own = pl.pallas_call(
+    count = len(chunks)
+    packed = pl.pallas_call(
         functools.partial(pack_kernel, chunks=chunks),
-        out_shape=[jax.ShapeDtypeStruct((2, c.lines, LANES), jnp.bfloat16) for c in chunks],
+        out_shape=[jax.ShapeDtypeStruct((2, c.lines, LANES), jnp.bfloat16) for c in chunks]
+        + [jax.ShapeDtypeStruct((4, c.kept, 128), jnp.float32) for c in chunks],
         grid_spec=pltpu.PrefetchScalarGridSpec(
-            num_scalar_prefetch=1, grid=(), in_specs=[VMEM], out_specs=[VMEM] * len(chunks)
+            num_scalar_prefetch=2, grid=(), in_specs=[VMEM], out_specs=[VMEM] * (2 * count)
         ),
         name="pack",
-    )(clip_width, latents)
+    )(clip_height, clip_width, latents)
+    own, masks = packed[:count], packed[count:]
+    parameters = jnp.concatenate(
+        [depth_weight.reshape(18, hidden_count), expand_bias, depth_bias], axis=0
+    )
     me = lax.axis_index("tensor").astype(jnp.int32).reshape(1)
     project_turned = project_weight.T
 
@@ -339,11 +406,11 @@
             [lax.ppermute(x, "row", beyond) for x in outer],
         )
 
-    def relay(mine):
+    def relay(mine, token):
         second = lax.ppermute(mine, "tensor", two_off)
         first = lax.ppermute(mine, "tensor", near)
-        across = lax.ppermute(after(mine, second), "tensor", middle)
-        passed = lax.ppermute(second, "tensor", to_end)
+        across = lax.ppermute(after(mine, second, token), "tensor", middle)
+        passed = lax.ppermute(after(second, token), "tensor", to_end)
         return [mine, first, second, across + passed]
 
     def direct(mine):
@@ -352,7 +419,18 @@
         ]
 
     out = None
-    packets = relay(own[0])
+    weights, token = pl.pallas_call(
+        functools.partial(load_kernel, shards=shards, depth=depth),
+        out_shape=[
+            jax.ShapeDtypeStruct(expand_weight.shape, jnp.bfloat16),
+            jax.ShapeDtypeStruct((8, 128), jnp.float32),
+        ],
+        in_specs=[pl.BlockSpec(memory_space=pl.ANY)],
+        out_specs=[VMEM, VMEM],
+        scratch_shapes=[pltpu.SemaphoreType.DMA((2, shards, 2))],
+        name="load_weights",
+    )(after(expand_weight, own[0]))
+    packets = relay(own[0], token)
     groups = ((0,), (1, 2), (3,))
     inner, outer = halos(packets, groups)
     upcoming = direct(after(own[1], packets[3]))
@@ -360,50 +438,38 @@
         if number:
             packets, groups = list(lax.optimization_barrier((*upcoming, hidden))[:shards]), ((0, 1, 2, 3),)
             inner, outer = halos(packets, groups)
-            packets[0] = after(packets[0], last_unit)
-        wide = 2 * TILE
+            packets[0] = after(packets[0], far)
         whole = lambda shape: pl.BlockSpec(shape, lambda f, *_: (0,) * len(shape))
-        lines = 4 * chunk.kept
+        rows = pl.pallas_call(
+            functools.partial(own_kernel, chunk=chunk, shards=shards),
+            out_shape=jax.ShapeDtypeStruct((2, chunk.tokens, hidden_count), jnp.float32),
+            in_specs=[VMEM] * (shards + 3),
+            out_specs=VMEM,
+            scratch_shapes=[pltpu.VMEM((chunk.tokens, full_depth), jnp.bfloat16)],
+            compiler_params=pltpu.CompilerParams(vmem_limit_bytes=16 * MIB),
+            cost_estimate=pl.CostEstimate(
+                flops=4 * chunk.tokens * full_depth * hidden_count,
+                bytes_accessed=4 * full_depth * hidden_count,
+                transcendentals=2 * chunk.tokens * hidden_count,
+            ),
+            name="expand_own",
+        )(*packets, masks[number], parameters, weights)
+        if number:
+            inner[0] = after(inner[0], last_unit)
         hidden = pl.pallas_call(
-            functools.partial(
-                hidden_kernel, chunk=chunk, shards=shards, groups=groups, count=len(groups)
-            ),
+            functools.partial(hidden_kernel, chunk=chunk, shards=shards, groups=groups),
             out_shape=jax.ShapeDtypeStruct((chunk.tokens, hidden_count), jnp.bfloat16),
-            grid_spec=pltpu.PrefetchScalarGridSpec(
-                num_scalar_prefetch=2,
-                grid=(-(-hidden_count // wide),),
-                in_specs=[whole(p.shape) for p in packets + inner + outer]
-                + [
-                    pl.BlockSpec((2, full_depth, wide), lambda f, *_: (0, 0, f)),
-                    pl.BlockSpec((2, wide), lambda f, *_: (0, f)),
-                    pl.BlockSpec((3, 3, 2, wide), lambda f, *_: (0, 0, 0, f)),
-                    pl.BlockSpec((2, wide), lambda f, *_: (0, f)),
-                ],
-                out_specs=pl.BlockSpec((chunk.tokens, wide), lambda f, *_: (0, f)),
-                scratch_shapes=[
-                    pltpu.VMEM((lines, full_depth), jnp.bfloat16),
-                    pltpu.VMEM((lines, 128), jnp.float32),
-                    pltpu.VMEM((2, 2, lines, TILE), jnp.float32),
-                ],
-            ),
-            compiler_params=pltpu.CompilerParams(vmem_limit_bytes=40 * MIB),
+            in_specs=[VMEM] * (2 * len(groups) + 4),
+            out_specs=VMEM,
+            scratch_shapes=[pltpu.VMEM((chunk.tokens, full_depth), jnp.bfloat16)],
+            compiler_params=pltpu.CompilerParams(vmem_limit_bytes=16 * MIB),
             cost_estimate=pl.CostEstimate(
-                flops=4 * lines * full_depth * hidden_count,
+                flops=4 * chunk.tokens * full_depth * hidden_count,
                 bytes_accessed=4 * full_depth * hidden_count,
-                transcendentals=3 * lines * hidden_count,
+                transcendentals=3 * chunk.tokens * hidden_count,
             ),
             name="expand_conv",
-        )(
-            clip_height,
-            clip_width,
-            *packets,
-            *inner,
-            *outer,
-            expand_weight,
-            expand_bias,
-            depth_weight,
-            depth_bias,
-        )
+        )(*inner, *outer, rows, masks[number], parameters, weights)
 
         weight_of = lambda j: pl.BlockSpec(
             (depth, hidden_count), lambda f, place, *_: (lax.bitwise_xor(place[0], j), 0)
@@ -447,9 +513,9 @@
             functools.partial(final_kernel, chunk=chunk, sources=len(arrived)),
             out_shape=jax.ShapeDtypeStruct(latents.shape, jnp.bfloat16),
             grid_spec=pltpu.PrefetchScalarGridSpec(
-                num_scalar_prefetch=3,
+                num_scalar_prefetch=2,
                 grid=(1,),
-                in_specs=[weight_of(0), whole(hidden.shape)]
+                in_specs=[whole(masks[number].shape), weight_of(0), whole(hidden.shape)]
                 + [whole(chunk.unit)] * len(arrived)
                 + [whole(latents.shape)] * len(extra),
                 out_specs=whole(latents.shape),
@@ -457,7 +523,7 @@
             compiler_params=pltpu.CompilerParams(vmem_limit_bytes=24 * MIB),
             cost_estimate=cost,
             name="finish",
-        )(me, clip_height, clip_width, project_turned, hidden, *arrived, *extra)
+        )(me, clip_width, masks[number], project_turned, hidden, *arrived, *extra)
     return out
 
 

time: 127 us -> 121 us (0.953)
  the two profiles are of different devices: /device:TPU:2 before, /device:TPU:0 now
where the time goes in v1:
time: 121 us; the launch traced here: 120 us
  starting transfers between devices  40.9 us (34%)
  Pallas kernels  38.6 us (32%)
  waiting for transfers between devices  32.6 us (27%)
  local copies, waits for them, and re-layouts  6.72 us (6%)
    ppermute x2, starting transfers between devices, on_device_packed(): lax.ppermute(after(close, relayed), 'tensor', near)  12.5 us
    pallas_call x2, Pallas kernels, on_device_packed(): pl.pallas_call(functools.partial(hidden_kernel, chunk=chunk, shards=shard...  11.9 us
    pallas_call x1, Pallas kernels, on_device_packed(): pl.pallas_call(functools.partial(load_kernel, shards=shards, depth=depth)...  9.33 us
    ppermute x2, waiting for transfers between devices, on_device_packed(): lax.ppermute(last_unit, 'tensor', two_off)  8.8 us
    ppermute x4, starting transfers between devices, halos(): lax.ppermute(x, 'row', sibling)  8.79 us
    ppermute x2, waiting for transfers between devices, on_device_packed(): lax.ppermute(after(close, relayed), 'tensor', near)  8.64 us
    pallas_call x2, Pallas kernels, on_device_packed(): pl.pallas_call(functools.partial(own_kernel, chunk=chunk, shards=shards),...  7.02 us
    ppermute x1, waiting for transfers between devices, relay(): passed = lax.ppermute(after(second, token), 'tensor', to_end)  5.78 us
  transfers between devices with their start and end apart: 23, of which 8 were waited for; matrix products, arithmetic and copies ran while one was open for 3% of the time, Pallas kernels for 27%

profile of v1, /device:TPU:0, one launch (start us, length us, event | category | flops | bytes accessed | tf_op | source)
XLA Modules:
  0.0 120.2 jit_solution(12766791799401273661)
XLA Ops:
  0.0 2.8 %pack.1 = (bf16[2,144,512]{2,1,0:T(8,128)(2,1)}, bf16[2,112,512]{2,1,0:T(8,128)(2,1)}, f32[4,128,128]{2,1,0:T(8,128)}, f32[4,96,128]{2,1,0:T(8,128)}) custom-call(s32[4]{0:T(128)} %height_ref.1, s32[4]{0:T(128)} %width_ref.5, bf16[4,2,64,560]{3,2,1,0:T(8,128)(2,1)} %x_ref.1), custom_call_target="tpu_custom_call" | custom-call | tf_op jit(solution)/shard_map/pack/pallas_call | solution.py:376
  2.8 4.0 %collective-permute-start = (bf16[2,144,512]{2,1,0:T(8,128)(2,1)}, bf16[2,144,512]{2,1,0:T(8,128)(2,1)S(1)}, u32[]{:S(2)}, u32[]{:S(2)}) collective-permute-start(bf16[2,144,512]{2,1,0:T(8,128)(2,1)} %get-tuple-element.33.refs_0_), channel_id=1, source_target_pairs={{0,2},{1,3},{2,0},{3,1},{4,6},{5,7},{6,4},{7,5},{8,10},{9,11},{10,... | collective-permute-start | bytes 884744 | tf_op jit(solution)/shard_map/ppermute | solution.py:410
  6.8 1.6 %collective-permute-start.7 = (bf16[2,144,512]{2,1,0:T(8,128)(2,1)}, bf16[2,144,512]{2,1,0:T(8,128)(2,1)S(1)}, u32[]{:S(2)}, u32[]{:S(2)}) collective-permute-start(bf16[2,144,512]{2,1,0:T(8,128)(2,1)} %get-tuple-element.33.refs_0_), channel_id=1, source_target_pairs={{0,1},{1,0},{2,3},{3,2},{4,5},{5,4},{6,7},{7,6},{8,9},{9,8},{10,11... | collective-permute-start | bytes 884744 | tf_op jit(solution)/shard_map/ppermute | solution.py:411
  8.4 1.0 fusion.3
  9.4 0.7 collective-permute-start.10
  10.1 2.9 %collective-permute-start.6 = (bf16[1,144,512]{2,1,0:T(8,128)(2,1)S(1)}, bf16[1,144,512]{2,1,0:T(8,128)(2,1)S(1)}, u32[]{:S(2)}, u32[]{:S(2)}) collective-permute-start(bf16[1,144,512]{2,1,0:T(8,128)(2,1)S(1)} %get-tuple-element.58), channel_id=1, source_target_pairs={{0,4},{4,0},{8,12},{12,8},{16,20},{20,16},{24,28},{28,24},{1,5},{5... | collective-permute-start | bytes 442376 | tf_op jit(solution)/shard_map/ppermute | solution.py:405
  13.0 1.0 reshape.7
  13.9 0.8 pad_maximum_fusion.4.refs_5_.refs_8_.refs_4_
  14.7 9.3 %load_weights.1 = (bf16[2,2240,1400]{2,1,0:T(8,128)(2,1)}, f32[8,128]{1,0:T(8,128)}) custom-call(bf16[2,2240,1400]{2,1,0:T(8,128)(2,1)} %w_ref), custom_call_target="tpu_custom_call" | custom-call | tf_op jit(solution)/shard_map/load_weights/pallas_call | solution.py:422
  24.1 0.7 collective-permute-start.1
  24.8 1.3 %collective-permute-start.2 = (bf16[2,144,512]{2,1,0:T(8,128)(2,1)S(1)}, bf16[2,144,512]{2,1,0:T(8,128)(2,1)S(1)}, u32[]{:S(2)}, u32[]{:S(2)}) collective-permute-start(bf16[2,144,512]{2,1,0:T(8,128)(2,1)S(1)} %collective-permute-done.refs_2_), channel_id=1, source_target_pairs={{2,3},{1,0},{6,7},{5,4},{10,11},{9,8},{14,15},{13,12},{18,19},{17,... | collective-permute-start | bytes 884744 | tf_op jit(solution)/shard_map/ppermute | solution.py:413
  26.2 0.7 collective-permute-start.11
  26.9 2.9 %collective-permute-start.8 = (bf16[2,144,512]{2,1,0:T(8,128)(2,1)S(1)}, bf16[2,144,512]{2,1,0:T(8,128)(2,1)S(1)}, u32[]{:S(2)}, u32[]{:S(2)}) collective-permute-start(bf16[2,144,512]{2,1,0:T(8,128)(2,1)S(1)} %pad_maximum_fusion.2), channel_id=1, source_target_pairs={{0,4},{4,0},{8,12},{12,8},{16,20},{20,16},{24,28},{28,24},{1,5},{5... | collective-permute-start | bytes 884744 | tf_op jit(solution)/shard_map/ppermute | solution.py:405
  29.8 5.8 %collective-permute-done.2 = bf16[2,144,512]{2,1,0:T(8,128)(2,1)S(1)} collective-permute-done((bf16[2,144,512]{2,1,0:T(8,128)(2,1)S(1)}, bf16[2,144,512]{2,1,0:T(8,128)(2,1)S(1)}, u32[]{:S(2)}, u32[]{:S(2)}) %collective-permute-start.2) | collective-permute-done | bytes 294944 | tf_op jit(solution)/shard_map/ppermute | solution.py:413
  35.6 0.1 add.3.refs_3_
  35.7 0.7 collective-permute-start.12
  36.4 2.9 %collective-permute-start.9 = (bf16[1,144,512]{2,1,0:T(8,128)(2,1)S(1)}, bf16[1,144,512]{2,1,0:T(8,128)(2,1)S(1)}, u32[]{:S(2)}, u32[]{:S(2)}) collective-permute-start(bf16[1,144,512]{2,1,0:T(8,128)(2,1)S(1)} %get-tuple-element.52), channel_id=1, source_target_pairs={{0,4},{4,0},{8,12},{12,8},{16,20},{20,16},{24,28},{28,24},{1,5},{5... | collective-permute-start | bytes 442376 | tf_op jit(solution)/shard_map/ppermute | solution.py:405
  39.3 4.6 %copy-done = bf16[2,2240,1400]{2,1,0:T(8,128)(2,1)S(1)} copy-done((bf16[2,2240,1400]{2,1,0:T(8,128)(2,1)S(1)}, bf16[2,2240,1400]{2,1,0:T(8,128)(2,1)}, u32[]{:S(2)}) %copy-start) | copy-done | bytes 12544024
  43.9 4.0 %expand_own.2.refs_6_ = f32[2,256,1400]{2,1,0:T(8,128)S(1)} custom-call(bf16[2,144,512]{2,1,0:T(8,128)(2,1)S(1)} %copy-done.4, bf16[2,144,512]{2,1,0:T(8,128)(2,1)S(1)} %collective-permute-done.7.refs_1_, bf16[2,144,512]{2,1,0:T(8,128)(2,1)S(1)} %collective-permute-done.refs_2_, bf16[2,144,512]{2,1,0:T(8,128)(2,1)S(1)} %add.3.refs_3_, ...), custom_call_target="tpu_custom_call" | custom-call | flops 3211264000 | bytes 12544000 | tf_op jit(solution)/shard_map/expand_own/pallas_call | solution.py:443
  47.9 0.1 collective-permute-start.3
  48.0 2.5 %collective-permute-start.4 = (bf16[2,112,512]{2,1,0:T(8,128)(2,1)S(1)}, bf16[2,112,512]{2,1,0:T(8,128)(2,1)S(1)}, u32[]{:S(2)}, u32[]{:S(2)}) collective-permute-start(bf16[2,112,512]{2,1,0:T(8,128)(2,1)S(1)} %copy-done.5), channel_id=1, source_target_pairs={{0,2},{1,3},{2,0},{3,1},{4,6},{5,7},{6,4},{7,5},{8,10},{9,11},{10,... | collective-permute-start | bytes 688136 | tf_op jit(solution)/shard_map/ppermute | solution.py:418
  50.5 1.9 %collective-permute-start.5 = (bf16[2,112,512]{2,1,0:T(8,128)(2,1)S(1)}, bf16[2,112,512]{2,1,0:T(8,128)(2,1)S(1)}, u32[]{:S(2)}, u32[]{:S(2)}) collective-permute-start(bf16[2,112,512]{2,1,0:T(8,128)(2,1)S(1)} %copy-done.5), channel_id=1, source_target_pairs={{0,3},{1,2},{2,1},{3,0},{4,7},{5,6},{6,5},{7,4},{8,11},{9,10},{10,... | collective-permute-start | bytes 688136 | tf_op jit(solution)/shard_map/ppermute | solution.py:418
  52.4 6.8 %expand_conv.2.hidden_ref = bf16[256,1400]{1,0:T(8,128)(2,1)S(1)} custom-call(bf16[1,144,512]{2,1,0:T(8,128)(2,1)S(1)} %collective-permute-done.6.refs_0_, bf16[2,144,512]{2,1,0:T(8,128)(2,1)S(1)} %collective-permute-done.8.refs_1_, bf16[1,144,512]{2,1,0:T(8,128)(2,1)S(1)} %collective-permute-done.9.refs_2_, ...), custom_call_target="tpu_custom_call" | custom-call | flops 3211264000 | bytes 12544000 | tf_op jit(solution)/shard_map/expand_conv/pallas_call | solution.py:459
  59.2 0.6 project_3.2
  59.8 1.3 %collective-permute-start.14 = (bf16[1120,128]{1,0:T(8,128)(2,1)S(1)}, bf16[1120,128]{1,0:T(8,128)(2,1)S(1)}, u32[]{:S(2)}, u32[]{:S(2)}) collective-permute-start(bf16[1120,128]{1,0:T(8,128)(2,1)S(1)} %project_3.2), channel_id=1, source_target_pairs={{0,1},{3,2},{4,5},{7,6},{8,9},{11,10},{12,13},{15,14},{16,17},{19,... | collective-permute-start | bytes 860168 | tf_op jit(solution)/shard_map/ppermute | solution.py:501
  61.1 0.7 collective-permute-start.15
  61.8 5.4 %collective-permute-done.4.refs_2_ = bf16[2,112,512]{2,1,0:T(8,128)(2,1)S(1)} collective-permute-done((bf16[2,112,512]{2,1,0:T(8,128)(2,1)S(1)}, bf16[2,112,512]{2,1,0:T(8,128)(2,1)S(1)}, u32[]{:S(2)}, u32[]{:S(2)}) %collective-permute-start.4) | collective-permute-done | bytes 229408 | tf_op jit(solution)/shard_map/ppermute | solution.py:418
  67.4 0.1 collective-permute-start.13
  67.6 1.0 collective-permute-start.16
  68.6 0.6 project_1.2
  69.3 8.7 %collective-permute-start.18 = (bf16[1120,128]{1,0:T(8,128)(2,1)S(1)}, bf16[1120,128]{1,0:T(8,128)(2,1)S(1)}, u32[]{:S(2)}, u32[]{:S(2)}) collective-permute-start(bf16[1120,128]{1,0:T(8,128)(2,1)S(1)} %project_1.2), channel_id=1, source_target_pairs={{0,1},{1,0},{2,3},{3,2},{4,5},{5,4},{6,7},{7,6},{8,9},{9,8},{10,11... | collective-permute-start | bytes 860168 | tf_op jit(solution)/shard_map/ppermute | solution.py:509
  78.0 0.6 project_2.2
  78.6 0.6 collective-permute-start.17
  79.2 3.1 %expand_own.3.refs_2_ = f32[2,192,1400]{2,1,0:T(8,128)S(1)} custom-call(bf16[2,112,512]{2,1,0:T(8,128)(2,1)S(1)} %copy-done.5, bf16[2,112,512]{2,1,0:T(8,128)(2,1)S(1)} %collective-permute-done.3.refs_1_, bf16[2,112,512]{2,1,0:T(8,128)(2,1)S(1)} %collective-permute-done.4.refs_2_, bf16[2,112,512]{2,1,0:T(8,128)(2,1)S(1)} %collective-permute-done.5.refs_3_, ...), custom_call_target="tpu_custom_call" | custom-call | flops 2408448000 | bytes 12544000 | tf_op jit(solution)/shard_map/expand_own/pallas_call | solution.py:443
  82.3 5.1 %expand_conv.3.hidden_ref = bf16[192,1400]{1,0:T(8,128)(2,1)S(1)} custom-call(bf16[4,112,512]{2,1,0:T(8,128)(2,1)S(1)} %collective-permute-done.13.refs_0_, bf16[4,112,512]{2,1,0:T(8,128)(2,1)S(1)} %collective-permute-done.16.refs_1_, f32[2,192,1400]{2,1,0:T(8,128)S(1)} %expand_own.3.refs_2_, f32[4,96,128]{2,1,0:T(8,128)S(1)} %copy-done.3, ...), custom_call_target="tpu_custom_call" | custom-call | flops 2408448000 | bytes 12544000 | tf_op jit(solution)/shard_map/expand_conv/pallas_call | solution.py:459
  87.4 2.0 %collective-permute-done.18.refs_2_ = bf16[1120,128]{1,0:T(8,128)(2,1)S(1)} collective-permute-done((bf16[1120,128]{1,0:T(8,128)(2,1)S(1)}, bf16[1120,128]{1,0:T(8,128)(2,1)S(1)}, u32[]{:S(2)}, u32[]{:S(2)}) %collective-permute-start.18) | collective-permute-done | bytes 286752 | tf_op jit(solution)/shard_map/ppermute | solution.py:509
  89.5 4.5 %collective-permute-done.17.refs_1_ = bf16[1120,128]{1,0:T(8,128)(2,1)S(1)} collective-permute-done((bf16[1120,128]{1,0:T(8,128)(2,1)S(1)}, bf16[1120,128]{1,0:T(8,128)(2,1)S(1)}, u32[]{:S(2)}, u32[]{:S(2)}) %collective-permute-start.17) | collective-permute-done | bytes 286752 | tf_op jit(solution)/shard_map/ppermute | solution.py:508
  93.9 0.7 project_3.3
  94.6 1.3 %collective-permute-start.19 = (bf16[848,128]{1,0:T(8,128)(2,1)S(1)}, bf16[848,128]{1,0:T(8,128)(2,1)S(1)}, u32[]{:S(2)}, u32[]{:S(2)}) collective-permute-start(bf16[848,128]{1,0:T(8,128)(2,1)S(1)} %project_3.3), channel_id=1, source_target_pairs={{0,1},{3,2},{4,5},{7,6},{8,9},{11,10},{12,13},{15,14},{16,17},{19,... | collective-permute-start | bytes 651272 | tf_op jit(solution)/shard_map/ppermute | solution.py:501
  95.9 0.7 collective-permute-start.20
  96.6 0.7 project_1.3
  97.3 3.8 %collective-permute-done.19.refs_0_ = bf16[848,128]{1,0:T(8,128)(2,1)S(1)} collective-permute-done((bf16[848,128]{1,0:T(8,128)(2,1)S(1)}, bf16[848,128]{1,0:T(8,128)(2,1)S(1)}, u32[]{:S(2)}, u32[]{:S(2)}) %collective-permute-start.19) | collective-permute-done | bytes 217120 | tf_op jit(solution)/shard_map/ppermute | solution.py:501
  101.1 0.7 project_2.3
  101.8 3.8 %collective-permute-start.22 = (bf16[848,128]{1,0:T(8,128)(2,1)S(1)}, bf16[848,128]{1,0:T(8,128)(2,1)S(1)}, u32[]{:S(2)}, u32[]{:S(2)}) collective-permute-start(bf16[848,128]{1,0:T(8,128)(2,1)S(1)} %project_1.3), channel_id=1, source_target_pairs={{0,1},{1,0},{2,3},{3,2},{4,5},{5,4},{6,7},{7,6},{8,9},{9,8},{10,11... | collective-permute-start | bytes 651272 | tf_op jit(solution)/shard_map/ppermute | solution.py:509
  105.7 1.3 %finish.2.refs_3_ = bf16[4,2,64,560]{3,2,1,0:T(8,128)(2,1)S(1)} custom-call(s32[1]{0:T(128)} %bitcast.place_ref, s32[4]{0:T(128)S(1)} %copy-done.6, f32[4,128,128]{2,1,0:T(8,128)S(1)} %copy-done.2, bf16[2240,1400]{1,0:T(8,128)(2,1)S(1)} %bitcast.10, bf16[256,1400]{1,0:T(8,128)(2,1)S(1)} %expand_conv.2.hidden_ref, ...), custom_call_target="tpu_custom_call" | custom-call | flops 401408000 | bytes 2284800 | tf_op jit(solution)/shard_map/finish/pallas_call | solution.py:512
  107.0 6.6 %collective-permute-done.22.refs_2_ = bf16[848,128]{1,0:T(8,128)(2,1)S(1)} collective-permute-done((bf16[848,128]{1,0:T(8,128)(2,1)S(1)}, bf16[848,128]{1,0:T(8,128)(2,1)S(1)}, u32[]{:S(2)}, u32[]{:S(2)}) %collective-permute-start.22) | collective-permute-done | bytes 217120 | tf_op jit(solution)/shard_map/ppermute | solution.py:509
  113.6 4.3 %collective-permute-done.21.refs_1_ = bf16[848,128]{1,0:T(8,128)(2,1)S(1)} collective-permute-done((bf16[848,128]{1,0:T(8,128)(2,1)S(1)}, bf16[848,128]{1,0:T(8,128)(2,1)S(1)}, u32[]{:S(2)}, u32[]{:S(2)}) %collective-permute-start.21) | collective-permute-done | bytes 217120 | tf_op jit(solution)/shard_map/ppermute | solution.py:508
  118.0 2.2 %finish.3 = bf16[4,2,64,560]{3,2,1,0:T(8,128)(2,1)} custom-call(s32[1]{0:T(128)} %bitcast.place_ref, s32[4]{0:T(128)S(1)} %copy-done.6, f32[4,96,128]{2,1,0:T(8,128)S(1)} %copy-done.3, bf16[2240,1400]{1,0:T(8,128)(2,1)S(1)} %bitcast.11, bf16[192,1400]{1,0:T(8,128)(2,1)S(1)} %expand_conv.3.hidden_ref, bf16[848,128]{1,0:T(8,128)(2,1)S(1)} %collective-permute-done.20.refs_0_, ...), custom_call_target="tpu_custom_call" | custom-call | flops 301056000 | bytes 2105600 | tf_op jit(solution)/shard_map/finish/pallas_call | solution.py:512
  (44 shorter events, 0.4 us)
Async XLA Ops:
  2.8 21.3 %collective-permute-start = (bf16[2,144,512]{2,1,0:T(8,128)(2,1)}, bf16[2,144,512]{2,1,0:T(8,128)(2,1)S(1)}, u32[]{:S(2)}, u32[]{:S(2)}) collective-permute-start(bf16[2,144,512]{2,1,0:T(8,128)(2,1)} %get-tuple-element.33.refs_0_), channel_id=1, source_target_pairs={{0,2},{1,3},{2,0},{3,1},{4,6},{5,7},{6,4},{7,5},{8,10},{9,11},{10,... | collective-permute-start | bytes 884744 | tf_op jit(solution)/shard_map/ppermute | solution.py:410
  6.8 19.3 %collective-permute-start.7 = (bf16[2,144,512]{2,1,0:T(8,128)(2,1)}, bf16[2,144,512]{2,1,0:T(8,128)(2,1)S(1)}, u32[]{:S(2)}, u32[]{:S(2)}) collective-permute-start(bf16[2,144,512]{2,1,0:T(8,128)(2,1)} %get-tuple-element.33.refs_0_), channel_id=1, source_target_pairs={{0,1},{1,0},{2,3},{3,2},{4,5},{5,4},{6,7},{7,6},{8,9},{9,8},{10,11... | collective-permute-start | bytes 884744 | tf_op jit(solution)/shard_map/ppermute | solution.py:411
  9.4 27.0 %collective-permute-start.10 = (bf16[1,144,512]{2,1,0:T(8,128)(2,1)S(1)}, bf16[1,144,512]{2,1,0:T(8,128)(2,1)S(1)}, u32[]{:S(2)}, u32[]{:S(2)}) collective-permute-start(bf16[1,144,512]{2,1,0:T(8,128)(2,1)S(1)} %get-tuple-element.57), channel_id=1, source_target_pairs={{4,8},{12,16},{20,24},{8,4},{16,12},{24,20},{5,9},{13,17},{21,25},... | collective-permute-start | bytes 442376 | tf_op jit(solution)/shard_map/ppermute | solution.py:406
  10.1 37.8 %collective-permute-start.6 = (bf16[1,144,512]{2,1,0:T(8,128)(2,1)S(1)}, bf16[1,144,512]{2,1,0:T(8,128)(2,1)S(1)}, u32[]{:S(2)}, u32[]{:S(2)}) collective-permute-start(bf16[1,144,512]{2,1,0:T(8,128)(2,1)S(1)} %get-tuple-element.58), channel_id=1, source_target_pairs={{0,4},{4,0},{8,12},{12,8},{16,20},{20,16},{24,28},{28,24},{1,5},{5... | collective-permute-start | bytes 442376 | tf_op jit(solution)/shard_map/ppermute | solution.py:405
  14.7 9.4 %copy-start.4 = (bf16[2,144,512]{2,1,0:T(8,128)(2,1)S(1)}, bf16[2,144,512]{2,1,0:T(8,128)(2,1)}, u32[]{:S(2)}) copy-start(bf16[2,144,512]{2,1,0:T(8,128)(2,1)} %get-tuple-element.33.refs_0_) | copy-start | bytes 884740
  14.7 24.6 %copy-start.2 = (f32[4,128,128]{2,1,0:T(8,128)S(1)}, f32[4,128,128]{2,1,0:T(8,128)}, u32[]{:S(2)}) copy-start(f32[4,128,128]{2,1,0:T(8,128)} %get-tuple-element.36.refs_4_.refs_7_.mask_ref) | copy-start | bytes 786436
  24.1 2.8 %collective-permute-start.1 = (bf16[2,144,512]{2,1,0:T(8,128)(2,1)S(1)}, bf16[2,144,512]{2,1,0:T(8,128)(2,1)S(1)}, u32[]{:S(2)}, u32[]{:S(2)}) collective-permute-start(bf16[2,144,512]{2,1,0:T(8,128)(2,1)S(1)} %copy-done.4), channel_id=1, source_target_pairs={{1,2},{2,1},{5,6},{6,5},{9,10},{10,9},{13,14},{14,13},{17,18},{18,... | collective-permute-start | bytes 884744 | tf_op jit(solution)/shard_map/ppermute | solution.py:412
  24.8 10.8 %collective-permute-start.2 = (bf16[2,144,512]{2,1,0:T(8,128)(2,1)S(1)}, bf16[2,144,512]{2,1,0:T(8,128)(2,1)S(1)}, u32[]{:S(2)}, u32[]{:S(2)}) collective-permute-start(bf16[2,144,512]{2,1,0:T(8,128)(2,1)S(1)} %collective-permute-done.refs_2_), channel_id=1, source_target_pairs={{2,3},{1,0},{6,7},{5,4},{10,11},{9,8},{14,15},{13,12},{18,19},{17,... | collective-permute-start | bytes 884744 | tf_op jit(solution)/shard_map/ppermute | solution.py:413
  26.2 21.8 %collective-permute-start.11 = (bf16[2,144,512]{2,1,0:T(8,128)(2,1)S(1)}, bf16[2,144,512]{2,1,0:T(8,128)(2,1)S(1)}, u32[]{:S(2)}, u32[]{:S(2)}) collective-permute-start(bf16[2,144,512]{2,1,0:T(8,128)(2,1)S(1)} %pad_maximum_fusion.3), channel_id=1, source_target_pairs={{4,8},{12,16},{20,24},{8,4},{16,12},{24,20},{5,9},{13,17},{21,25},... | collective-permute-start | bytes 884744 | tf_op jit(solution)/shard_map/ppermute | solution.py:406
  26.9 23.6 %collective-permute-start.8 = (bf16[2,144,512]{2,1,0:T(8,128)(2,1)S(1)}, bf16[2,144,512]{2,1,0:T(8,128)(2,1)S(1)}, u32[]{:S(2)}, u32[]{:S(2)}) collective-permute-start(bf16[2,144,512]{2,1,0:T(8,128)(2,1)S(1)} %pad_maximum_fusion.2), channel_id=1, source_target_pairs={{0,4},{4,0},{8,12},{12,8},{16,20},{20,16},{24,28},{28,24},{1,5},{5... | collective-permute-start | bytes 884744 | tf_op jit(solution)/shard_map/ppermute | solution.py:405
  35.7 16.7 %collective-permute-start.12 = (bf16[1,144,512]{2,1,0:T(8,128)(2,1)S(1)}, bf16[1,144,512]{2,1,0:T(8,128)(2,1)S(1)}, u32[]{:S(2)}, u32[]{:S(2)}) collective-permute-start(bf16[1,144,512]{2,1,0:T(8,128)(2,1)S(1)} %get-tuple-element.51), channel_id=1, source_target_pairs={{4,8},{12,16},{20,24},{8,4},{16,12},{24,20},{5,9},{13,17},{21,25},... | collective-permute-start | bytes 442376 | tf_op jit(solution)/shard_map/ppermute | solution.py:406
  36.4 16.0 %collective-permute-start.9 = (bf16[1,144,512]{2,1,0:T(8,128)(2,1)S(1)}, bf16[1,144,512]{2,1,0:T(8,128)(2,1)S(1)}, u32[]{:S(2)}, u32[]{:S(2)}) collective-permute-start(bf16[1,144,512]{2,1,0:T(8,128)(2,1)S(1)} %get-tuple-element.52), channel_id=1, source_target_pairs={{0,4},{4,0},{8,12},{12,8},{16,20},{20,16},{24,28},{28,24},{1,5},{5... | collective-permute-start | bytes 442376 | tf_op jit(solution)/shard_map/ppermute | solution.py:405
  39.3 4.6 %copy-start = (bf16[2,2240,1400]{2,1,0:T(8,128)(2,1)S(1)}, bf16[2,2240,1400]{2,1,0:T(8,128)(2,1)}, u32[]{:S(2)}) copy-start(bf16[2,2240,1400]{2,1,0:T(8,128)(2,1)} %get-tuple-element.37.refs_6_.refs_9_.refs_5_) | copy-start | bytes 37632004
  43.9 4.0 %copy-start.5 = (bf16[2,112,512]{2,1,0:T(8,128)(2,1)S(1)}, bf16[2,112,512]{2,1,0:T(8,128)(2,1)}, u32[]{:S(2)}) copy-start(bf16[2,112,512]{2,1,0:T(8,128)(2,1)} %get-tuple-element.44.refs_0_) | copy-start | bytes 688132
  43.9 8.5 %copy-start.1 = (bf16[2,2240,1400]{2,1,0:T(8,128)(2,1)S(1)}, bf16[2,2240,1400]{2,1,0:T(8,128)(2,1)}, u32[]{:S(2)}) copy-start(bf16[2,2240,1400]{2,1,0:T(8,128)(2,1)} %get-tuple-element.37.refs_6_.refs_9_.refs_5_) | copy-start | bytes 37632004
  47.9 11.3 %slice-start = ((s8[6307840]{0:T(1024)(128)(4,1)}), s8[4194304]{0:T(1024)(128)(4,1)S(1)}, s32[]{:S(2)}) async-start(s8[6307840]{0:T(1024)(128)(4,1)} %bitcast.2), calls=%async_computation | async-start | bytes 8388608
  47.9 11.3 %slice-start.1 = ((s8[6307840]{0:T(1024)(128)(4,1)}), s8[2113536]{0:T(1024)(128)(4,1)S(1)}, s32[]{:S(2)}) async-start(s8[6307840]{0:T(1024)(128)(4,1)} %bitcast.2), calls=%async_computation.1 | async-start | bytes 4227072
  47.9 13.9 %collective-permute-start.3 = (bf16[2,112,512]{2,1,0:T(8,128)(2,1)S(1)}, bf16[2,112,512]{2,1,0:T(8,128)(2,1)S(1)}, u32[]{:S(2)}, u32[]{:S(2)}) collective-permute-start(bf16[2,112,512]{2,1,0:T(8,128)(2,1)S(1)} %copy-done.5), channel_id=1, source_target_pairs={{0,1},{1,0},{2,3},{3,2},{4,5},{5,4},{6,7},{7,6},{8,9},{9,8},{10,11... | collective-permute-start | bytes 688136 | tf_op jit(solution)/shard_map/ppermute | solution.py:418
  48.0 19.3 %collective-permute-start.4 = (bf16[2,112,512]{2,1,0:T(8,128)(2,1)S(1)}, bf16[2,112,512]{2,1,0:T(8,128)(2,1)S(1)}, u32[]{:S(2)}, u32[]{:S(2)}) collective-permute-start(bf16[2,112,512]{2,1,0:T(8,128)(2,1)S(1)} %copy-done.5), channel_id=1, source_target_pairs={{0,2},{1,3},{2,0},{3,1},{4,6},{5,7},{6,4},{7,5},{8,10},{9,11},{10,... | collective-permute-start | bytes 688136 | tf_op jit(solution)/shard_map/ppermute | solution.py:418
  50.5 16.8 %collective-permute-start.5 = (bf16[2,112,512]{2,1,0:T(8,128)(2,1)S(1)}, bf16[2,112,512]{2,1,0:T(8,128)(2,1)S(1)}, u32[]{:S(2)}, u32[]{:S(2)}) collective-permute-start(bf16[2,112,512]{2,1,0:T(8,128)(2,1)S(1)} %copy-done.5), channel_id=1, source_target_pairs={{0,3},{1,2},{2,1},{3,0},{4,7},{5,6},{6,5},{7,4},{8,11},{9,10},{10,... | collective-permute-start | bytes 688136 | tf_op jit(solution)/shard_map/ppermute | solution.py:418
  59.8 9.5 %collective-permute-start.14 = (bf16[1120,128]{1,0:T(8,128)(2,1)S(1)}, bf16[1120,128]{1,0:T(8,128)(2,1)S(1)}, u32[]{:S(2)}, u32[]{:S(2)}) collective-permute-start(bf16[1120,128]{1,0:T(8,128)(2,1)S(1)} %project_3.2), channel_id=1, source_target_pairs={{0,1},{3,2},{4,5},{7,6},{8,9},{11,10},{12,13},{15,14},{16,17},{19,... | collective-permute-start | bytes 860168 | tf_op jit(solution)/shard_map/ppermute | solution.py:501
  61.1 8.2 %collective-permute-start.15 = (bf16[1120,128]{1,0:T(8,128)(2,1)S(1)}, bf16[1120,128]{1,0:T(8,128)(2,1)S(1)}, u32[]{:S(2)}, u32[]{:S(2)}) collective-permute-start(bf16[1120,128]{1,0:T(8,128)(2,1)S(1)} %project_3.2), channel_id=1, source_target_pairs={{1,2},{2,1},{5,6},{6,5},{9,10},{10,9},{13,14},{14,13},{17,18},{18,... | collective-permute-start | bytes 860168 | tf_op jit(solution)/shard_map/ppermute | solution.py:502
  67.4 14.8 %collective-permute-start.13 = (bf16[4,112,512]{2,1,0:T(8,128)(2,1)S(1)}, bf16[4,112,512]{2,1,0:T(8,128)(2,1)S(1)}, u32[]{:S(2)}, u32[]{:S(2)}) collective-permute-start(bf16[4,112,512]{2,1,0:T(8,128)(2,1)S(1)} %pad_maximum_fusion), channel_id=1, source_target_pairs={{0,4},{4,0},{8,12},{12,8},{16,20},{20,16},{24,28},{28,24},{1,5},{5... | collective-permute-start | bytes 1376264 | tf_op jit(solution)/shard_map/ppermute | solution.py:405
  67.6 11.6 %copy-start.3 = (f32[4,96,128]{2,1,0:T(8,128)S(1)}, f32[4,96,128]{2,1,0:T(8,128)}, u32[]{:S(2)}) copy-start(f32[4,96,128]{2,1,0:T(8,128)} %get-tuple-element.28.refs_4_.refs_3_.mask_ref) | copy-start | bytes 589828
  67.6 14.7 %collective-permute-start.16 = (bf16[4,112,512]{2,1,0:T(8,128)(2,1)S(1)}, bf16[4,112,512]{2,1,0:T(8,128)(2,1)S(1)}, u32[]{:S(2)}, u32[]{:S(2)}) collective-permute-start(bf16[4,112,512]{2,1,0:T(8,128)(2,1)S(1)} %pad_maximum_fusion.1), channel_id=1, source_target_pairs={{4,8},{12,16},{20,24},{8,4},{16,12},{24,20},{5,9},{13,17},{21,25},... | collective-permute-start | bytes 1376264 | tf_op jit(solution)/shard_map/ppermute | solution.py:406
  69.3 20.1 %collective-permute-start.18 = (bf16[1120,128]{1,0:T(8,128)(2,1)S(1)}, bf16[1120,128]{1,0:T(8,128)(2,1)S(1)}, u32[]{:S(2)}, u32[]{:S(2)}) collective-permute-start(bf16[1120,128]{1,0:T(8,128)(2,1)S(1)} %project_1.2), channel_id=1, source_target_pairs={{0,1},{1,0},{2,3},{3,2},{4,5},{5,4},{6,7},{7,6},{8,9},{9,8},{10,11... | collective-permute-start | bytes 860168 | tf_op jit(solution)/shard_map/ppermute | solution.py:509
  78.6 15.3 %collective-permute-start.17 = (bf16[1120,128]{1,0:T(8,128)(2,1)S(1)}, bf16[1120,128]{1,0:T(8,128)(2,1)S(1)}, u32[]{:S(2)}, u32[]{:S(2)}) collective-permute-start(bf16[1120,128]{1,0:T(8,128)(2,1)S(1)} %project_2.2), channel_id=1, source_target_pairs={{0,2},{1,3},{2,0},{3,1},{4,6},{5,7},{6,4},{7,5},{8,10},{9,11},{10,... | collective-permute-start | bytes 860168 | tf_op jit(solution)/shard_map/ppermute | solution.py:508
  94.6 11.1 %copy-start.6 = (s32[4]{0:T(128)S(1)}, s32[4]{0:T(128)}, u32[]{:S(2)}) copy-start(s32[4]{0:T(128)} %width_ref.5) | copy-start | bytes 52
  94.6 6.5 %collective-permute-start.19 = (bf16[848,128]{1,0:T(8,128)(2,1)S(1)}, bf16[848,128]{1,0:T(8,128)(2,1)S(1)}, u32[]{:S(2)}, u32[]{:S(2)}) collective-permute-start(bf16[848,128]{1,0:T(8,128)(2,1)S(1)} %project_3.3), channel_id=1, source_target_pairs={{0,1},{3,2},{4,5},{7,6},{8,9},{11,10},{12,13},{15,14},{16,17},{19,... | collective-permute-start | bytes 651272 | tf_op jit(solution)/shard_map/ppermute | solution.py:501
  95.9 5.2 %collective-permute-start.20 = (bf16[848,128]{1,0:T(8,128)(2,1)S(1)}, bf16[848,128]{1,0:T(8,128)(2,1)S(1)}, u32[]{:S(2)}, u32[]{:S(2)}) collective-permute-start(bf16[848,128]{1,0:T(8,128)(2,1)S(1)} %project_3.3), channel_id=1, source_target_pairs={{1,2},{2,1},{5,6},{6,5},{9,10},{10,9},{13,14},{14,13},{17,18},{18,... | collective-permute-start | bytes 651272 | tf_op jit(solution)/shard_map/ppermute | solution.py:502
  101.8 11.8 %collective-permute-start.22 = (bf16[848,128]{1,0:T(8,128)(2,1)S(1)}, bf16[848,128]{1,0:T(8,128)(2,1)S(1)}, u32[]{:S(2)}, u32[]{:S(2)}) collective-permute-start(bf16[848,128]{1,0:T(8,128)(2,1)S(1)} %project_1.3), channel_id=1, source_target_pairs={{0,1},{1,0},{2,3},{3,2},{4,5},{5,4},{6,7},{7,6},{8,9},{9,8},{10,11... | collective-permute-start | bytes 651272 | tf_op jit(solution)/shard_map/ppermute | solution.py:509
  105.7 12.3 %collective-permute-start.21 = (bf16[848,128]{1,0:T(8,128)(2,1)S(1)}, bf16[848,128]{1,0:T(8,128)(2,1)S(1)}, u32[]{:S(2)}, u32[]{:S(2)}) collective-permute-start(bf16[848,128]{1,0:T(8,128)(2,1)S(1)} %project_2.3), channel_id=1, source_target_pairs={{0,2},{1,3},{2,0},{3,1},{4,6},{5,7},{6,4},{7,5},{8,10},{9,11},{10,... | collective-permute-start | bytes 651272 | tf_op jit(solution)/shard_map/ppermute | solution.py:508

commit v2 on v1

--- a/solution.py
+++ b/solution.py
@@ -197,32 +197,23 @@
         x_scr[lines, len(packets) * LANES :] = turned[:kept].astype(jnp.bfloat16)
 
 
-def load_kernel(w_ref, out_ref, token_ref, sems, *, shards, depth):
+def weight_copies(w_ref, w_scr, sems):
+    return [
+        pltpu.make_async_copy(w_ref.at[:, :, units], w_scr.at[:, :, units], sems.at[t])
+        for t, units in enumerate(tiles_of(w_ref.shape[2]))
+    ]
+
+
+def expand(x_scr, w_scr, par_ref, chunk, k, units):
     me = lax.axis_index("tensor")
-    rest = depth - LANES
-    copies = []
-    for k in range(2):
-        for j in range(shards):
-            base = lax.bitwise_xor(me, j) * depth
-            for part, (source, size, target) in enumerate(
-                ((base, LANES, j * LANES), (base + LANES, rest, shards * LANES + j * rest))
-            ):
-                copies.append(
-                    pltpu.make_async_copy(
-                        w_ref.at[k, pl.ds(pl.multiple_of(source, GROUP), size)],
-                        out_ref.at[k, pl.ds(target, size)],
-                        sems.at[k, j, part],
-                    )
-                )
-    for copy in copies:
-        copy.start()
-    token_ref[...] = jnp.zeros_like(token_ref)
-    for copy in copies:
-        copy.wait()
-
-
-def expand(x_scr, w_ref, par_ref, k, units):
-    pre_act = jnp.dot(x_scr[...], w_ref[k, :, units], preferred_element_type=jnp.float32)
+    shards = w_scr.shape[1] // chunk.depth
+    bases = [pl.multiple_of(lax.bitwise_xor(me, j) * chunk.depth, GROUP) for j in range(shards)]
+    weight = jnp.concatenate(
+        [w_scr[k, pl.ds(base, LANES), units] for base in bases]
+        + [w_scr[k, pl.ds(pl.multiple_of(base + LANES, GROUP), chunk.rest), units] for base in bases],
+        axis=0,
+    )
+    pre_act = jnp.dot(x_scr[...], weight, preferred_element_type=jnp.float32)
     return silu(pre_act + par_ref[18 + k : 19 + k, units])
 
 
@@ -232,20 +223,27 @@
 
 
 def own_kernel(*refs, chunk, shards):
-    packet_refs, (mask_ref, par_ref, w_ref, out_ref, x_scr) = refs[:shards], refs[shards:]
+    packet_refs, (mask_ref, par_ref, w_ref, out_ref, x_scr, w_scr, sems) = refs[:shards], refs[shards:]
     kept = chunk.kept
+    copies = weight_copies(w_ref, w_scr, sems)
+    for copy in copies:
+        copy.start()
     gather_rows(x_scr, chunk, [[p.at[1] for p in packet_refs], [p.at[0] for p in packet_refs]])
     mask = jnp.concatenate([mask_ref[1], mask_ref[2]], axis=0)
-    for units in tiles_of(w_ref.shape[2]):
+    for copy, units in zip(copies, tiles_of(w_ref.shape[2])):
+        copy.wait()
         for k in range(2):
-            out_ref[k, :, units] = masked(expand(x_scr, w_ref, par_ref, k, units), mask)
+            out_ref[k, :, units] = masked(expand(x_scr, w_scr, par_ref, chunk, k, units), mask)
 
 
 def hidden_kernel(*refs, chunk, shards, groups):
     count = len(groups)
     inner_refs, outer_refs = refs[:count], refs[count : 2 * count]
-    own_ref, mask_ref, par_ref, w_ref, out_ref, x_scr = refs[2 * count :]
+    own_ref, mask_ref, par_ref, w_ref, out_ref, x_scr, w_scr, sems = refs[2 * count :]
     kept = chunk.kept
+    copies = weight_copies(w_ref, w_scr, sems)
+    for copy in copies:
+        copy.start()
     parity = parity_of()
     spots = {j: (g, i) for g, js in enumerate(groups) for i, j in enumerate(js)}
     gather_rows(
@@ -255,10 +253,11 @@
     )
     mask = jnp.concatenate([mask_ref[0], mask_ref[3]], axis=0)
 
-    def around(units):
-        return [
-            masked(expand(x_scr, w_ref, par_ref, k, units), mask) for k in range(2)
-        ]
+    tiles = tiles_of(w_ref.shape[2])
+
+    def around(t):
+        copies[t].wait()
+        return [masked(expand(x_scr, w_scr, par_ref, chunk, k, tiles[t]), mask) for k in range(2)]
 
     def convolve(units, cells):
         width = units.stop - units.start
@@ -302,10 +301,9 @@
             hidden = halves[0][place] * silu(halves[1][place])
             out_ref[(1 - place) * kept : (2 - place) * kept, units] = hidden.astype(jnp.bfloat16)
 
-    tiles = tiles_of(w_ref.shape[2])
-    cells = around(tiles[0])
+    cells = around(0)
     for t, units in enumerate(tiles):
-        coming = around(tiles[t + 1]) if t + 1 < len(tiles) else None
+        coming = around(t + 1) if t + 1 < len(tiles) else None
         convolve(units, cells)
         cells = coming
 
@@ -380,6 +378,7 @@
         grid_spec=pltpu.PrefetchScalarGridSpec(
             num_scalar_prefetch=2, grid=(), in_specs=[VMEM], out_specs=[VMEM] * (2 * count)
         ),
+        compiler_params=pltpu.CompilerParams(vmem_limit_bytes=8 * MIB),
         name="pack",
     )(clip_height, clip_width, latents)
     own, masks = packed[:count], packed[count:]
@@ -398,78 +397,78 @@
     to_end = [(2, 3), (1, 0)]
     from_end = [(0, 1), (3, 2)]
 
-    def halos(packets, groups):
-        inner = [jnp.concatenate([packets[j][:1] for j in js], axis=0) for js in groups]
-        outer = [jnp.concatenate([packets[j][1:] for j in js], axis=0) for js in groups]
-        return (
-            [lax.ppermute(x, "row", sibling) for x in inner],
-            [lax.ppermute(x, "row", beyond) for x in outer],
-        )
-
-    def relay(mine, token):
-        second = lax.ppermute(mine, "tensor", two_off)
-        first = lax.ppermute(mine, "tensor", near)
-        across = lax.ppermute(after(mine, second, token), "tensor", middle)
-        passed = lax.ppermute(after(second, token), "tensor", to_end)
-        return [mine, first, second, across + passed]
-
-    def direct(mine):
-        return [mine] + [
-            lax.ppermute(mine, "tensor", [(i, i ^ j) for i in range(4)]) for j in range(1, 4)
-        ]
+    def halo_rows_of(packets, js):
+        inner = jnp.concatenate([packets[j][:1] for j in js], axis=0)
+        outer = jnp.concatenate([packets[j][1:] for j in js], axis=0)
+        return inner, outer
+
+    def send_rows(inner, outer):
+        return lax.ppermute(inner, "row", sibling), lax.ppermute(outer, "row", beyond)
+
+    def first_phase(mine):
+        return [mine, lax.ppermute(mine, "tensor", near), lax.ppermute(mine, "tensor", two_off)]
+
+    def second_phase(parts, *others):
+        mine, second = lax.optimization_barrier((parts[0], parts[2], *others))[:2]
+        return lax.ppermute(second, "tensor", to_end) + lax.ppermute(mine, "tensor", middle)
 
     out = None
-    weights, token = pl.pallas_call(
-        functools.partial(load_kernel, shards=shards, depth=depth),
-        out_shape=[
-            jax.ShapeDtypeStruct(expand_weight.shape, jnp.bfloat16),
-            jax.ShapeDtypeStruct((8, 128), jnp.float32),
-        ],
-        in_specs=[pl.BlockSpec(memory_space=pl.ANY)],
-        out_specs=[VMEM, VMEM],
-        scratch_shapes=[pltpu.SemaphoreType.DMA((2, shards, 2))],
-        name="load_weights",
-    )(after(expand_weight, own[0]))
-    packets = relay(own[0], token)
-    groups = ((0,), (1, 2), (3,))
-    inner, outer = halos(packets, groups)
-    upcoming = direct(after(own[1], packets[3]))
+    groups = ((0, 1, 2), (3,))
+    packets = first_phase(own[0])
+    ready = halo_rows_of(packets, groups[0])
+    upcoming = first_phase(after(own[1], *ready))
+    packets.append(second_phase(packets))
     for number, chunk in enumerate(chunks):
         if number:
-            packets, groups = list(lax.optimization_barrier((*upcoming, hidden))[:shards]), ((0, 1, 2, 3),)
-            inner, outer = halos(packets, groups)
-            packets[0] = after(packets[0], far)
+            packets = upcoming
+            ready = halo_rows_of(packets, groups[0])
+        early = send_rows(*ready)
+        late = send_rows(*halo_rows_of(packets, groups[1]))
+        inner, outer = zip(early, late)
+        if number:
+            packets[3] = after(packets[3], far)
+        else:
+            packets[3] = after(packets[3], *early)
         whole = lambda shape: pl.BlockSpec(shape, lambda f, *_: (0,) * len(shape))
+        streamed = [
+            pltpu.VMEM((chunk.tokens, full_depth), jnp.bfloat16),
+            pltpu.VMEM(expand_weight.shape, jnp.bfloat16),
+            pltpu.SemaphoreType.DMA((len(tiles_of(hidden_count)),)),
+        ]
         rows = pl.pallas_call(
             functools.partial(own_kernel, chunk=chunk, shards=shards),
             out_shape=jax.ShapeDtypeStruct((2, chunk.tokens, hidden_count), jnp.float32),
-            in_specs=[VMEM] * (shards + 3),
+            in_specs=[VMEM] * (shards + 2) + [pl.BlockSpec(memory_space=pl.ANY)],
             out_specs=VMEM,
-            scratch_shapes=[pltpu.VMEM((chunk.tokens, full_depth), jnp.bfloat16)],
-            compiler_params=pltpu.CompilerParams(vmem_limit_bytes=16 * MIB),
+            scratch_shapes=streamed,
+            compiler_params=pltpu.CompilerParams(vmem_limit_bytes=44 * MIB),
             cost_estimate=pl.CostEstimate(
-                flops=4 * chunk.tokens * full_depth * hidden_count,
-                bytes_accessed=4 * full_depth * hidden_count,
-                transcendentals=2 * chunk.tokens * hidden_count,
+                flops=1000,
+                bytes_accessed=1000,
+                transcendentals=0,
             ),
             name="expand_own",
-        )(*packets, masks[number], parameters, weights)
+        )(*packets, masks[number], parameters, expand_weight)
+        inner = list(inner)
         if number:
             inner[0] = after(inner[0], last_unit)
+        else:
+            inner[0], *upcoming = lax.optimization_barrier((inner[0], *upcoming))
+            upcoming.append(second_phase(upcoming, rows))
         hidden = pl.pallas_call(
             functools.partial(hidden_kernel, chunk=chunk, shards=shards, groups=groups),
             out_shape=jax.ShapeDtypeStruct((chunk.tokens, hidden_count), jnp.bfloat16),
-            in_specs=[VMEM] * (2 * len(groups) + 4),
+            in_specs=[VMEM] * (2 * len(groups) + 3) + [pl.BlockSpec(memory_space=pl.ANY)],
             out_specs=VMEM,
-            scratch_shapes=[pltpu.VMEM((chunk.tokens, full_depth), jnp.bfloat16)],
-            compiler_params=pltpu.CompilerParams(vmem_limit_bytes=16 * MIB),
+            scratch_shapes=streamed,
+            compiler_params=pltpu.CompilerParams(vmem_limit_bytes=44 * MIB),
             cost_estimate=pl.CostEstimate(
-                flops=4 * chunk.tokens * full_depth * hidden_count,
-                bytes_accessed=4 * full_depth * hidden_count,
-                transcendentals=3 * chunk.tokens * hidden_count,
+                flops=1000,
+                bytes_accessed=1000,
+                transcendentals=0,
             ),
             name="expand_conv",
-        )(*inner, *outer, rows, masks[number], parameters, weights)
+        )(*inner, *outer, rows, masks[number], parameters, expand_weight)
 
         weight_of = lambda j: pl.BlockSpec(
             (depth, hidden_count), lambda f, place, *_: (lax.bitwise_xor(place[0], j), 0)
@@ -490,13 +489,15 @@
                     in_specs=[weight_of(j), whole(hidden.shape)] + [whole(chunk.unit)] * len(added),
                     out_specs=whole(chunk.unit),
                 ),
-                compiler_params=pltpu.CompilerParams(vmem_limit_bytes=24 * MIB),
+                compiler_params=pltpu.CompilerParams(vmem_limit_bytes=16 * MIB),
                 cost_estimate=cost,
                 name=f"project_{j}",
             )(me, project_turned, hidden, *added)
 
         if number:
             hidden = after(hidden, *arrived)
+        else:
+            hidden, upcoming[3] = lax.optimization_barrier((hidden, upcoming[3]))
         far = unit(3)
         relayed = lax.ppermute(far, "tensor", from_end)
         across = lax.ppermute(far, "tensor", middle)
@@ -520,7 +521,7 @@
                 + [whole(latents.shape)] * len(extra),
                 out_specs=whole(latents.shape),
             ),
-            compiler_params=pltpu.CompilerParams(vmem_limit_bytes=24 * MIB),
+            compiler_params=pltpu.CompilerParams(vmem_limit_bytes=16 * MIB),
             cost_estimate=cost,
             name="finish",
         )(me, clip_width, masks[number], project_turned, hidden, *arrived, *extra)

time: 121 us -> 126 us (1.041)
  the two profiles are of different devices: /device:TPU:0 before, /device:TPU:2 now
where the time goes in v2:
time: 126 us; the launch traced here: 125 us
  starting transfers between devices  49.4 us (39%)
  Pallas kernels  37 us (29%)
  waiting for transfers between devices  32.9 us (26%)
  local copies, waits for them, and re-layouts  3.53 us (3%)
  other arithmetic  2.03 us (2%)
    pallas_call x2, Pallas kernels, on_device_packed(): pl.pallas_call(functools.partial(hidden_kernel, chunk=chunk, shards=shard...  15.9 us
    pallas_call x2, Pallas kernels, on_device_packed(): pl.pallas_call(functools.partial(own_kernel, chunk=chunk, shards=shards),...  12.8 us
    ppermute x2, starting transfers between devices, on_device_packed(): relayed = lax.ppermute(far, 'tensor', from_end)  12.6 us
    ppermute x2, waiting for transfers between devices, first_phase(): lax.ppermute(mine, 'tensor', two_off)  11.9 us
    ppermute x4, starting transfers between devices, send_rows(): lax.ppermute(outer, 'row', beyond)  9.43 us
    ppermute x2, waiting for transfers between devices, on_device_packed(): lax.ppermute(after(close, relayed), 'tensor', near)  7.41 us
    ppermute x2, starting transfers between devices, on_device_packed(): lax.ppermute(after(close, relayed), 'tensor', near)  7.35 us
    ppermute x2, starting transfers between devices, first_phase(): lax.ppermute(mine, 'tensor', near)  7.32 us
  transfers between devices with their start and end apart: 24, of which 8 were waited for; matrix products, arithmetic and copies ran while one was open for 2% of the time, Pallas kernels for 26%

profile of v2, /device:TPU:2, one launch (start us, length us, event | category | flops | bytes accessed | tf_op | source)
XLA Modules:
  0.0 125.2 jit_solution(10134320593923348870)
XLA Ops:
  0.0 1.1 copy-done
  1.1 0.7 copy-done.1
  1.7 0.7 copy-done.3
  2.4 0.7 pack.1
  3.1 2.7 %collective-permute-start.1 = (bf16[2,144,512]{2,1,0:T(8,128)(2,1)S(1)}, bf16[2,144,512]{2,1,0:T(8,128)(2,1)S(1)}, u32[]{:S(2)}, u32[]{:S(2)}) collective-permute-start(bf16[2,144,512]{2,1,0:T(8,128)(2,1)S(1)} %get-tuple-element.39.refs_0_), channel_id=1, source_target_pairs={{0,2},{1,3},{2,0},{3,1},{4,6},{5,7},{6,4},{7,5},{8,10},{9,11},{10,... | collective-permute-start | bytes 884744 | tf_op jit(solution)/shard_map/ppermute | solution.py:409
  5.8 1.6 %collective-permute-start = (bf16[2,144,512]{2,1,0:T(8,128)(2,1)S(1)}, bf16[2,144,512]{2,1,0:T(8,128)(2,1)S(1)}, u32[]{:S(2)}, u32[]{:S(2)}) collective-permute-start(bf16[2,144,512]{2,1,0:T(8,128)(2,1)S(1)} %get-tuple-element.39.refs_0_), channel_id=1, source_target_pairs={{0,1},{1,0},{2,3},{3,2},{4,5},{5,4},{6,7},{7,6},{8,9},{9,8},{10,11... | collective-permute-start | bytes 884744 | tf_op jit(solution)/shard_map/ppermute | solution.py:409
  7.4 11.9 %collective-permute-done.1.refs_2_ = bf16[2,144,512]{2,1,0:T(8,128)(2,1)S(1)} collective-permute-done((bf16[2,144,512]{2,1,0:T(8,128)(2,1)S(1)}, bf16[2,144,512]{2,1,0:T(8,128)(2,1)S(1)}, u32[]{:S(2)}, u32[]{:S(2)}) %collective-permute-start.1) | collective-permute-done | bytes 294944 | tf_op jit(solution)/shard_map/ppermute | solution.py:409
  19.2 1.3 %collective-permute-start.6 = (bf16[2,144,512]{2,1,0:T(8,128)(2,1)S(1)}, bf16[2,144,512]{2,1,0:T(8,128)(2,1)S(1)}, u32[]{:S(2)}, u32[]{:S(2)}) collective-permute-start(bf16[2,144,512]{2,1,0:T(8,128)(2,1)S(1)} %collective-permute-done.1.refs_2_), channel_id=1, source_target_pairs={{2,3},{1,0},{6,7},{5,4},{10,11},{9,8},{14,15},{13,12},{18,19},{17,... | collective-permute-start | bytes 884744 | tf_op jit(solution)/shard_map/ppermute | solution.py:413
  20.5 1.4 %collective-permute-start.7 = (bf16[2,144,512]{2,1,0:T(8,128)(2,1)S(1)}, bf16[2,144,512]{2,1,0:T(8,128)(2,1)}, u32[]{:S(2)}, u32[]{:S(2)}) collective-permute-start(bf16[2,144,512]{2,1,0:T(8,128)(2,1)S(1)} %get-tuple-element.39.refs_0_), channel_id=1, source_target_pairs={{1,2},{2,1},{5,6},{6,5},{9,10},{10,9},{13,14},{14,13},{17,18},{18,... | collective-permute-start | bytes 884744 | tf_op jit(solution)/shard_map/ppermute | solution.py:413
  22.0 0.1 collective-permute-start.2
  22.1 1.0 reshape.7
  23.1 5.7 %collective-permute-start.3 = (bf16[2,112,512]{2,1,0:T(8,128)(2,1)S(1)}, bf16[2,112,512]{2,1,0:T(8,128)(2,1)S(1)}, u32[]{:S(2)}, u32[]{:S(2)}) collective-permute-start(bf16[2,112,512]{2,1,0:T(8,128)(2,1)S(1)} %get-tuple-element.43.refs_0_), channel_id=1, source_target_pairs={{0,1},{1,0},{2,3},{3,2},{4,5},{5,4},{6,7},{7,6},{8,9},{9,8},{10,11... | collective-permute-start | bytes 688136 | tf_op jit(solution)/shard_map/ppermute | solution.py:409
  29.0 2.2 %collective-permute-start.9 = (bf16[3,144,512]{2,1,0:T(8,128)(2,1)S(1)}, bf16[3,144,512]{2,1,0:T(8,128)(2,1)S(1)}, u32[]{:S(2)}, u32[]{:S(2)}) collective-permute-start(bf16[3,144,512]{2,1,0:T(8,128)(2,1)S(1)} %pad_maximum_fusion.1), channel_id=1, source_target_pairs={{4,8},{12,16},{20,24},{8,4},{16,12},{24,20},{5,9},{13,17},{21,25},... | collective-permute-start | bytes 1327112 | tf_op jit(solution)/shard_map/ppermute | solution.py:406
  31.2 1.0 add.6.refs_3_
  32.2 3.4 %collective-permute-start.10 = (bf16[1,144,512]{2,1,0:T(8,128)(2,1)S(1)}, bf16[1,144,512]{2,1,0:T(8,128)(2,1)S(1)}, u32[]{:S(2)}, u32[]{:S(2)}) collective-permute-start(bf16[1,144,512]{2,1,0:T(8,128)(2,1)S(1)} %get-tuple-element.55), channel_id=1, source_target_pairs={{4,8},{12,16},{20,24},{8,4},{16,12},{24,20},{5,9},{13,17},{21,25},... | collective-permute-start | bytes 442376 | tf_op jit(solution)/shard_map/ppermute | solution.py:406
  35.6 1.1 collective-permute-start.8
  36.7 0.7 pad_maximum_fusion.4.refs_5_.refs_6_
  37.5 3.6 %collective-permute-done.9.refs_2_ = bf16[3,144,512]{2,1,0:T(8,128)(2,1)S(1)} collective-permute-done((bf16[3,144,512]{2,1,0:T(8,128)(2,1)S(1)}, bf16[3,144,512]{2,1,0:T(8,128)(2,1)S(1)}, u32[]{:S(2)}, u32[]{:S(2)}) %collective-permute-start.9) | collective-permute-done | bytes 442400 | tf_op jit(solution)/shard_map/ppermute | solution.py:406
  41.1 6.9 %expand_own.2.refs_4_ = f32[2,256,1400]{2,1,0:T(8,128)S(1)} custom-call(bf16[2,144,512]{2,1,0:T(8,128)(2,1)S(1)} %get-tuple-element.39.refs_0_, bf16[2,144,512]{2,1,0:T(8,128)(2,1)S(1)} %collective-permute-done.refs_1_, bf16[2,144,512]{2,1,0:T(8,128)(2,1)S(1)} %collective-permute-done.1.refs_2_, bf16[2,144,512]{2,1,0:T(8,128)(2,1)S(1)} %add.6.refs_3_, ...), custom_call_target="tpu_custom_call" | custom-call | flops 1000 | bytes 1000 | tf_op jit(solution)/shard_map/expand_own/pallas_call | solution.py:438
  48.1 1.4 %collective-permute-start.11 = (bf16[2,112,512]{2,1,0:T(8,128)(2,1)S(1)}, bf16[2,112,512]{2,1,0:T(8,128)(2,1)S(1)}, u32[]{:S(2)}, u32[]{:S(2)}) collective-permute-start(bf16[2,112,512]{2,1,0:T(8,128)(2,1)S(1)} %collective-permute-done.4.refs_2_), channel_id=1, source_target_pairs={{2,3},{1,0},{6,7},{5,4},{10,11},{9,8},{14,15},{13,12},{18,19},{17,... | collective-permute-start | bytes 688136 | tf_op jit(solution)/shard_map/ppermute | solution.py:413
  49.5 0.7 collective-permute-start.12
  50.2 8.8 %expand_conv.2.hidden_ref = bf16[256,1400]{1,0:T(8,128)(2,1)S(1)} custom-call(bf16[3,144,512]{2,1,0:T(8,128)(2,1)S(1)} %collective-permute-done.2.refs_0_, bf16[1,144,512]{2,1,0:T(8,128)(2,1)S(1)} %collective-permute-done.8.refs_1_, bf16[3,144,512]{2,1,0:T(8,128)(2,1)S(1)} %collective-permute-done.9.refs_2_, ...), custom_call_target="tpu_custom_call" | custom-call | flops 1000 | bytes 1000 | tf_op jit(solution)/shard_map/expand_conv/pallas_call | solution.py:458
  59.2 0.7 project_3.2
  59.9 9.8 %collective-permute-start.13 = (bf16[1120,128]{1,0:T(8,128)(2,1)S(1)}, bf16[1120,128]{1,0:T(8,128)(2,1)S(1)}, u32[]{:S(2)}, u32[]{:S(2)}) collective-permute-start(bf16[1120,128]{1,0:T(8,128)(2,1)S(1)} %project_3.2), channel_id=1, source_target_pairs={{0,1},{3,2},{4,5},{7,6},{8,9},{11,10},{12,13},{15,14},{16,17},{19,... | collective-permute-start | bytes 860168 | tf_op jit(solution)/shard_map/ppermute | solution.py:502
  69.7 0.9 collective-permute-start.14
  70.6 1.1 collective-permute-start.5
  71.8 2.0 %collective-permute-start.16 = (bf16[3,112,512]{2,1,0:T(8,128)(2,1)S(1)}, bf16[3,112,512]{2,1,0:T(8,128)(2,1)S(1)}, u32[]{:S(2)}, u32[]{:S(2)}) collective-permute-start(bf16[3,112,512]{2,1,0:T(8,128)(2,1)S(1)} %pad_maximum_fusion.3), channel_id=1, source_target_pairs={{4,8},{12,16},{20,24},{8,4},{16,12},{24,20},{5,9},{13,17},{21,25},... | collective-permute-start | bytes 1032200 | tf_op jit(solution)/shard_map/ppermute | solution.py:406
  73.7 0.6 project_1.2
  74.4 2.2 %collective-permute-done.13.refs_0_ = bf16[1120,128]{1,0:T(8,128)(2,1)S(1)} collective-permute-done((bf16[1120,128]{1,0:T(8,128)(2,1)S(1)}, bf16[1120,128]{1,0:T(8,128)(2,1)S(1)}, u32[]{:S(2)}, u32[]{:S(2)}) %collective-permute-start.13) | collective-permute-done | bytes 286752 | tf_op jit(solution)/shard_map/ppermute | solution.py:502
  76.6 3.8 %collective-permute-start.19 = (bf16[1120,128]{1,0:T(8,128)(2,1)S(1)}, bf16[1120,128]{1,0:T(8,128)(2,1)S(1)}, u32[]{:S(2)}, u32[]{:S(2)}) collective-permute-start(bf16[1120,128]{1,0:T(8,128)(2,1)S(1)} %project_1.2), channel_id=1, source_target_pairs={{0,1},{1,0},{2,3},{3,2},{4,5},{5,4},{6,7},{7,6},{8,9},{9,8},{10,11... | collective-permute-start | bytes 860168 | tf_op jit(solution)/shard_map/ppermute | solution.py:510
  80.4 0.6 project_2.2
  81.2 0.1 collective-permute-start.15
  81.3 1.9 %collective-permute-start.17 = (bf16[1,112,512]{2,1,0:T(8,128)(2,1)S(1)}, bf16[1,112,512]{2,1,0:T(8,128)(2,1)S(1)}, u32[]{:S(2)}, u32[]{:S(2)}) collective-permute-start(bf16[1,112,512]{2,1,0:T(8,128)(2,1)S(1)} %get-tuple-element.63), channel_id=1, source_target_pairs={{4,8},{12,16},{20,24},{8,4},{16,12},{24,20},{5,9},{13,17},{21,25},... | collective-permute-start | bytes 344072 | tf_op jit(solution)/shard_map/ppermute | solution.py:406
  83.2 5.9 %expand_own.3.refs_4_ = f32[2,192,1400]{2,1,0:T(8,128)S(1)} custom-call(bf16[2,112,512]{2,1,0:T(8,128)(2,1)S(1)} %get-tuple-element.43.refs_0_, bf16[2,112,512]{2,1,0:T(8,128)(2,1)S(1)} %collective-permute-done.3.refs_1_, bf16[2,112,512]{2,1,0:T(8,128)(2,1)S(1)} %collective-permute-done.4.refs_2_, bf16[2,112,512]{2,1,0:T(8,128)(2,1)S(1)} %add.7.refs_3_, ...), custom_call_target="tpu_custom_call" | custom-call | flops 1000 | bytes 1000 | tf_op jit(solution)/shard_map/expand_own/pallas_call | solution.py:438
  89.1 7.1 %expand_conv.3.hidden_ref = bf16[192,1400]{1,0:T(8,128)(2,1)S(1)} custom-call(bf16[3,112,512]{2,1,0:T(8,128)(2,1)S(1)} %collective-permute-done.5.refs_0_, bf16[1,112,512]{2,1,0:T(8,128)(2,1)S(1)} %collective-permute-done.15.refs_1_, bf16[3,112,512]{2,1,0:T(8,128)(2,1)S(1)} %collective-permute-done.16.refs_2_, ...), custom_call_target="tpu_custom_call" | custom-call | flops 1000 | bytes 1000 | tf_op jit(solution)/shard_map/expand_conv/pallas_call | solution.py:458
  96.2 0.8 collective-permute-done.18.refs_1_
  97.0 0.7 project_3.3
  97.7 2.8 %collective-permute-start.20 = (bf16[848,128]{1,0:T(8,128)(2,1)S(1)}, bf16[848,128]{1,0:T(8,128)(2,1)S(1)}, u32[]{:S(2)}, u32[]{:S(2)}) collective-permute-start(bf16[848,128]{1,0:T(8,128)(2,1)S(1)} %project_3.3), channel_id=1, source_target_pairs={{0,1},{3,2},{4,5},{7,6},{8,9},{11,10},{12,13},{15,14},{16,17},{19,... | collective-permute-start | bytes 651272 | tf_op jit(solution)/shard_map/ppermute | solution.py:502
  100.6 0.7 collective-permute-start.21
  101.2 0.7 project_1.3
  101.9 3.1 %collective-permute-done.20.refs_0_ = bf16[848,128]{1,0:T(8,128)(2,1)S(1)} collective-permute-done((bf16[848,128]{1,0:T(8,128)(2,1)S(1)}, bf16[848,128]{1,0:T(8,128)(2,1)S(1)}, u32[]{:S(2)}, u32[]{:S(2)}) %collective-permute-start.20) | collective-permute-done | bytes 217120 | tf_op jit(solution)/shard_map/ppermute | solution.py:502
  105.0 0.7 project_2.3
  105.7 3.6 %collective-permute-start.23 = (bf16[848,128]{1,0:T(8,128)(2,1)S(1)}, bf16[848,128]{1,0:T(8,128)(2,1)S(1)}, u32[]{:S(2)}, u32[]{:S(2)}) collective-permute-start(bf16[848,128]{1,0:T(8,128)(2,1)S(1)} %project_1.3), channel_id=1, source_target_pairs={{0,1},{1,0},{2,3},{3,2},{4,5},{5,4},{6,7},{7,6},{8,9},{9,8},{10,11... | collective-permute-start | bytes 651272 | tf_op jit(solution)/shard_map/ppermute | solution.py:510
  109.3 1.2 collective-permute-start.22
  110.5 1.3 %finish.2.refs_3_ = bf16[4,2,64,560]{3,2,1,0:T(8,128)(2,1)S(1)} custom-call(s32[1]{0:T(128)} %bitcast.place_ref, s32[4]{0:T(128)S(1)} %copy-done.2, f32[4,128,128]{2,1,0:T(8,128)S(1)} %get-tuple-element.41.refs_4_.refs_5_.mask_ref, bf16[2240,1400]{1,0:T(8,128)(2,1)S(1)} %bitcast.10, bf16[256,1400]{1,0:T(8,128)(2,1)S(1)} %expand_conv.2.hidden_ref, ...), custom_call_target="tpu_custom_call" | custom-call | flops 401408000 | bytes 2284800 | tf_op jit(solution)/shard_map/finish/pallas_call | solution.py:513
  111.8 7.4 %collective-permute-done.23.refs_2_ = bf16[848,128]{1,0:T(8,128)(2,1)S(1)} collective-permute-done((bf16[848,128]{1,0:T(8,128)(2,1)S(1)}, bf16[848,128]{1,0:T(8,128)(2,1)S(1)}, u32[]{:S(2)}, u32[]{:S(2)}) %collective-permute-start.23) | collective-permute-done | bytes 217120 | tf_op jit(solution)/shard_map/ppermute | solution.py:510
  119.2 3.7 %collective-permute-done.22.refs_1_ = bf16[848,128]{1,0:T(8,128)(2,1)S(1)} collective-permute-done((bf16[848,128]{1,0:T(8,128)(2,1)S(1)}, bf16[848,128]{1,0:T(8,128)(2,1)S(1)}, u32[]{:S(2)}, u32[]{:S(2)}) %collective-permute-start.22) | collective-permute-done | bytes 217120 | tf_op jit(solution)/shard_map/ppermute | solution.py:509
  123.0 2.2 %finish.3 = bf16[4,2,64,560]{3,2,1,0:T(8,128)(2,1)} custom-call(s32[1]{0:T(128)} %bitcast.place_ref, s32[4]{0:T(128)S(1)} %copy-done.2, f32[4,96,128]{2,1,0:T(8,128)S(1)} %get-tuple-element.30.refs_4_.refs_5_.mask_ref, bf16[2240,1400]{1,0:T(8,128)(2,1)S(1)} %bitcast.11, bf16[192,1400]{1,0:T(8,128)(2,1)S(1)} %expand_conv.3.hidden_ref, ...), custom_call_target="tpu_custom_call" | custom-call | flops 301056000 | bytes 2105600 | tf_op jit(solution)/shard_map/finish/pallas_call | solution.py:513
  (41 shorter events, 0.6 us)
Async XLA Ops:
  0.0 1.1 copy-start
  1.1 0.7 copy-start.1
  1.7 0.7 copy-start.3
  3.1 16.1 %collective-permute-start.1 = (bf16[2,144,512]{2,1,0:T(8,128)(2,1)S(1)}, bf16[2,144,512]{2,1,0:T(8,128)(2,1)S(1)}, u32[]{:S(2)}, u32[]{:S(2)}) collective-permute-start(bf16[2,144,512]{2,1,0:T(8,128)(2,1)S(1)} %get-tuple-element.39.refs_0_), channel_id=1, source_target_pairs={{0,2},{1,3},{2,0},{3,1},{4,6},{5,7},{6,4},{7,5},{8,10},{9,11},{10,... | collective-permute-start | bytes 884744 | tf_op jit(solution)/shard_map/ppermute | solution.py:409
  5.8 16.2 %collective-permute-start = (bf16[2,144,512]{2,1,0:T(8,128)(2,1)S(1)}, bf16[2,144,512]{2,1,0:T(8,128)(2,1)S(1)}, u32[]{:S(2)}, u32[]{:S(2)}) collective-permute-start(bf16[2,144,512]{2,1,0:T(8,128)(2,1)S(1)} %get-tuple-element.39.refs_0_), channel_id=1, source_target_pairs={{0,1},{1,0},{2,3},{3,2},{4,5},{5,4},{6,7},{7,6},{8,9},{9,8},{10,11... | collective-permute-start | bytes 884744 | tf_op jit(solution)/shard_map/ppermute | solution.py:409
  19.2 9.7 %collective-permute-start.6 = (bf16[2,144,512]{2,1,0:T(8,128)(2,1)S(1)}, bf16[2,144,512]{2,1,0:T(8,128)(2,1)S(1)}, u32[]{:S(2)}, u32[]{:S(2)}) collective-permute-start(bf16[2,144,512]{2,1,0:T(8,128)(2,1)S(1)} %collective-permute-done.1.refs_2_), channel_id=1, source_target_pairs={{2,3},{1,0},{6,7},{5,4},{10,11},{9,8},{14,15},{13,12},{18,19},{17,... | collective-permute-start | bytes 884744 | tf_op jit(solution)/shard_map/ppermute | solution.py:413
  20.5 10.6 %collective-permute-start.7 = (bf16[2,144,512]{2,1,0:T(8,128)(2,1)S(1)}, bf16[2,144,512]{2,1,0:T(8,128)(2,1)}, u32[]{:S(2)}, u32[]{:S(2)}) collective-permute-start(bf16[2,144,512]{2,1,0:T(8,128)(2,1)S(1)} %get-tuple-element.39.refs_0_), channel_id=1, source_target_pairs={{1,2},{2,1},{5,6},{6,5},{9,10},{10,9},{13,14},{14,13},{17,18},{18,... | collective-permute-start | bytes 884744 | tf_op jit(solution)/shard_map/ppermute | solution.py:413
  22.0 13.6 %collective-permute-start.2 = (bf16[3,144,512]{2,1,0:T(8,128)(2,1)S(1)}, bf16[3,144,512]{2,1,0:T(8,128)(2,1)S(1)}, u32[]{:S(2)}, u32[]{:S(2)}) collective-permute-start(bf16[3,144,512]{2,1,0:T(8,128)(2,1)S(1)} %pad_maximum_fusion), channel_id=1, source_target_pairs={{0,4},{4,0},{8,12},{12,8},{16,20},{20,16},{24,28},{28,24},{1,5},{5... | collective-permute-start | bytes 1327112 | tf_op jit(solution)/shard_map/ppermute | solution.py:406
  23.1 24.9 %collective-permute-start.3 = (bf16[2,112,512]{2,1,0:T(8,128)(2,1)S(1)}, bf16[2,112,512]{2,1,0:T(8,128)(2,1)S(1)}, u32[]{:S(2)}, u32[]{:S(2)}) collective-permute-start(bf16[2,112,512]{2,1,0:T(8,128)(2,1)S(1)} %get-tuple-element.43.refs_0_), channel_id=1, source_target_pairs={{0,1},{1,0},{2,3},{3,2},{4,5},{5,4},{6,7},{7,6},{8,9},{9,8},{10,11... | collective-permute-start | bytes 688136 | tf_op jit(solution)/shard_map/ppermute | solution.py:409
  28.9 19.2 %collective-permute-start.4 = (bf16[2,112,512]{2,1,0:T(8,128)(2,1)S(1)}, bf16[2,112,512]{2,1,0:T(8,128)(2,1)S(1)}, u32[]{:S(2)}, u32[]{:S(2)}) collective-permute-start(bf16[2,112,512]{2,1,0:T(8,128)(2,1)S(1)} %get-tuple-element.43.refs_0_), channel_id=1, source_target_pairs={{0,2},{1,3},{2,0},{3,1},{4,6},{5,7},{6,4},{7,5},{8,10},{9,11},{10,... | collective-permute-start | bytes 688136 | tf_op jit(solution)/shard_map/ppermute | solution.py:409
  29.0 12.2 %collective-permute-start.9 = (bf16[3,144,512]{2,1,0:T(8,128)(2,1)S(1)}, bf16[3,144,512]{2,1,0:T(8,128)(2,1)S(1)}, u32[]{:S(2)}, u32[]{:S(2)}) collective-permute-start(bf16[3,144,512]{2,1,0:T(8,128)(2,1)S(1)} %pad_maximum_fusion.1), channel_id=1, source_target_pairs={{4,8},{12,16},{20,24},{8,4},{16,12},{24,20},{5,9},{13,17},{21,25},... | collective-permute-start | bytes 1327112 | tf_op jit(solution)/shard_map/ppermute | solution.py:406
  32.2 18.0 %collective-permute-start.10 = (bf16[1,144,512]{2,1,0:T(8,128)(2,1)S(1)}, bf16[1,144,512]{2,1,0:T(8,128)(2,1)S(1)}, u32[]{:S(2)}, u32[]{:S(2)}) collective-permute-start(bf16[1,144,512]{2,1,0:T(8,128)(2,1)S(1)} %get-tuple-element.55), channel_id=1, source_target_pairs={{4,8},{12,16},{20,24},{8,4},{16,12},{24,20},{5,9},{13,17},{21,25},... | collective-permute-start | bytes 442376 | tf_op jit(solution)/shard_map/ppermute | solution.py:406
  35.6 14.6 %collective-permute-start.8 = (bf16[1,144,512]{2,1,0:T(8,128)(2,1)S(1)}, bf16[1,144,512]{2,1,0:T(8,128)(2,1)S(1)}, u32[]{:S(2)}, u32[]{:S(2)}) collective-permute-start(bf16[1,144,512]{2,1,0:T(8,128)(2,1)S(1)} %get-tuple-element.56), channel_id=1, source_target_pairs={{0,4},{4,0},{8,12},{12,8},{16,20},{20,16},{24,28},{28,24},{1,5},{5... | collective-permute-start | bytes 442376 | tf_op jit(solution)/shard_map/ppermute | solution.py:406
  41.1 18.1 %slice-start = ((s8[6307840]{0:T(1024)(128)(4,1)}), s8[4194304]{0:T(1024)(128)(4,1)S(1)}, s32[]{:S(2)}) async-start(s8[6307840]{0:T(1024)(128)(4,1)} %bitcast.2), calls=%async_computation | async-start | bytes 8388608
  48.1 11.2 %slice-start.1 = ((s8[6307840]{0:T(1024)(128)(4,1)}), s8[2113536]{0:T(1024)(128)(4,1)S(1)}, s32[]{:S(2)}) async-start(s8[6307840]{0:T(1024)(128)(4,1)} %bitcast.2), calls=%async_computation.1 | async-start | bytes 4227072
  48.1 11.0 %collective-permute-start.11 = (bf16[2,112,512]{2,1,0:T(8,128)(2,1)S(1)}, bf16[2,112,512]{2,1,0:T(8,128)(2,1)S(1)}, u32[]{:S(2)}, u32[]{:S(2)}) collective-permute-start(bf16[2,112,512]{2,1,0:T(8,128)(2,1)S(1)} %collective-permute-done.4.refs_2_), channel_id=1, source_target_pairs={{2,3},{1,0},{6,7},{5,4},{10,11},{9,8},{14,15},{13,12},{18,19},{17,... | collective-permute-start | bytes 688136 | tf_op jit(solution)/shard_map/ppermute | solution.py:413
  49.5 9.6 %collective-permute-start.12 = (bf16[2,112,512]{2,1,0:T(8,128)(2,1)S(1)}, bf16[2,112,512]{2,1,0:T(8,128)(2,1)S(1)}, u32[]{:S(2)}, u32[]{:S(2)}) collective-permute-start(bf16[2,112,512]{2,1,0:T(8,128)(2,1)S(1)} %get-tuple-element.43.refs_0_), channel_id=1, source_target_pairs={{1,2},{2,1},{5,6},{6,5},{9,10},{10,9},{13,14},{14,13},{17,18},{18,... | collective-permute-start | bytes 688136 | tf_op jit(solution)/shard_map/ppermute | solution.py:413
  59.9 16.7 %collective-permute-start.13 = (bf16[1120,128]{1,0:T(8,128)(2,1)S(1)}, bf16[1120,128]{1,0:T(8,128)(2,1)S(1)}, u32[]{:S(2)}, u32[]{:S(2)}) collective-permute-start(bf16[1120,128]{1,0:T(8,128)(2,1)S(1)} %project_3.2), channel_id=1, source_target_pairs={{0,1},{3,2},{4,5},{7,6},{8,9},{11,10},{12,13},{15,14},{16,17},{19,... | collective-permute-start | bytes 860168 | tf_op jit(solution)/shard_map/ppermute | solution.py:502
  69.7 6.9 %collective-permute-start.14 = (bf16[1120,128]{1,0:T(8,128)(2,1)S(1)}, bf16[1120,128]{1,0:T(8,128)(2,1)S(1)}, u32[]{:S(2)}, u32[]{:S(2)}) collective-permute-start(bf16[1120,128]{1,0:T(8,128)(2,1)S(1)} %project_3.2), channel_id=1, source_target_pairs={{1,2},{2,1},{5,6},{6,5},{9,10},{10,9},{13,14},{14,13},{17,18},{18,... | collective-permute-start | bytes 860168 | tf_op jit(solution)/shard_map/ppermute | solution.py:503
  70.6 10.7 %collective-permute-start.5 = (bf16[3,112,512]{2,1,0:T(8,128)(2,1)S(1)}, bf16[3,112,512]{2,1,0:T(8,128)(2,1)S(1)}, u32[]{:S(2)}, u32[]{:S(2)}) collective-permute-start(bf16[3,112,512]{2,1,0:T(8,128)(2,1)S(1)} %pad_maximum_fusion.2), channel_id=1, source_target_pairs={{0,4},{4,0},{8,12},{12,8},{16,20},{20,16},{24,28},{28,24},{1,5},{5... | collective-permute-start | bytes 1032200 | tf_op jit(solution)/shard_map/ppermute | solution.py:406
  71.8 17.3 %collective-permute-start.16 = (bf16[3,112,512]{2,1,0:T(8,128)(2,1)S(1)}, bf16[3,112,512]{2,1,0:T(8,128)(2,1)S(1)}, u32[]{:S(2)}, u32[]{:S(2)}) collective-permute-start(bf16[3,112,512]{2,1,0:T(8,128)(2,1)S(1)} %pad_maximum_fusion.3), channel_id=1, source_target_pairs={{4,8},{12,16},{20,24},{8,4},{16,12},{24,20},{5,9},{13,17},{21,25},... | collective-permute-start | bytes 1032200 | tf_op jit(solution)/shard_map/ppermute | solution.py:406
  76.6 19.6 %collective-permute-start.19 = (bf16[1120,128]{1,0:T(8,128)(2,1)S(1)}, bf16[1120,128]{1,0:T(8,128)(2,1)S(1)}, u32[]{:S(2)}, u32[]{:S(2)}) collective-permute-start(bf16[1120,128]{1,0:T(8,128)(2,1)S(1)} %project_1.2), channel_id=1, source_target_pairs={{0,1},{1,0},{2,3},{3,2},{4,5},{5,4},{6,7},{7,6},{8,9},{9,8},{10,11... | collective-permute-start | bytes 860168 | tf_op jit(solution)/shard_map/ppermute | solution.py:510
  81.1 16.0 %collective-permute-start.18 = (bf16[1120,128]{1,0:T(8,128)(2,1)S(1)}, bf16[1120,128]{1,0:T(8,128)(2,1)S(1)}, u32[]{:S(2)}, u32[]{:S(2)}) collective-permute-start(bf16[1120,128]{1,0:T(8,128)(2,1)S(1)} %project_2.2), channel_id=1, source_target_pairs={{0,2},{1,3},{2,0},{3,1},{4,6},{5,7},{6,4},{7,5},{8,10},{9,11},{10,... | collective-permute-start | bytes 860168 | tf_op jit(solution)/shard_map/ppermute | solution.py:509
  81.2 7.9 %collective-permute-start.15 = (bf16[1,112,512]{2,1,0:T(8,128)(2,1)S(1)}, bf16[1,112,512]{2,1,0:T(8,128)(2,1)S(1)}, u32[]{:S(2)}, u32[]{:S(2)}) collective-permute-start(bf16[1,112,512]{2,1,0:T(8,128)(2,1)S(1)} %get-tuple-element.64), channel_id=1, source_target_pairs={{0,4},{4,0},{8,12},{12,8},{16,20},{20,16},{24,28},{28,24},{1,5},{5... | collective-permute-start | bytes 344072 | tf_op jit(solution)/shard_map/ppermute | solution.py:406
  81.3 7.8 %collective-permute-start.17 = (bf16[1,112,512]{2,1,0:T(8,128)(2,1)S(1)}, bf16[1,112,512]{2,1,0:T(8,128)(2,1)S(1)}, u32[]{:S(2)}, u32[]{:S(2)}) collective-permute-start(bf16[1,112,512]{2,1,0:T(8,128)(2,1)S(1)} %get-tuple-element.63), channel_id=1, source_target_pairs={{4,8},{12,16},{20,24},{8,4},{16,12},{24,20},{5,9},{13,17},{21,25},... | collective-permute-start | bytes 344072 | tf_op jit(solution)/shard_map/ppermute | solution.py:406
  97.7 12.8 %copy-start.2 = (s32[4]{0:T(128)S(1)}, s32[4]{0:T(128)}, u32[]{:S(2)}) copy-start(s32[4]{0:T(128)} %width_ref.5) | copy-start | bytes 52
  97.7 7.3 %collective-permute-start.20 = (bf16[848,128]{1,0:T(8,128)(2,1)S(1)}, bf16[848,128]{1,0:T(8,128)(2,1)S(1)}, u32[]{:S(2)}, u32[]{:S(2)}) collective-permute-start(bf16[848,128]{1,0:T(8,128)(2,1)S(1)} %project_3.3), channel_id=1, source_target_pairs={{0,1},{3,2},{4,5},{7,6},{8,9},{11,10},{12,13},{15,14},{16,17},{19,... | collective-permute-start | bytes 651272 | tf_op jit(solution)/shard_map/ppermute | solution.py:502
  100.6 4.5 %collective-permute-start.21 = (bf16[848,128]{1,0:T(8,128)(2,1)S(1)}, bf16[848,128]{1,0:T(8,128)(2,1)S(1)}, u32[]{:S(2)}, u32[]{:S(2)}) collective-permute-start(bf16[848,128]{1,0:T(8,128)(2,1)S(1)} %project_3.3), channel_id=1, source_target_pairs={{1,2},{2,1},{5,6},{6,5},{9,10},{10,9},{13,14},{14,13},{17,18},{18,... | collective-permute-start | bytes 651272 | tf_op jit(solution)/shard_map/ppermute | solution.py:503
  105.7 13.5 %collective-permute-start.23 = (bf16[848,128]{1,0:T(8,128)(2,1)S(1)}, bf16[848,128]{1,0:T(8,128)(2,1)S(1)}, u32[]{:S(2)}, u32[]{:S(2)}) collective-permute-start(bf16[848,128]{1,0:T(8,128)(2,1)S(1)} %project_1.3), channel_id=1, source_target_pairs={{0,1},{1,0},{2,3},{3,2},{4,5},{5,4},{6,7},{7,6},{8,9},{9,8},{10,11... | collective-permute-start | bytes 651272 | tf_op jit(solution)/shard_map/ppermute | solution.py:510
  109.3 13.7 %collective-permute-start.22 = (bf16[848,128]{1,0:T(8,128)(2,1)S(1)}, bf16[848,128]{1,0:T(8,128)(2,1)S(1)}, u32[]{:S(2)}, u32[]{:S(2)}) collective-permute-start(bf16[848,128]{1,0:T(8,128)(2,1)S(1)} %project_2.3), channel_id=1, source_target_pairs={{0,2},{1,3},{2,0},{3,1},{4,6},{5,7},{6,4},{7,5},{8,10},{9,11},{10,... | collective-permute-start | bytes 651272 | tf_op jit(solution)/shard_map/ppermute | solution.py:509

commit v3 on v1

--- a/solution.py
+++ b/solution.py
@@ -398,9 +398,13 @@
     to_end = [(2, 3), (1, 0)]
     from_end = [(0, 1), (3, 2)]
 
-    def halos(packets, groups):
-        inner = [jnp.concatenate([packets[j][:1] for j in js], axis=0) for js in groups]
-        outer = [jnp.concatenate([packets[j][1:] for j in js], axis=0) for js in groups]
+    def edge_rows(packets, groups):
+        return [
+            [jnp.concatenate([packets[j][side : side + 1] for j in js], axis=0) for js in groups]
+            for side in range(2)
+        ]
+
+    def send_rows(inner, outer):
         return (
             [lax.ppermute(x, "row", sibling) for x in inner],
             [lax.ppermute(x, "row", beyond) for x in outer],
@@ -428,16 +432,18 @@
         in_specs=[pl.BlockSpec(memory_space=pl.ANY)],
         out_specs=[VMEM, VMEM],
         scratch_shapes=[pltpu.SemaphoreType.DMA((2, shards, 2))],
+        compiler_params=pltpu.CompilerParams(vmem_limit_bytes=36 * MIB),
         name="load_weights",
     )(after(expand_weight, own[0]))
     packets = relay(own[0], token)
     groups = ((0,), (1, 2), (3,))
-    inner, outer = halos(packets, groups)
-    upcoming = direct(after(own[1], packets[3]))
+    edges = edge_rows(packets, groups)
+    inner, outer = send_rows(*edges)
+    upcoming = direct(after(own[1], edges[0][-1], edges[1][-1]))
     for number, chunk in enumerate(chunks):
         if number:
             packets, groups = list(lax.optimization_barrier((*upcoming, hidden))[:shards]), ((0, 1, 2, 3),)
-            inner, outer = halos(packets, groups)
+            inner, outer = send_rows(*edge_rows(packets, groups))
             packets[0] = after(packets[0], far)
         whole = lambda shape: pl.BlockSpec(shape, lambda f, *_: (0,) * len(shape))
         rows = pl.pallas_call(
@@ -448,9 +454,9 @@
             scratch_shapes=[pltpu.VMEM((chunk.tokens, full_depth), jnp.bfloat16)],
             compiler_params=pltpu.CompilerParams(vmem_limit_bytes=16 * MIB),
             cost_estimate=pl.CostEstimate(
-                flops=4 * chunk.tokens * full_depth * hidden_count,
-                bytes_accessed=4 * full_depth * hidden_count,
-                transcendentals=2 * chunk.tokens * hidden_count,
+                flops=1000,
+                bytes_accessed=1000,
+                transcendentals=0,
             ),
             name="expand_own",
         )(*packets, masks[number], parameters, weights)
@@ -464,9 +470,9 @@
             scratch_shapes=[pltpu.VMEM((chunk.tokens, full_depth), jnp.bfloat16)],
             compiler_params=pltpu.CompilerParams(vmem_limit_bytes=16 * MIB),
             cost_estimate=pl.CostEstimate(
-                flops=4 * chunk.tokens * full_depth * hidden_count,
-                bytes_accessed=4 * full_depth * hidden_count,
-                transcendentals=3 * chunk.tokens * hidden_count,
+                flops=1000,
+                bytes_accessed=1000,
+                transcendentals=0,
             ),
             name="expand_conv",
         )(*inner, *outer, rows, masks[number], parameters, weights)
@@ -490,7 +496,7 @@
                     in_specs=[weight_of(j), whole(hidden.shape)] + [whole(chunk.unit)] * len(added),
                     out_specs=whole(chunk.unit),
                 ),
-                compiler_params=pltpu.CompilerParams(vmem_limit_bytes=24 * MIB),
+                compiler_params=pltpu.CompilerParams(vmem_limit_bytes=16 * MIB),
                 cost_estimate=cost,
                 name=f"project_{j}",
             )(me, project_turned, hidden, *added)
@@ -520,7 +526,7 @@
                 + [whole(latents.shape)] * len(extra),
                 out_specs=whole(latents.shape),
             ),
-            compiler_params=pltpu.CompilerParams(vmem_limit_bytes=24 * MIB),
+            compiler_params=pltpu.CompilerParams(vmem_limit_bytes=16 * MIB),
             cost_estimate=cost,
             name="finish",
         )(me, clip_width, masks[number], project_turned, hidden, *arrived, *extra)

time: 121 us -> 111 us (0.917)
  the two profiles are of different devices: /device:TPU:0 before, /device:TPU:2 now
where the time goes in v3:
time: 111 us; the launch traced here: 110 us
  starting transfers between devices  41.3 us (37%)
  Pallas kernels  34.7 us (31%)
  waiting for transfers between devices  23.2 us (21%)
  local copies, waits for them, and re-layouts  10.6 us (10%)
    pallas_call x2, Pallas kernels, on_device_packed(): pl.pallas_call(functools.partial(hidden_kernel, chunk=chunk, shards=shard...  12 us
    unnamed x26, local copies, waits for them, and re-layouts  9.71 us
    ppermute x2, waiting for transfers between devices, on_device_packed(): lax.ppermute(last_unit, 'tensor', two_off)  8.4 us
    ppermute x4, starting transfers between devices, send_rows(): lax.ppermute(x, 'row', beyond)  8.12 us
    ppermute x2, starting transfers between devices, on_device_packed(): lax.ppermute(after(close, relayed), 'tensor', near)  7.68 us
    ppermute x3, starting transfers between devices, direct(): lax.ppermute(mine, 'tensor', [(i, i ^ j) for i in range(4)])  7.39 us
    pallas_call x2, Pallas kernels, on_device_packed(): pl.pallas_call(functools.partial(own_kernel, chunk=chunk, shards=shards),...  7.05 us
    ppermute x2, waiting for transfers between devices, on_device_packed(): lax.ppermute(after(close, relayed), 'tensor', near)  6.34 us
  transfers between devices with their start and end apart: 23, of which 9 were waited for; matrix products, arithmetic and copies ran while one was open for 1% of the time, Pallas kernels for 26%

profile of v3, /device:TPU:2, one launch (start us, length us, event | category | flops | bytes accessed | tf_op | source)
XLA Modules:
  0.0 110.5 jit_solution(9168464457474509656)
XLA Ops:
  0.0 2.8 %pack.1 = (bf16[2,144,512]{2,1,0:T(8,128)(2,1)}, bf16[2,112,512]{2,1,0:T(8,128)(2,1)}, f32[4,128,128]{2,1,0:T(8,128)}, f32[4,96,128]{2,1,0:T(8,128)}) custom-call(s32[4]{0:T(128)} %height_ref.1, s32[4]{0:T(128)} %width_ref.5, bf16[4,2,64,560]{3,2,1,0:T(8,128)(2,1)} %x_ref.1), custom_call_target="tpu_custom_call" | custom-call | tf_op jit(solution)/shard_map/pack/pallas_call | solution.py:376
  2.8 2.7 %collective-permute-start = (bf16[2,144,512]{2,1,0:T(8,128)(2,1)}, bf16[2,144,512]{2,1,0:T(8,128)(2,1)S(1)}, u32[]{:S(2)}, u32[]{:S(2)}) collective-permute-start(bf16[2,144,512]{2,1,0:T(8,128)(2,1)} %get-tuple-element.33.refs_0_), channel_id=1, source_target_pairs={{0,2},{1,3},{2,0},{3,1},{4,6},{5,7},{6,4},{7,5},{8,10},{9,11},{10,... | collective-permute-start | bytes 884744 | tf_op jit(solution)/shard_map/ppermute | solution.py:414
  5.5 1.6 %collective-permute-start.7 = (bf16[2,144,512]{2,1,0:T(8,128)(2,1)}, bf16[2,144,512]{2,1,0:T(8,128)(2,1)S(1)}, u32[]{:S(2)}, u32[]{:S(2)}) collective-permute-start(bf16[2,144,512]{2,1,0:T(8,128)(2,1)} %get-tuple-element.33.refs_0_), channel_id=1, source_target_pairs={{0,1},{1,0},{2,3},{3,2},{4,5},{5,4},{6,7},{7,6},{8,9},{9,8},{10,11... | collective-permute-start | bytes 884744 | tf_op jit(solution)/shard_map/ppermute | solution.py:415
  7.0 5.3 %load_weights.1 = (bf16[2,2240,1400]{2,1,0:T(8,128)(2,1)S(1)}, f32[8,128]{1,0:T(8,128)}) custom-call(bf16[2,2240,1400]{2,1,0:T(8,128)(2,1)} %w_ref), custom_call_target="tpu_custom_call" | custom-call | tf_op jit(solution)/shard_map/load_weights/pallas_call | solution.py:426
  12.4 4.5 %copy-done = bf16[2,2240,1400]{2,1,0:T(8,128)(2,1)} copy-done((bf16[2,2240,1400]{2,1,0:T(8,128)(2,1)}, bf16[2,2240,1400]{2,1,0:T(8,128)(2,1)S(1)}, u32[]{:S(2)}) %copy-start) | copy-done | bytes 12544024
  16.9 2.2 %collective-permute-done.refs_2_ = bf16[2,144,512]{2,1,0:T(8,128)(2,1)S(1)} collective-permute-done((bf16[2,144,512]{2,1,0:T(8,128)(2,1)}, bf16[2,144,512]{2,1,0:T(8,128)(2,1)S(1)}, u32[]{:S(2)}, u32[]{:S(2)}) %collective-permute-start) | collective-permute-done | bytes 294944 | tf_op jit(solution)/shard_map/ppermute | solution.py:414
  19.2 0.7 collective-permute-start.1
  19.8 1.3 %collective-permute-start.2 = (bf16[2,144,512]{2,1,0:T(8,128)(2,1)S(1)}, bf16[2,144,512]{2,1,0:T(8,128)(2,1)S(1)}, u32[]{:S(2)}, u32[]{:S(2)}) collective-permute-start(bf16[2,144,512]{2,1,0:T(8,128)(2,1)S(1)} %collective-permute-done.refs_2_), channel_id=1, source_target_pairs={{2,3},{1,0},{6,7},{5,4},{10,11},{9,8},{14,15},{13,12},{18,19},{17,... | collective-permute-start | bytes 884744 | tf_op jit(solution)/shard_map/ppermute | solution.py:417
  21.2 1.9 %collective-permute-start.11 = (bf16[2,144,512]{2,1,0:T(8,128)(2,1)S(1)}, bf16[2,144,512]{2,1,0:T(8,128)(2,1)S(1)}, u32[]{:S(2)}, u32[]{:S(2)}) collective-permute-start(bf16[2,144,512]{2,1,0:T(8,128)(2,1)S(1)} %pad_maximum_fusion.3), channel_id=1, source_target_pairs={{4,8},{12,16},{20,24},{8,4},{16,12},{24,20},{5,9},{13,17},{21,25},... | collective-permute-start | bytes 884744 | tf_op jit(solution)/shard_map/ppermute | solution.py:410
  23.2 1.7 %collective-permute-start.8 = (bf16[2,144,512]{2,1,0:T(8,128)(2,1)S(1)}, bf16[2,144,512]{2,1,0:T(8,128)(2,1)S(1)}, u32[]{:S(2)}, u32[]{:S(2)}) collective-permute-start(bf16[2,144,512]{2,1,0:T(8,128)(2,1)S(1)} %pad_maximum_fusion.2), channel_id=1, source_target_pairs={{0,4},{4,0},{8,12},{12,8},{16,20},{20,16},{24,28},{28,24},{1,5},{5... | collective-permute-start | bytes 884744 | tf_op jit(solution)/shard_map/ppermute | solution.py:409
  24.9 0.7 fusion.2
  25.6 2.0 %collective-permute-start.10 = (bf16[1,144,512]{2,1,0:T(8,128)(2,1)}, bf16[1,144,512]{2,1,0:T(8,128)(2,1)S(1)}, u32[]{:S(2)}, u32[]{:S(2)}) collective-permute-start(bf16[1,144,512]{2,1,0:T(8,128)(2,1)} %get-tuple-element.55), channel_id=1, source_target_pairs={{4,8},{12,16},{20,24},{8,4},{16,12},{24,20},{5,9},{13,17},{21,25},... | collective-permute-start | bytes 442376 | tf_op jit(solution)/shard_map/ppermute | solution.py:410
  27.8 1.5 %collective-permute-start.6 = (bf16[1,144,512]{2,1,0:T(8,128)(2,1)}, bf16[1,144,512]{2,1,0:T(8,128)(2,1)S(1)}, u32[]{:S(2)}, u32[]{:S(2)}) collective-permute-start(bf16[1,144,512]{2,1,0:T(8,128)(2,1)} %get-tuple-element.56), channel_id=1, source_target_pairs={{0,4},{4,0},{8,12},{12,8},{16,20},{20,16},{24,28},{28,24},{1,5},{5... | collective-permute-start | bytes 442376 | tf_op jit(solution)/shard_map/ppermute | solution.py:409
  29.3 0.9 collective-permute-done.2
  30.3 1.9 %collective-permute-start.12 = (bf16[1,144,512]{2,1,0:T(8,128)(2,1)S(1)}, bf16[1,144,512]{2,1,0:T(8,128)(2,1)S(1)}, u32[]{:S(2)}, u32[]{:S(2)}) collective-permute-start(bf16[1,144,512]{2,1,0:T(8,128)(2,1)S(1)} %get-tuple-element.57), channel_id=1, source_target_pairs={{4,8},{12,16},{20,24},{8,4},{16,12},{24,20},{5,9},{13,17},{21,25},... | collective-permute-start | bytes 442376 | tf_op jit(solution)/shard_map/ppermute | solution.py:410
  32.3 0.7 collective-permute-done.10.refs_3_
  32.9 1.9 %collective-permute-start.9 = (bf16[1,144,512]{2,1,0:T(8,128)(2,1)S(1)}, bf16[1,144,512]{2,1,0:T(8,128)(2,1)S(1)}, u32[]{:S(2)}, u32[]{:S(2)}) collective-permute-start(bf16[1,144,512]{2,1,0:T(8,128)(2,1)S(1)} %get-tuple-element.58), channel_id=1, source_target_pairs={{0,4},{4,0},{8,12},{12,8},{16,20},{20,16},{24,28},{28,24},{1,5},{5... | collective-permute-start | bytes 442376 | tf_op jit(solution)/shard_map/ppermute | solution.py:409
  34.8 3.1 %collective-permute-start.3 = (bf16[2,112,512]{2,1,0:T(8,128)(2,1)S(1)}, bf16[2,112,512]{2,1,0:T(8,128)(2,1)S(1)}, u32[]{:S(2)}, u32[]{:S(2)}) collective-permute-start(bf16[2,112,512]{2,1,0:T(8,128)(2,1)S(1)} %copy-done.6), channel_id=1, source_target_pairs={{0,1},{1,0},{2,3},{3,2},{4,5},{5,4},{6,7},{7,6},{8,9},{9,8},{10,11... | collective-permute-start | bytes 688136 | tf_op jit(solution)/shard_map/ppermute | solution.py:422
  37.9 2.8 %collective-permute-start.4 = (bf16[2,112,512]{2,1,0:T(8,128)(2,1)S(1)}, bf16[2,112,512]{2,1,0:T(8,128)(2,1)S(1)}, u32[]{:S(2)}, u32[]{:S(2)}) collective-permute-start(bf16[2,112,512]{2,1,0:T(8,128)(2,1)S(1)} %copy-done.6), channel_id=1, source_target_pairs={{0,2},{1,3},{2,0},{3,1},{4,6},{5,7},{6,4},{7,5},{8,10},{9,11},{10,... | collective-permute-start | bytes 688136 | tf_op jit(solution)/shard_map/ppermute | solution.py:422
  40.8 1.5 %collective-permute-start.5 = (bf16[2,112,512]{2,1,0:T(8,128)(2,1)S(1)}, bf16[2,112,512]{2,1,0:T(8,128)(2,1)S(1)}, u32[]{:S(2)}, u32[]{:S(2)}) collective-permute-start(bf16[2,112,512]{2,1,0:T(8,128)(2,1)S(1)} %copy-done.6), channel_id=1, source_target_pairs={{0,3},{1,2},{2,1},{3,0},{4,7},{5,6},{6,5},{7,4},{8,11},{9,10},{10,... | collective-permute-start | bytes 688136 | tf_op jit(solution)/shard_map/ppermute | solution.py:422
  42.3 4.6 %copy-done.1 = bf16[2,2240,1400]{2,1,0:T(8,128)(2,1)S(1)} copy-done((bf16[2,2240,1400]{2,1,0:T(8,128)(2,1)S(1)}, bf16[2,2240,1400]{2,1,0:T(8,128)(2,1)}, u32[]{:S(2)}) %copy-start.1) | copy-done | bytes 12544024
  46.9 4.0 %expand_own.2.refs_6_ = f32[2,256,1400]{2,1,0:T(8,128)S(1)} custom-call(bf16[2,144,512]{2,1,0:T(8,128)(2,1)S(1)} %copy-done.5, bf16[2,144,512]{2,1,0:T(8,128)(2,1)S(1)} %collective-permute-done.7.refs_1_, bf16[2,144,512]{2,1,0:T(8,128)(2,1)S(1)} %collective-permute-done.refs_2_, bf16[2,144,512]{2,1,0:T(8,128)(2,1)S(1)} %add.3.refs_3_, ...), custom_call_target="tpu_custom_call" | custom-call | flops 1000 | bytes 1000 | tf_op jit(solution)/shard_map/expand_own/pallas_call | solution.py:449
  50.9 0.5 copy-done.2
  51.4 6.8 %expand_conv.2.hidden_ref = bf16[256,1400]{1,0:T(8,128)(2,1)S(1)} custom-call(bf16[1,144,512]{2,1,0:T(8,128)(2,1)S(1)} %collective-permute-done.6.refs_0_, bf16[2,144,512]{2,1,0:T(8,128)(2,1)S(1)} %collective-permute-done.8.refs_1_, bf16[1,144,512]{2,1,0:T(8,128)(2,1)S(1)} %collective-permute-done.9.refs_2_, ...), custom_call_target="tpu_custom_call" | custom-call | flops 1000 | bytes 1000 | tf_op jit(solution)/shard_map/expand_conv/pallas_call | solution.py:465
  58.3 0.6 project_3.2
  59.0 2.4 %collective-permute-start.14 = (bf16[1120,128]{1,0:T(8,128)(2,1)S(1)}, bf16[1120,128]{1,0:T(8,128)(2,1)S(1)}, u32[]{:S(2)}, u32[]{:S(2)}) collective-permute-start(bf16[1120,128]{1,0:T(8,128)(2,1)S(1)} %project_3.2), channel_id=1, source_target_pairs={{0,1},{3,2},{4,5},{7,6},{8,9},{11,10},{12,13},{15,14},{16,17},{19,... | collective-permute-start | bytes 860168 | tf_op jit(solution)/shard_map/ppermute | solution.py:507
  61.4 0.7 collective-permute-start.15
  62.4 2.2 %collective-permute-start.16 = (bf16[4,112,512]{2,1,0:T(8,128)(2,1)S(1)}, bf16[4,112,512]{2,1,0:T(8,128)(2,1)S(1)}, u32[]{:S(2)}, u32[]{:S(2)}) collective-permute-start(bf16[4,112,512]{2,1,0:T(8,128)(2,1)S(1)} %pad_maximum_fusion.1), channel_id=1, source_target_pairs={{4,8},{12,16},{20,24},{8,4},{16,12},{24,20},{5,9},{13,17},{21,25},... | collective-permute-start | bytes 1376264 | tf_op jit(solution)/shard_map/ppermute | solution.py:410
  64.7 0.7 project_1.2
  65.3 1.8 %collective-permute-done.14.refs_0_ = bf16[1120,128]{1,0:T(8,128)(2,1)S(1)} collective-permute-done((bf16[1120,128]{1,0:T(8,128)(2,1)S(1)}, bf16[1120,128]{1,0:T(8,128)(2,1)S(1)}, u32[]{:S(2)}, u32[]{:S(2)}) %collective-permute-start.14) | collective-permute-done | bytes 286752 | tf_op jit(solution)/shard_map/ppermute | solution.py:507
  67.1 0.6 project_2.2
  67.8 3.8 %collective-permute-start.18 = (bf16[1120,128]{1,0:T(8,128)(2,1)S(1)}, bf16[1120,128]{1,0:T(8,128)(2,1)S(1)}, u32[]{:S(2)}, u32[]{:S(2)}) collective-permute-start(bf16[1120,128]{1,0:T(8,128)(2,1)S(1)} %project_1.2), channel_id=1, source_target_pairs={{0,1},{1,0},{2,3},{3,2},{4,5},{5,4},{6,7},{7,6},{8,9},{9,8},{10,11... | collective-permute-start | bytes 860168 | tf_op jit(solution)/shard_map/ppermute | solution.py:515
  71.6 1.2 %collective-permute-start.17 = (bf16[1120,128]{1,0:T(8,128)(2,1)S(1)}, bf16[1120,128]{1,0:T(8,128)(2,1)S(1)}, u32[]{:S(2)}, u32[]{:S(2)}) collective-permute-start(bf16[1120,128]{1,0:T(8,128)(2,1)S(1)} %project_2.2), channel_id=1, source_target_pairs={{0,2},{1,3},{2,0},{3,1},{4,6},{5,7},{6,4},{7,5},{8,10},{9,11},{10,... | collective-permute-start | bytes 860168 | tf_op jit(solution)/shard_map/ppermute | solution.py:514
  72.9 3.0 %expand_own.3.refs_2_ = f32[2,192,1400]{2,1,0:T(8,128)S(1)} custom-call(bf16[2,112,512]{2,1,0:T(8,128)(2,1)S(1)} %copy-done.6, bf16[2,112,512]{2,1,0:T(8,128)(2,1)S(1)} %collective-permute-done.3.refs_1_, bf16[2,112,512]{2,1,0:T(8,128)(2,1)S(1)} %collective-permute-done.4.refs_2_, bf16[2,112,512]{2,1,0:T(8,128)(2,1)S(1)} %collective-permute-done.5.refs_3_, ...), custom_call_target="tpu_custom_call" | custom-call | flops 1000 | bytes 1000 | tf_op jit(solution)/shard_map/expand_own/pallas_call | solution.py:449
  76.0 5.2 %expand_conv.3.hidden_ref = bf16[192,1400]{1,0:T(8,128)(2,1)S(1)} custom-call(bf16[4,112,512]{2,1,0:T(8,128)(2,1)S(1)} %collective-permute-done.13.refs_0_, bf16[4,112,512]{2,1,0:T(8,128)(2,1)S(1)} %collective-permute-done.16.refs_1_, f32[2,192,1400]{2,1,0:T(8,128)S(1)} %expand_own.3.refs_2_, f32[4,96,128]{2,1,0:T(8,128)S(1)} %copy-done.4, ...), custom_call_target="tpu_custom_call" | custom-call | flops 1000 | bytes 1000 | tf_op jit(solution)/shard_map/expand_conv/pallas_call | solution.py:465
  81.2 2.0 %collective-permute-done.18.refs_2_ = bf16[1120,128]{1,0:T(8,128)(2,1)S(1)} collective-permute-done((bf16[1120,128]{1,0:T(8,128)(2,1)S(1)}, bf16[1120,128]{1,0:T(8,128)(2,1)S(1)}, u32[]{:S(2)}, u32[]{:S(2)}) %collective-permute-start.18) | collective-permute-done | bytes 286752 | tf_op jit(solution)/shard_map/ppermute | solution.py:515
  83.1 3.2 %collective-permute-done.17.refs_1_ = bf16[1120,128]{1,0:T(8,128)(2,1)S(1)} collective-permute-done((bf16[1120,128]{1,0:T(8,128)(2,1)S(1)}, bf16[1120,128]{1,0:T(8,128)(2,1)S(1)}, u32[]{:S(2)}, u32[]{:S(2)}) %collective-permute-start.17) | collective-permute-done | bytes 286752 | tf_op jit(solution)/shard_map/ppermute | solution.py:514
  86.3 0.7 project_3.3
  87.0 1.7 %collective-permute-start.19 = (bf16[848,128]{1,0:T(8,128)(2,1)S(1)}, bf16[848,128]{1,0:T(8,128)(2,1)S(1)}, u32[]{:S(2)}, u32[]{:S(2)}) collective-permute-start(bf16[848,128]{1,0:T(8,128)(2,1)S(1)} %project_3.3), channel_id=1, source_target_pairs={{0,1},{3,2},{4,5},{7,6},{8,9},{11,10},{12,13},{15,14},{16,17},{19,... | collective-permute-start | bytes 651272 | tf_op jit(solution)/shard_map/ppermute | solution.py:507
  88.7 0.7 collective-permute-start.20
  89.4 0.7 project_1.3
  90.1 2.7 %collective-permute-done.19.refs_0_ = bf16[848,128]{1,0:T(8,128)(2,1)S(1)} collective-permute-done((bf16[848,128]{1,0:T(8,128)(2,1)S(1)}, bf16[848,128]{1,0:T(8,128)(2,1)S(1)}, u32[]{:S(2)}, u32[]{:S(2)}) %collective-permute-start.19) | collective-permute-done | bytes 217120 | tf_op jit(solution)/shard_map/ppermute | solution.py:507
  92.8 0.7 project_2.3
  93.5 3.8 %collective-permute-start.22 = (bf16[848,128]{1,0:T(8,128)(2,1)S(1)}, bf16[848,128]{1,0:T(8,128)(2,1)S(1)}, u32[]{:S(2)}, u32[]{:S(2)}) collective-permute-start(bf16[848,128]{1,0:T(8,128)(2,1)S(1)} %project_1.3), channel_id=1, source_target_pairs={{0,1},{1,0},{2,3},{3,2},{4,5},{5,4},{6,7},{7,6},{8,9},{9,8},{10,11... | collective-permute-start | bytes 651272 | tf_op jit(solution)/shard_map/ppermute | solution.py:515
  97.4 1.3 %finish.2.refs_3_ = bf16[4,2,64,560]{3,2,1,0:T(8,128)(2,1)S(1)} custom-call(s32[1]{0:T(128)} %bitcast.place_ref, s32[4]{0:T(128)S(1)} %copy-done.7, f32[4,128,128]{2,1,0:T(8,128)S(1)} %copy-done.3, bf16[2240,1400]{1,0:T(8,128)(2,1)S(1)} %bitcast.10, bf16[256,1400]{1,0:T(8,128)(2,1)S(1)} %expand_conv.2.hidden_ref, ...), custom_call_target="tpu_custom_call" | custom-call | flops 401408000 | bytes 2284800 | tf_op jit(solution)/shard_map/finish/pallas_call | solution.py:518
  98.7 4.4 %collective-permute-done.22.refs_2_ = bf16[848,128]{1,0:T(8,128)(2,1)S(1)} collective-permute-done((bf16[848,128]{1,0:T(8,128)(2,1)S(1)}, bf16[848,128]{1,0:T(8,128)(2,1)S(1)}, u32[]{:S(2)}, u32[]{:S(2)}) %collective-permute-start.22) | collective-permute-done | bytes 217120 | tf_op jit(solution)/shard_map/ppermute | solution.py:515
  103.1 5.2 %collective-permute-done.21.refs_1_ = bf16[848,128]{1,0:T(8,128)(2,1)S(1)} collective-permute-done((bf16[848,128]{1,0:T(8,128)(2,1)S(1)}, bf16[848,128]{1,0:T(8,128)(2,1)S(1)}, u32[]{:S(2)}, u32[]{:S(2)}) %collective-permute-start.21) | collective-permute-done | bytes 217120 | tf_op jit(solution)/shard_map/ppermute | solution.py:514
  108.3 2.2 %finish.3 = bf16[4,2,64,560]{3,2,1,0:T(8,128)(2,1)} custom-call(s32[1]{0:T(128)} %bitcast.place_ref, s32[4]{0:T(128)S(1)} %copy-done.7, f32[4,96,128]{2,1,0:T(8,128)S(1)} %copy-done.4, bf16[2240,1400]{1,0:T(8,128)(2,1)S(1)} %bitcast.11, bf16[192,1400]{1,0:T(8,128)(2,1)S(1)} %expand_conv.3.hidden_ref, bf16[848,128]{1,0:T(8,128)(2,1)S(1)} %collective-permute-done.20.refs_0_, ...), custom_call_target="tpu_custom_call" | custom-call | flops 301056000 | bytes 2105600 | tf_op jit(solution)/shard_map/finish/pallas_call | solution.py:518
  (52 shorter events, 0.7 us)
Async XLA Ops:
  2.8 16.4 %copy-start.5 = (bf16[2,144,512]{2,1,0:T(8,128)(2,1)S(1)}, bf16[2,144,512]{2,1,0:T(8,128)(2,1)}, u32[]{:S(2)}) copy-start(bf16[2,144,512]{2,1,0:T(8,128)(2,1)} %get-tuple-element.33.refs_0_) | copy-start | bytes 884740
  2.8 24.9 %copy-start.8 = (f32[3,3,2,1400]{3,2,1,0:T(2,128)S(1)}, f32[3,3,2,1400]{3,2,1,0:T(2,128)}, u32[]{:S(2)}) copy-start(f32[3,3,2,1400]{3,2,1,0:T(2,128)} %param.13) | copy-start | bytes 302404
  2.8 32.1 %copy-start.6 = (bf16[2,112,512]{2,1,0:T(8,128)(2,1)S(1)}, bf16[2,112,512]{2,1,0:T(8,128)(2,1)}, u32[]{:S(2)}) copy-start(bf16[2,112,512]{2,1,0:T(8,128)(2,1)} %get-tuple-element.44.refs_0_) | copy-start | bytes 688132
  2.8 39.5 %copy-start.9 = (f32[2,1400]{1,0:T(2,128)S(1)}, f32[2,1400]{1,0:T(2,128)}, u32[]{:S(2)}) copy-start(f32[2,1400]{1,0:T(2,128)} %param.14) | copy-start | bytes 33604
  2.8 39.4 %copy-start.10 = (f32[2,1400]{1,0:T(2,128)S(1)}, f32[2,1400]{1,0:T(2,128)}, u32[]{:S(2)}) copy-start(f32[2,1400]{1,0:T(2,128)} %param.12) | copy-start | bytes 33604
  2.8 39.5 %copy-start.3 = (f32[4,128,128]{2,1,0:T(8,128)S(1)}, f32[4,128,128]{2,1,0:T(8,128)}, u32[]{:S(2)}) copy-start(f32[4,128,128]{2,1,0:T(8,128)} %get-tuple-element.36.refs_4_.refs_7_.mask_ref) | copy-start | bytes 786436
  2.8 16.3 %collective-permute-start = (bf16[2,144,512]{2,1,0:T(8,128)(2,1)}, bf16[2,144,512]{2,1,0:T(8,128)(2,1)S(1)}, u32[]{:S(2)}, u32[]{:S(2)}) collective-permute-start(bf16[2,144,512]{2,1,0:T(8,128)(2,1)} %get-tuple-element.33.refs_0_), channel_id=1, source_target_pairs={{0,2},{1,3},{2,0},{3,1},{4,6},{5,7},{6,4},{7,5},{8,10},{9,11},{10,... | collective-permute-start | bytes 884744 | tf_op jit(solution)/shard_map/ppermute | solution.py:414
  5.5 15.7 %collective-permute-start.7 = (bf16[2,144,512]{2,1,0:T(8,128)(2,1)}, bf16[2,144,512]{2,1,0:T(8,128)(2,1)S(1)}, u32[]{:S(2)}, u32[]{:S(2)}) collective-permute-start(bf16[2,144,512]{2,1,0:T(8,128)(2,1)} %get-tuple-element.33.refs_0_), channel_id=1, source_target_pairs={{0,1},{1,0},{2,3},{3,2},{4,5},{5,4},{6,7},{7,6},{8,9},{9,8},{10,11... | collective-permute-start | bytes 884744 | tf_op jit(solution)/shard_map/ppermute | solution.py:415
  12.4 4.6 %copy-start = (bf16[2,2240,1400]{2,1,0:T(8,128)(2,1)}, bf16[2,2240,1400]{2,1,0:T(8,128)(2,1)S(1)}, u32[]{:S(2)}) copy-start(bf16[2,2240,1400]{2,1,0:T(8,128)(2,1)S(1)} %get-tuple-element.37.refs_6_.refs_9_.refs_5_) | copy-start | bytes 37632004
  19.2 8.6 %collective-permute-start.1 = (bf16[2,144,512]{2,1,0:T(8,128)(2,1)S(1)}, bf16[2,144,512]{2,1,0:T(8,128)(2,1)S(1)}, u32[]{:S(2)}, u32[]{:S(2)}) collective-permute-start(bf16[2,144,512]{2,1,0:T(8,128)(2,1)S(1)} %copy-done.5), channel_id=1, source_target_pairs={{1,2},{2,1},{5,6},{6,5},{9,10},{10,9},{13,14},{14,13},{17,18},{18,... | collective-permute-start | bytes 884744 | tf_op jit(solution)/shard_map/ppermute | solution.py:416
  19.8 10.4 %collective-permute-start.2 = (bf16[2,144,512]{2,1,0:T(8,128)(2,1)S(1)}, bf16[2,144,512]{2,1,0:T(8,128)(2,1)S(1)}, u32[]{:S(2)}, u32[]{:S(2)}) collective-permute-start(bf16[2,144,512]{2,1,0:T(8,128)(2,1)S(1)} %collective-permute-done.refs_2_), channel_id=1, source_target_pairs={{2,3},{1,0},{6,7},{5,4},{10,11},{9,8},{14,15},{13,12},{18,19},{17,... | collective-permute-start | bytes 884744 | tf_op jit(solution)/shard_map/ppermute | solution.py:417
  21.2 16.7 %collective-permute-start.11 = (bf16[2,144,512]{2,1,0:T(8,128)(2,1)S(1)}, bf16[2,144,512]{2,1,0:T(8,128)(2,1)S(1)}, u32[]{:S(2)}, u32[]{:S(2)}) collective-permute-start(bf16[2,144,512]{2,1,0:T(8,128)(2,1)S(1)} %pad_maximum_fusion.3), channel_id=1, source_target_pairs={{4,8},{12,16},{20,24},{8,4},{16,12},{24,20},{5,9},{13,17},{21,25},... | collective-permute-start | bytes 884744 | tf_op jit(solution)/shard_map/ppermute | solution.py:410
  23.2 17.6 %collective-permute-start.8 = (bf16[2,144,512]{2,1,0:T(8,128)(2,1)S(1)}, bf16[2,144,512]{2,1,0:T(8,128)(2,1)S(1)}, u32[]{:S(2)}, u32[]{:S(2)}) collective-permute-start(bf16[2,144,512]{2,1,0:T(8,128)(2,1)S(1)} %pad_maximum_fusion.2), channel_id=1, source_target_pairs={{0,4},{4,0},{8,12},{12,8},{16,20},{20,16},{24,28},{28,24},{1,5},{5... | collective-permute-start | bytes 884744 | tf_op jit(solution)/shard_map/ppermute | solution.py:409
  25.6 7.3 %collective-permute-start.10 = (bf16[1,144,512]{2,1,0:T(8,128)(2,1)}, bf16[1,144,512]{2,1,0:T(8,128)(2,1)S(1)}, u32[]{:S(2)}, u32[]{:S(2)}) collective-permute-start(bf16[1,144,512]{2,1,0:T(8,128)(2,1)} %get-tuple-element.55), channel_id=1, source_target_pairs={{4,8},{12,16},{20,24},{8,4},{16,12},{24,20},{5,9},{13,17},{21,25},... | collective-permute-start | bytes 442376 | tf_op jit(solution)/shard_map/ppermute | solution.py:410
  27.8 7.1 %collective-permute-start.6 = (bf16[1,144,512]{2,1,0:T(8,128)(2,1)}, bf16[1,144,512]{2,1,0:T(8,128)(2,1)S(1)}, u32[]{:S(2)}, u32[]{:S(2)}) collective-permute-start(bf16[1,144,512]{2,1,0:T(8,128)(2,1)} %get-tuple-element.56), channel_id=1, source_target_pairs={{0,4},{4,0},{8,12},{12,8},{16,20},{20,16},{24,28},{28,24},{1,5},{5... | collective-permute-start | bytes 442376 | tf_op jit(solution)/shard_map/ppermute | solution.py:409
  30.3 20.6 %collective-permute-start.12 = (bf16[1,144,512]{2,1,0:T(8,128)(2,1)S(1)}, bf16[1,144,512]{2,1,0:T(8,128)(2,1)S(1)}, u32[]{:S(2)}, u32[]{:S(2)}) collective-permute-start(bf16[1,144,512]{2,1,0:T(8,128)(2,1)S(1)} %get-tuple-element.57), channel_id=1, source_target_pairs={{4,8},{12,16},{20,24},{8,4},{16,12},{24,20},{5,9},{13,17},{21,25},... | collective-permute-start | bytes 442376 | tf_op jit(solution)/shard_map/ppermute | solution.py:410
  32.9 18.0 %collective-permute-start.9 = (bf16[1,144,512]{2,1,0:T(8,128)(2,1)S(1)}, bf16[1,144,512]{2,1,0:T(8,128)(2,1)S(1)}, u32[]{:S(2)}, u32[]{:S(2)}) collective-permute-start(bf16[1,144,512]{2,1,0:T(8,128)(2,1)S(1)} %get-tuple-element.58), channel_id=1, source_target_pairs={{0,4},{4,0},{8,12},{12,8},{16,20},{20,16},{24,28},{28,24},{1,5},{5... | collective-permute-start | bytes 442376 | tf_op jit(solution)/shard_map/ppermute | solution.py:409
  34.8 27.3 %collective-permute-start.3 = (bf16[2,112,512]{2,1,0:T(8,128)(2,1)S(1)}, bf16[2,112,512]{2,1,0:T(8,128)(2,1)S(1)}, u32[]{:S(2)}, u32[]{:S(2)}) collective-permute-start(bf16[2,112,512]{2,1,0:T(8,128)(2,1)S(1)} %copy-done.6), channel_id=1, source_target_pairs={{0,1},{1,0},{2,3},{3,2},{4,5},{5,4},{6,7},{7,6},{8,9},{9,8},{10,11... | collective-permute-start | bytes 688136 | tf_op jit(solution)/shard_map/ppermute | solution.py:422
  37.9 24.2 %collective-permute-start.4 = (bf16[2,112,512]{2,1,0:T(8,128)(2,1)S(1)}, bf16[2,112,512]{2,1,0:T(8,128)(2,1)S(1)}, u32[]{:S(2)}, u32[]{:S(2)}) collective-permute-start(bf16[2,112,512]{2,1,0:T(8,128)(2,1)S(1)} %copy-done.6), channel_id=1, source_target_pairs={{0,2},{1,3},{2,0},{3,1},{4,6},{5,7},{6,4},{7,5},{8,10},{9,11},{10,... | collective-permute-start | bytes 688136 | tf_op jit(solution)/shard_map/ppermute | solution.py:422
  40.8 21.3 %collective-permute-start.5 = (bf16[2,112,512]{2,1,0:T(8,128)(2,1)S(1)}, bf16[2,112,512]{2,1,0:T(8,128)(2,1)S(1)}, u32[]{:S(2)}, u32[]{:S(2)}) collective-permute-start(bf16[2,112,512]{2,1,0:T(8,128)(2,1)S(1)} %copy-done.6), channel_id=1, source_target_pairs={{0,3},{1,2},{2,1},{3,0},{4,7},{5,6},{6,5},{7,4},{8,11},{9,10},{10,... | collective-permute-start | bytes 688136 | tf_op jit(solution)/shard_map/ppermute | solution.py:422
  42.3 4.6 %copy-start.1 = (bf16[2,2240,1400]{2,1,0:T(8,128)(2,1)S(1)}, bf16[2,2240,1400]{2,1,0:T(8,128)(2,1)}, u32[]{:S(2)}) copy-start(bf16[2,2240,1400]{2,1,0:T(8,128)(2,1)} %copy-done) | copy-start | bytes 37632004
  46.9 4.6 %copy-start.2 = (bf16[2,2240,1400]{2,1,0:T(8,128)(2,1)S(1)}, bf16[2,2240,1400]{2,1,0:T(8,128)(2,1)}, u32[]{:S(2)}) copy-start(bf16[2,2240,1400]{2,1,0:T(8,128)(2,1)} %copy-done) | copy-start | bytes 37632004
  46.9 11.4 %slice-start = ((s8[6307840]{0:T(1024)(128)(4,1)}), s8[4194304]{0:T(1024)(128)(4,1)S(1)}, s32[]{:S(2)}) async-start(s8[6307840]{0:T(1024)(128)(4,1)} %bitcast.2), calls=%async_computation | async-start | bytes 8388608
  50.9 7.4 %slice-start.1 = ((s8[6307840]{0:T(1024)(128)(4,1)}), s8[2113536]{0:T(1024)(128)(4,1)S(1)}, s32[]{:S(2)}) async-start(s8[6307840]{0:T(1024)(128)(4,1)} %bitcast.2), calls=%async_computation.1 | async-start | bytes 4227072
  59.0 8.2 %collective-permute-start.14 = (bf16[1120,128]{1,0:T(8,128)(2,1)S(1)}, bf16[1120,128]{1,0:T(8,128)(2,1)S(1)}, u32[]{:S(2)}, u32[]{:S(2)}) collective-permute-start(bf16[1120,128]{1,0:T(8,128)(2,1)S(1)} %project_3.2), channel_id=1, source_target_pairs={{0,1},{3,2},{4,5},{7,6},{8,9},{11,10},{12,13},{15,14},{16,17},{19,... | collective-permute-start | bytes 860168 | tf_op jit(solution)/shard_map/ppermute | solution.py:507
  61.4 5.7 %collective-permute-start.15 = (bf16[1120,128]{1,0:T(8,128)(2,1)S(1)}, bf16[1120,128]{1,0:T(8,128)(2,1)S(1)}, u32[]{:S(2)}, u32[]{:S(2)}) collective-permute-start(bf16[1120,128]{1,0:T(8,128)(2,1)S(1)} %project_3.2), channel_id=1, source_target_pairs={{1,2},{2,1},{5,6},{6,5},{9,10},{10,9},{13,14},{14,13},{17,18},{18,... | collective-permute-start | bytes 860168 | tf_op jit(solution)/shard_map/ppermute | solution.py:508
  62.3 13.7 %collective-permute-start.13 = (bf16[4,112,512]{2,1,0:T(8,128)(2,1)S(1)}, bf16[4,112,512]{2,1,0:T(8,128)(2,1)S(1)}, u32[]{:S(2)}, u32[]{:S(2)}) collective-permute-start(bf16[4,112,512]{2,1,0:T(8,128)(2,1)S(1)} %pad_maximum_fusion), channel_id=1, source_target_pairs={{0,4},{4,0},{8,12},{12,8},{16,20},{20,16},{24,28},{28,24},{1,5},{5... | collective-permute-start | bytes 1376264 | tf_op jit(solution)/shard_map/ppermute | solution.py:409
  62.4 10.5 %copy-start.4 = (f32[4,96,128]{2,1,0:T(8,128)S(1)}, f32[4,96,128]{2,1,0:T(8,128)}, u32[]{:S(2)}) copy-start(f32[4,96,128]{2,1,0:T(8,128)} %get-tuple-element.28.refs_4_.refs_3_.mask_ref) | copy-start | bytes 589828
  62.4 13.5 %collective-permute-start.16 = (bf16[4,112,512]{2,1,0:T(8,128)(2,1)S(1)}, bf16[4,112,512]{2,1,0:T(8,128)(2,1)S(1)}, u32[]{:S(2)}, u32[]{:S(2)}) collective-permute-start(bf16[4,112,512]{2,1,0:T(8,128)(2,1)S(1)} %pad_maximum_fusion.1), channel_id=1, source_target_pairs={{4,8},{12,16},{20,24},{8,4},{16,12},{24,20},{5,9},{13,17},{21,25},... | collective-permute-start | bytes 1376264 | tf_op jit(solution)/shard_map/ppermute | solution.py:410
  67.8 15.3 %collective-permute-start.18 = (bf16[1120,128]{1,0:T(8,128)(2,1)S(1)}, bf16[1120,128]{1,0:T(8,128)(2,1)S(1)}, u32[]{:S(2)}, u32[]{:S(2)}) collective-permute-start(bf16[1120,128]{1,0:T(8,128)(2,1)S(1)} %project_1.2), channel_id=1, source_target_pairs={{0,1},{1,0},{2,3},{3,2},{4,5},{5,4},{6,7},{7,6},{8,9},{9,8},{10,11... | collective-permute-start | bytes 860168 | tf_op jit(solution)/shard_map/ppermute | solution.py:515
  71.6 14.6 %collective-permute-start.17 = (bf16[1120,128]{1,0:T(8,128)(2,1)S(1)}, bf16[1120,128]{1,0:T(8,128)(2,1)S(1)}, u32[]{:S(2)}, u32[]{:S(2)}) collective-permute-start(bf16[1120,128]{1,0:T(8,128)(2,1)S(1)} %project_2.2), channel_id=1, source_target_pairs={{0,2},{1,3},{2,0},{3,1},{4,6},{5,7},{6,4},{7,5},{8,10},{9,11},{10,... | collective-permute-start | bytes 860168 | tf_op jit(solution)/shard_map/ppermute | solution.py:514
  87.0 10.4 %copy-start.7 = (s32[4]{0:T(128)S(1)}, s32[4]{0:T(128)}, u32[]{:S(2)}) copy-start(s32[4]{0:T(128)} %width_ref.5) | copy-start | bytes 52
  87.0 5.8 %collective-permute-start.19 = (bf16[848,128]{1,0:T(8,128)(2,1)S(1)}, bf16[848,128]{1,0:T(8,128)(2,1)S(1)}, u32[]{:S(2)}, u32[]{:S(2)}) collective-permute-start(bf16[848,128]{1,0:T(8,128)(2,1)S(1)} %project_3.3), channel_id=1, source_target_pairs={{0,1},{3,2},{4,5},{7,6},{8,9},{11,10},{12,13},{15,14},{16,17},{19,... | collective-permute-start | bytes 651272 | tf_op jit(solution)/shard_map/ppermute | solution.py:507
  88.7 4.1 %collective-permute-start.20 = (bf16[848,128]{1,0:T(8,128)(2,1)S(1)}, bf16[848,128]{1,0:T(8,128)(2,1)S(1)}, u32[]{:S(2)}, u32[]{:S(2)}) collective-permute-start(bf16[848,128]{1,0:T(8,128)(2,1)S(1)} %project_3.3), channel_id=1, source_target_pairs={{1,2},{2,1},{5,6},{6,5},{9,10},{10,9},{13,14},{14,13},{17,18},{18,... | collective-permute-start | bytes 651272 | tf_op jit(solution)/shard_map/ppermute | solution.py:508
  93.5 9.6 %collective-permute-start.22 = (bf16[848,128]{1,0:T(8,128)(2,1)S(1)}, bf16[848,128]{1,0:T(8,128)(2,1)S(1)}, u32[]{:S(2)}, u32[]{:S(2)}) collective-permute-start(bf16[848,128]{1,0:T(8,128)(2,1)S(1)} %project_1.3), channel_id=1, source_target_pairs={{0,1},{1,0},{2,3},{3,2},{4,5},{5,4},{6,7},{7,6},{8,9},{9,8},{10,11... | collective-permute-start | bytes 651272 | tf_op jit(solution)/shard_map/ppermute | solution.py:515
  97.4 11.0 %collective-permute-start.21 = (bf16[848,128]{1,0:T(8,128)(2,1)S(1)}, bf16[848,128]{1,0:T(8,128)(2,1)S(1)}, u32[]{:S(2)}, u32[]{:S(2)}) collective-permute-start(bf16[848,128]{1,0:T(8,128)(2,1)S(1)} %project_2.3), channel_id=1, source_target_pairs={{0,2},{1,3},{2,0},{3,1},{4,6},{5,7},{6,4},{7,5},{8,10},{9,11},{10,... | collective-permute-start | bytes 651272 | tf_op jit(solution)/shard_map/ppermute | solution.py:514
